TPU v7x, 256 devices: a whole 4x4x8 slice. The times are simulated.
256 devices in a mesh: dp: 8 (over x, core), seq: 32 (over y, z).
Axes of the slice: x: 4, y: 4, z: 8, core: 2. Of those that a mesh axis runs over, the one named last changes fastest.
Arguments:
- nodes: bfloat16 [8, 4096, 1024], P('dp', 'seq'), may hold values from -40 to 40
- w_qkv: bfloat16 [1024, 3072], replicated, may hold values from -1 to 1, as said below
- incoming_adjoint: bfloat16 [8, 4096, 1024], P('dp', 'seq'), may hold values from -6 to 6
- block_cols: int32 [8, 32, 4], P('dp'), may hold values from 0 to 31, as said below
- block_counts: int32 [8, 32], P('dp'), may hold values from 1 to 4, as said below
Outputs:
- mixture_output: bfloat16 [8, 4096, 1024], P('dp', 'seq')
- grad_nodes: bfloat16 [8, 4096, 1024], P('dp', 'seq')
- weight_grad: float32 [3072, 1024], P('dp', 'seq')
Inputs may be any that keep to these rules, and one draw needn't show every extreme that they name: `block_cols`: slot 0 of row block r names r itself; the 4 slots of a row block name distinct column blocks. `block_counts`: slots at or beyond the count are ignored; in every subgraph some row block uses all 4 slots. `w_qkv`: projection weights.
All inputs are finite; a program needn't handle non-finite values.
Results may differ from a plain program's by a relative error of at most 0.033.
Values may be sent and summed in bfloat16 or wider, within the bound.
A program may use at most 64 MiB of HBM per device.

v0:
```python
import math

import jax
import jax.numpy as jnp
from jax import lax
from jax.sharding import PartitionSpec as P

LENS_TALLY = 32
TILE_SPAN = 128


def attend_heads(mapped_vectors, adjoint_lenses, col_table, target_tallies):
    node_total, unused, head_count, head_dim = mapped_vectors.shape
    tile_tally = node_total // TILE_SPAN
    slot_count = col_table.shape[1]
    per_turn = math.gcd(tile_tally, 16)
    turn_count = tile_tally // per_turn
    score_scale = 1.0 / math.sqrt(head_dim)
    blocks = mapped_vectors.reshape(tile_tally, TILE_SPAN, 3, head_count, head_dim)
    q_blocks = blocks[:, :, 0]
    key_blocks = blocks[:, :, 1]
    value_blocks = blocks[:, :, 2]
    cot_blocks = adjoint_lenses.reshape(tile_tally, TILE_SPAN, head_count, head_dim)

    def block_step(carry, inputs_now):
        lookup_totals, payload_totals = carry
        query_now, cot_now, cols_now, count_now = inputs_now
        keys_now = key_blocks[cols_now].reshape(
            per_turn, slot_count * TILE_SPAN, head_count, head_dim
        )
        values_now = value_blocks[cols_now].reshape(
            per_turn, slot_count * TILE_SPAN, head_count, head_dim
        )
        scores = (
            jnp.einsum("rqhd,rkhd->rhqk", query_now, keys_now, preferred_element_type=jnp.float32)
            * score_scale
        )
        slot_live = jnp.repeat(
            jnp.arange(slot_count, dtype=jnp.int32)[None, :] < count_now[:, None], TILE_SPAN, axis=1
        )
        scores = jnp.where(slot_live[:, None, None, :], scores, -jnp.inf)
        weights = jnp.exp(scores - jnp.max(scores, axis=-1, keepdims=True))
        probability = weights / jnp.sum(weights, axis=-1, keepdims=True)
        prob_bf = probability.astype(jnp.bfloat16)
        tile_output = jnp.einsum(
            "rhqk,rkhd->rqhd", prob_bf, values_now, preferred_element_type=jnp.float32
        ).astype(jnp.bfloat16)
        row_delta = jnp.sum(cot_now.astype(jnp.float32) * tile_output.astype(jnp.float32), axis=-1)
        row_delta = jnp.transpose(row_delta, (0, 2, 1))[..., None]
        value_part = jnp.einsum(
            "rhqk,rqhd->rkhd", prob_bf, cot_now, preferred_element_type=jnp.float32
        )
        grad_prob = jnp.einsum(
            "rqhd,rkhd->rhqk", cot_now, values_now, preferred_element_type=jnp.float32
        )
        grad_score = (probability * (grad_prob - row_delta) * score_scale).astype(jnp.bfloat16)
        deriv_request = jnp.einsum(
            "rhqk,rkhd->rqhd", grad_score, keys_now, preferred_element_type=jnp.float32
        ).astype(jnp.bfloat16)
        key_part = jnp.einsum(
            "rhqk,rqhd->rkhd", grad_score, query_now, preferred_element_type=jnp.float32
        )
        flat_cols = cols_now.reshape(-1)
        lookup_totals = lookup_totals.at[flat_cols].add(
            key_part.reshape(per_turn * slot_count, TILE_SPAN, head_count, head_dim)
        )
        payload_totals = payload_totals.at[flat_cols].add(
            value_part.reshape(per_turn * slot_count, TILE_SPAN, head_count, head_dim)
        )
        return ((lookup_totals, payload_totals), (tile_output, deriv_request))

    inputs_all = (
        q_blocks.reshape(turn_count, per_turn, TILE_SPAN, head_count, head_dim),
        cot_blocks.reshape(turn_count, per_turn, TILE_SPAN, head_count, head_dim),
        col_table.reshape(turn_count, per_turn, slot_count),
        target_tallies.reshape(turn_count, per_turn),
    )
    empty = jnp.zeros((tile_tally, TILE_SPAN, head_count, head_dim), jnp.float32)
    (lookup_totals, payload_totals), (out_blocks, query_grads) = lax.scan(
        block_step, (empty, empty), inputs_all
    )
    lens_output = out_blocks.reshape(node_total, 1, head_count, head_dim)
    head_grads = jnp.stack(
        [
            query_grads.reshape(tile_tally, TILE_SPAN, head_count, head_dim),
            lookup_totals.astype(jnp.bfloat16),
            payload_totals.astype(jnp.bfloat16),
        ],
        axis=2,
    )
    return (lens_output, head_grads.reshape(node_total, 3, head_count, head_dim))


def per_device(nodes, w_qkv, incoming_adjoint, block_cols, block_counts):
    features = nodes[0]
    adjoint_vertices = incoming_adjoint[0]
    col_table = block_cols[0]
    target_tallies = block_counts[0]
    row_count, width = features.shape
    head_dim = width // LENS_TALLY
    seq_count = lax.axis_size("seq")
    local_heads = LENS_TALLY // seq_count
    mapped_vectors = jnp.dot(features, w_qkv, preferred_element_type=jnp.float32).astype(
        jnp.bfloat16
    )
    mapped_vectors = mapped_vectors.reshape(row_count, 3, seq_count, local_heads, head_dim)
    adjoint_lenses = adjoint_vertices.reshape(row_count, 1, seq_count, local_heads, head_dim)
    lens_part, grads_part = attend_heads(
        lax.all_to_all(mapped_vectors, "seq", split_axis=2, concat_axis=0, tiled=True)[:, :, 0],
        lax.all_to_all(adjoint_lenses, "seq", split_axis=2, concat_axis=0, tiled=True)[:, :, 0],
        col_table,
        target_tallies,
    )
    lens_output = lens_part[:, :, None]
    head_grads = grads_part[:, :, None]
    node_out, node_grads = (
        lax.all_to_all(lens_output, "seq", split_axis=0, concat_axis=2, tiled=True),
        lax.all_to_all(head_grads, "seq", split_axis=0, concat_axis=2, tiled=True),
    )
    mixture_output = node_out.reshape(1, row_count, width)
    flattened_derivs = node_grads.reshape(row_count, 3 * width)
    grad_nodes = (
        lax.dot_general(
            flattened_derivs, w_qkv, (((1,), (1,)), ((), ())), preferred_element_type=jnp.float32
        )
        .astype(jnp.bfloat16)
        .reshape(1, row_count, width)
    )
    partial_value = lax.dot_general(
        flattened_derivs, features, (((0,), (0,)), ((), ())), preferred_element_type=jnp.float32
    )
    column_share = lax.psum_scatter(
        partial_value.astype(jnp.bfloat16), "seq", scatter_dimension=1, tiled=True
    )
    weight_grad = lax.psum_scatter(column_share, "dp", scatter_dimension=0, tiled=True).astype(
        jnp.float32
    )
    return (mixture_output, grad_nodes, weight_grad)


def solution(mesh):
    in_specs = (P("dp", "seq", None), P(), P("dp", "seq", None), P("dp", None, None), P("dp", None))
    out_specs = (P("dp", "seq", None), P("dp", "seq", None), P("dp", "seq"))
    return jax.shard_map(
        per_device, mesh=mesh, in_specs=in_specs, out_specs=out_specs, check_vma=False
    )
```

profile of v0, /device:TPU:2, one launch (start us, length us, event | category | flops | bytes accessed | tf_op | source)
XLA Modules:
  0.0 446.2 jit_solution(12159782424131211356)
XLA Ops:
  8.1 3.8 convolution_convert_fusion.3
  13.3 11.5 %all-to-all-start = ((bf16[128,3,32,1,32]{0,4,1,3,2:T(8,128)(2,1)}), bf16[128,3,32,1,32]{0,4,1,3,2:T(8,128)(2,1)S(1)}, u32[]{:S(2)}, u32[]{:S(2)}) async-start(bf16[128,3,32,1,32]{0,4,1,3,2:T(8,128)(2,1)} %copy.102), calls=%async_computation | async-start | bytes 1572864 | tf_op jit(solution)/shard_map/all_to_all | solution.py:109
  25.6 22.5 %all-to-all-done = bf16[128,3,32,1,32]{0,4,1,3,2:T(8,128)(2,1)S(1)} async-done(((bf16[128,3,32,1,32]{0,4,1,3,2:T(8,128)(2,1)}), bf16[128,3,32,1,32]{0,4,1,3,2:T(8,128)(2,1)S(1)}, u32[]{:S(2)}, u32[]{:S(2)}) %all-to-all-start) | async-done | bytes 786464 | tf_op jit(solution)/shard_map/all_to_all | solution.py:109
  48.1 4.7 %all-to-all-start.1 = ((bf16[128,1,32,1,32]{0,4,3,1,2:T(8,128)(2,1)}), bf16[128,1,32,1,32]{0,4,3,1,2:T(8,128)(2,1)S(1)}, u32[]{:S(2)}, u32[]{:S(2)}) async-start(bf16[128,1,32,1,32]{0,4,3,1,2:T(8,128)(2,1)} %bitcast.34), calls=%async_computation.1 | async-start | bytes 524288 | tf_op jit(solution)/shard_map/all_to_all | solution.py:110
  56.4 8.3 %all-to-all-done.1 = bf16[128,1,32,1,32]{0,4,3,1,2:T(8,128)(2,1)S(1)} async-done(((bf16[128,1,32,1,32]{0,4,3,1,2:T(8,128)(2,1)}), bf16[128,1,32,1,32]{0,4,3,1,2:T(8,128)(2,1)S(1)}, u32[]{:S(2)}, u32[]{:S(2)}) %all-to-all-start.1) | async-done | bytes 262176 | tf_op jit(solution)/shard_map/all_to_all | solution.py:110
  65.5 64.6 %while.16 = (s32[]{:T(128)}, f32[32,128,1,32]{1,3,0,2:T(8,128)S(1)}, f32[32,128,1,32]{1,3,0,2:T(8,128)S(1)}, bf16[2,16,128,1,32]{2,1,0,4,3:T(8,128)(2,1)}, bf16[...) while((s32[]{:T(128)}, ...), condition=%wide.region_6.7_spmd, body=%wide.region_0.6_spmd.sunk | while | flops 417202112 | bytes 87509408 | solution.py:79
  70.4 1.7 fusion.71
  72.0 3.4 fusion.73
  79.4 1.8 copy.172
  81.3 3.3 scatter_fusion.1
  84.6 3.9 multiply_convert_fusion.2
  91.3 1.8 copy.170
  93.2 3.1 scatter_fusion
  102.7 1.7 fusion.71
  104.3 3.4 fusion.73
  111.7 1.8 copy.172
  113.6 3.3 scatter_fusion.1
  116.8 4.0 multiply_convert_fusion.2
  123.6 1.8 copy.170
  125.4 3.1 scatter_fusion
  131.8 4.7 %copy.115 = bf16[4096,3,1,1,32]{4,1,3,2,0:T(4,128)(2,1)} copy(bf16[4096,3,1,1,32]{0,4,3,2,1:T(8,128)(2,1)S(1)} %pad_maximum_fusion) | data formatting | bytes 1572864 | tf_op jit(solution)/shard_map/stack | solution.py:83
  136.5 6.2 %reshape.247 = bf16[32,2,6144]{2,1,0:T(2,128)(2,1)S(1)} reshape(bf16[4096,1,1,3,32]{4,3,2,1,0:T(4,128)(2,1)} %bitcast.196) | data formatting | bytes 1572864
  142.7 26.4 %all_to_all.60 = bf16[32,2,6144]{2,1,0:T(2,128)(2,1)S(1)} all-to-all(bf16[32,2,6144]{2,1,0:T(2,128)(2,1)S(1)} %reshape.247), channel_id=1, replica_groups=mesh['dp'=8,'seq'=32] {'seq'}, dimensions={0} | all-to-all | bytes 1572864 | tf_op jit(solution)/shard_map/all_to_all | solution.py:118
  169.1 4.8 %reshape.248 = bf16[4096,1,1,3,32]{4,3,2,1,0:T(4,128)(2,1)} reshape(bf16[32,2,6144]{2,1,0:T(2,128)(2,1)S(1)} %all_to_all.60) | data formatting | bytes 1572864
  173.9 5.4 %copy.120 = bf16[32,128,3,1,1,32]{1,5,0,2,3,4:T(8,128)(2,1)S(1)} copy(bf16[32,128,3,1,1,32]{5,2,1,0,4,3:T(4,128)(2,1)} %bitcast.197) | data formatting | bytes 1572864 | tf_op jit(solution)/shard_map/all_to_all | solution.py:118
  179.4 4.5 %convolution_convert_fusion.2 = bf16[3072,1024]{0,1:T(8,128)(2,1)} fusion(bf16[128,3072]{0,1:T(8,128)(2,1)S(1)} %bitcast.199, bf16[1,128,1024]{2,1,0:T(8,128)(2,1)S(1)} %copy-done), kind=kOutput, calls=%fused_computation.51 | convolution fusion | flops 808452096 | bytes 7340032 | tf_op jit(solution)/shard_map/dot_general | solution.py:129
  187.7 18.6 %all_to_all.61 = bf16[32,2,2048]{2,1,0:T(2,128)(2,1)S(1)} all-to-all(bf16[32,2,2048]{2,1,0:T(2,128)(2,1)S(1)} %reshape.245), channel_id=1, replica_groups=mesh['dp'=8,'seq'=32] {'seq'}, dimensions={0} | all-to-all | bytes 524288 | tf_op jit(solution)/shard_map/all_to_all | solution.py:117
  207.7 2.1 copy.110
  210.8 195.3 %reduce-scatter.5.cloned.1.call-done = bf16[3072,32]{0,1:T(8,128)(2,1)} async-done(((bf16[3072,1024]{0,1:T(8,128)(2,1)}), bf16[3072,32]{0,1:T(8,128)(2,1)}) %reduce-scatter.5.cloned.1.call-update) | async-done | bytes 196624 | tf_op jit(solution)/shard_map/reduce_scatter | solution.py:132
  406.0 2.1 copy.121
  408.1 5.7 %fusion.29 = bf16[1,128,1024]{2,1,0:T(8,128)(2,1)} fusion(bf16[128,3072]{0,1:T(8,128)(2,1)S(1)} %bitcast.200, bf16[1024,3072]{1,0:T(8,128)(2,1)} %param.8), kind=kOutput, calls=%fused_computation.54 | convolution fusion | flops 805437440 | bytes 7340032 | tf_op jit(solution)/shard_map/dot_general | solution.py:123
  413.8 23.9 %reduce-scatter.7.cloned.1.call-done = bf16[384,32]{1,0:T(8,128)(2,1)} async-done(((bf16[3072,32]{1,0:T(8,128)(2,1)}), bf16[384,32]{1,0:T(8,128)(2,1)}) %reduce-scatter.7.cloned.1.call-update) | async-done | bytes 24592
  (131 shorter events, 42.9 us)
Async XLA Ops:
  7.2 1.0 copy-start
  11.9 12.8 %copy-start.6 = (bf16[1,128,1024]{2,1,0:T(8,128)(2,1)S(1)}, bf16[1,128,1024]{2,1,0:T(8,128)(2,1)}, u32[]{:S(2)}) copy-start(bf16[1,128,1024]{2,1,0:T(8,128)(2,1)} %param.9) | copy-start | bytes 786436
  11.9 41.7 %copy-start.12 = (s32[1,32]{1,0:T(1,128)S(1)}, s32[1,32]{1,0:T(1,128)}, u32[]{:S(2)}) copy-start(s32[1,32]{1,0:T(1,128)} %param.11) | copy-start | bytes 388
  11.9 43.0 %copy-start.11 = (s32[1,32,4]{1,2,0:T(4,128)S(1)}, s32[1,32,4]{1,2,0:T(4,128)}, u32[]{:S(2)}) copy-start(s32[1,32,4]{1,2,0:T(4,128)} %param.10) | copy-start | bytes 1540
  13.3 34.9 %all-to-all-start = ((bf16[128,3,32,1,32]{0,4,1,3,2:T(8,128)(2,1)}), bf16[128,3,32,1,32]{0,4,1,3,2:T(8,128)(2,1)S(1)}, u32[]{:S(2)}, u32[]{:S(2)}) async-start(bf16[128,3,32,1,32]{0,4,1,3,2:T(8,128)(2,1)} %copy.102), calls=%async_computation | async-start | bytes 1572864 | tf_op jit(solution)/shard_map/all_to_all | solution.py:109
  48.1 16.5 %all-to-all-start.1 = ((bf16[128,1,32,1,32]{0,4,3,1,2:T(8,128)(2,1)}), bf16[128,1,32,1,32]{0,4,3,1,2:T(8,128)(2,1)S(1)}, u32[]{:S(2)}, u32[]{:S(2)}) async-start(bf16[128,1,32,1,32]{0,4,3,1,2:T(8,128)(2,1)} %bitcast.34), calls=%async_computation.1 | async-start | bytes 524288 | tf_op jit(solution)/shard_map/all_to_all | solution.py:110
  52.9 353.2 %reduce-scatter.5.cloned.1.call-start = ((), (), s32[]{:S(2)}) async-start(), calls=%async_computation.6 | async-start | bytes 6488064 | tf_op jit(solution)/shard_map/reduce_scatter | solution.py:132
  64.7 0.7 copy-start.3
  69.2 6.7 %copy-start.2 = (bf16[16,512,32]{1,0,2:T(8,128)(2,1)}, bf16[16,512,32]{1,0,2:T(8,128)(2,1)S(1)}, u32[]{:S(2)}) copy-start(bf16[16,512,32]{1,0,2:T(8,128)(2,1)S(1)} %reshape.274) | copy-start | bytes 1572868 | tf_op jit(solution)/shard_map/while
  75.4 1.9 copy-start.1
  75.5 1.1 copy-start.4
  84.6 4.7 %copy-start.5 = (bf16[2,16,128,1,32]{2,4,1,3,0:T(8,128)(2,1)S(1)}, bf16[2,16,128,1,32]{2,4,1,3,0:T(8,128)(2,1)}, u32[]{:S(2)}) copy-start(bf16[2,16,128,1,32]{2,4,1,3,0:T(8,128)(2,1)} %get-tuple-element.274) | copy-start | bytes 786436 | tf_op jit(solution)/shard_map/while
  89.2 3.9 copy-start.10
  93.1 3.2 copy-start.7
  97.1 0.7 copy-start.8
  101.5 6.7 %copy-start.2 = (bf16[16,512,32]{1,0,2:T(8,128)(2,1)}, bf16[16,512,32]{1,0,2:T(8,128)(2,1)S(1)}, u32[]{:S(2)}) copy-start(bf16[16,512,32]{1,0,2:T(8,128)(2,1)S(1)} %reshape.274) | copy-start | bytes 1572868 | tf_op jit(solution)/shard_map/while
  107.7 1.9 copy-start.1
  107.7 1.1 copy-start.4
  116.8 4.7 %copy-start.5 = (bf16[2,16,128,1,32]{2,4,1,3,0:T(8,128)(2,1)S(1)}, bf16[2,16,128,1,32]{2,4,1,3,0:T(8,128)(2,1)}, u32[]{:S(2)}) copy-start(bf16[2,16,128,1,32]{2,4,1,3,0:T(8,128)(2,1)} %get-tuple-element.274) | copy-start | bytes 786436 | tf_op jit(solution)/shard_map/while
  121.5 3.9 copy-start.10
  125.4 3.2 copy-start.7
  129.4 0.7 copy-start.8
  183.9 0.9 copy-start.9
  183.9 253.9 %reduce-scatter.7.cloned.1.call-start = ((), (), s32[]{:S(2)}) async-start(), calls=%async_computation.7 | async-start | bytes 884736
Sparse Core Ops, SparseCore 0:
  184.0 221.9 reduce-scatter.4
  408.7 28.9 reduce-scatter.6
where the time goes:
time: 450 us; the launch traced here: 446 us
  waiting for transfers between devices  250 us (56%)
  local copies, waits for them, and re-layouts  66.5 us (15%)
  blocking collectives  45 us (10%)
  matrix products  29.6 us (7%)
  other arithmetic  23.9 us (5%)
  starting transfers between devices  16.5 us (4%)
  between operations  14.3 us (3%)
    reduce_scatter x1, waiting for transfers between devices, per_device(): lax.psum_scatter(partial_value.astype(jnp.bfloat16), 'seq', scatter_dimen...  195 us
    all_to_all x1, blocking collectives, per_device(): lax.all_to_all(head_grads, 'seq', split_axis=0, concat_axis=2, tiled=True)  26.4 us
    unnamed x3, waiting for transfers between devices  24 us
    all_to_all x1, waiting for transfers between devices, per_device(): lax.all_to_all(mapped_vectors, 'seq', split_axis=2, concat_axis=0, tiled=...  22.5 us
    unnamed x23, local copies, waits for them, and re-layouts  21.7 us
    all_to_all x1, blocking collectives, per_device(): lax.all_to_all(lens_output, 'seq', split_axis=0, concat_axis=2, tiled=True)  18.6 us
    all_to_all x1, starting transfers between devices, per_device(): lax.all_to_all(mapped_vectors, 'seq', split_axis=2, concat_axis=0, tiled=...  11.5 us
  transfers between devices with their start and end apart: 4, of which 4 were waited for; matrix products, arithmetic and copies ran while one was open for 4% of the time, Pallas kernels for 0%

commit v1 on v0

v1 whole, which is shorter than its diff:
```python
import functools
import math

import jax
import jax.numpy as jnp
from jax import lax
from jax.experimental import pallas as pl
from jax.experimental.pallas import tpu as pltpu
from jax.sharding import PartitionSpec as P

MESH = pl.DeviceIdType.MESH
BLK = 128
FEAT = 32
SLOTS = 4
F32 = jnp.float32
BF16 = jnp.bfloat16
VMEM_LIMIT = 48 * 1024 * 1024


def lane_ids(shape):
    return lax.broadcasted_iota(jnp.int32, shape, len(shape) - 1)


def swap_quarters(tiles):
    lane = lane_ids(tiles[0].shape)
    low = lane < 64
    even = (lane // 32) % 2 == 0
    a0, a1, a2, a3 = tiles
    b0 = jnp.where(low, a0, pltpu.roll(a2, 64, 1))
    b2 = jnp.where(low, pltpu.roll(a0, 64, 1), a2)
    b1 = jnp.where(low, a1, pltpu.roll(a3, 64, 1))
    b3 = jnp.where(low, pltpu.roll(a1, 64, 1), a3)
    return (
        jnp.where(even, b0, pltpu.roll(b1, 32, 1)),
        jnp.where(even, pltpu.roll(b0, 96, 1), b1),
        jnp.where(even, b2, pltpu.roll(b3, 32, 1)),
        jnp.where(even, pltpu.roll(b2, 96, 1), b3),
    )


def greet(me_d, me_s, nd, ns):
    barrier = pltpu.get_barrier_semaphore()

    def seq_hello(k, c):
        pl.semaphore_signal(
            barrier, inc=1, device_id=(me_d, lax.rem(me_s + k, ns)), device_id_type=MESH
        )
        return c

    def dp_hello(k, c):
        pl.semaphore_signal(
            barrier, inc=1, device_id=(lax.rem(me_d + k, nd), me_s), device_id_type=MESH
        )
        return c

    lax.fori_loop(1, ns, seq_hello, 0)
    lax.fori_loop(1, nd, dp_hello, 0)
    return barrier


def peer_at(me_s, i, j, ng, sign):
    group = lax.rem(me_s // 4 + sign * i + ng, ng)
    return 4 * group + lax.rem(me_s % 4 + sign * j + 4, 4)


def spread_kernel(
    nd, ns, x_ref, w_ref, do_ref, recv_ref, xt_all, w_vm, send_buf, xt_vm,
    w_sem, send_sem, recv_sem, xs_sem, xr_sem, own_sem,
):
    me_d, me_s = lax.axis_index("dp"), lax.axis_index("seq")
    ng = ns // 4
    my_group = me_s // 4

    def w_copy(i, m):
        g = lax.rem(my_group + i, ng)
        return pltpu.make_async_copy(
            w_ref.at[:, pl.ds(pl.multiple_of((m * ng + g) * BLK, BLK), BLK)],
            w_vm.at[i, :, pl.ds(m * BLK, BLK)],
            w_sem.at[i, m],
        )

    def w_start(i, c):
        for m in range(3):
            w_copy(i, m).start()
        return c

    lax.fori_loop(0, ng, w_start, 0)
    barrier = greet(me_d, me_s, nd, ns)
    xt_vm[...] = jnp.transpose(x_ref[...].astype(F32)).astype(BF16)

    def xt_slot(d):
        return xt_all.at[:, pl.ds(pl.multiple_of(d * BLK, BLK), BLK)]

    def xt_copy(k):
        return pltpu.make_async_remote_copy(
            src_ref=xt_vm,
            dst_ref=xt_slot(me_d),
            send_sem=xs_sem.at[k],
            recv_sem=xr_sem.at[k],
            device_id=(lax.rem(me_d + k, nd), me_s),
            device_id_type=MESH,
        )

    def head_copy(i, j):
        peer = peer_at(me_s, i, j, ng, 1)
        return pltpu.make_async_remote_copy(
            src_ref=send_buf.at[peer],
            dst_ref=recv_ref.at[me_s],
            send_sem=send_sem.at[i, j],
            recv_sem=recv_sem.at[i, j],
            device_id=(me_d, peer),
            device_id_type=MESH,
        )

    own_head = pltpu.make_async_copy(send_buf.at[me_s], recv_ref.at[me_s], own_sem.at[0])
    own_xt = pltpu.make_async_copy(xt_vm, xt_slot(me_d), own_sem.at[1])

    def project(i, c):
        g = lax.rem(my_group + i, ng)
        for m in range(3):
            w_copy(i, m).wait()
        qkv = jnp.dot(x_ref[...], w_vm[i], preferred_element_type=F32).astype(BF16)
        cot = do_ref[:, pl.ds(pl.multiple_of(g * BLK, BLK), BLK)]
        packed = swap_quarters(
            (qkv[:, :BLK], qkv[:, BLK : 2 * BLK], qkv[:, 2 * BLK :], cot)
        )
        for j in range(4):
            send_buf[4 * g + j] = packed[j]

        @pl.when(i == 0)
        def _():
            pl.semaphore_wait(barrier, ns + nd - 2)
            own_head.start()
            own_xt.start()

            def xt_start(k, c):
                xt_copy(k).start()
                return c

            lax.fori_loop(1, nd, xt_start, 0)

        @pl.when(i > 0)
        def _():
            head_copy(i, 0).start()

        for j in range(1, 4):
            head_copy(i, j).start()
        return c

    lax.fori_loop(0, ng, project, 0)
    own_head.wait()
    own_xt.wait()

    def finish(i, c):
        @pl.when(i > 0)
        def _():
            head_copy(i, 0).wait()

        for j in range(1, 4):
            head_copy(i, j).wait()
        return c

    lax.fori_loop(0, ng, finish, 0)

    def xt_wait(k, c):
        xt_copy(k).wait()
        return c

    lax.fori_loop(1, nd, xt_wait, 0)


def attend_kernel(nb, cols_ref, counts_ref, a_ref, out_ref, kvt, acc):
    scale = 1.0 / math.sqrt(FEAT)
    to_exp2 = scale * math.log2(math.e)
    lane = lane_ids((BLK, BLK))

    def prepare(b, c):
        kvt[b] = jnp.transpose(a_ref[b].astype(F32))[FEAT : 3 * FEAT].astype(BF16)
        acc[b] = jnp.zeros((BLK, BLK), F32)
        return c

    lax.fori_loop(0, nb, prepare, 0)

    def row_block(r, c):
        mine = a_ref[r]
        zero = jnp.zeros_like(mine)
        quarter = lane // FEAT
        left = jnp.concatenate(
            [
                jnp.where(quarter == 1, pltpu.roll(mine, 32, 1), zero),
                jnp.where(quarter == 2, pltpu.roll(mine, 96, 1), zero),
            ],
            axis=0,
        )
        right = jnp.concatenate(
            [
                jnp.where(quarter == 3, mine, zero),
                jnp.where(quarter == 2, pltpu.roll(mine, 64, 1), zero),
            ],
            axis=0,
        )
        count = counts_ref[r]
        named = [cols_ref[r * SLOTS + s] for s in range(SLOTS)]
        keys = jnp.concatenate([a_ref[n] for n in named], axis=0)
        both = lax.dot_general(
            keys, left, (((1,), (1,)), ((), ())), preferred_element_type=F32
        )
        scores = [
            jnp.where(s < count, both[s * BLK : (s + 1) * BLK, :BLK], -jnp.inf)
            for s in range(SLOTS)
        ]
        scores = jnp.concatenate(scores, axis=0)
        grad_prob = both[:, BLK:]
        top = jnp.max(scores, axis=0, keepdims=True)
        weights = jnp.exp2((scores - top) * to_exp2)
        prob = weights * (1.0 / jnp.sum(weights, axis=0, keepdims=True))
        delta = jnp.sum(prob * grad_prob, axis=0, keepdims=True)
        grad_score = prob * (grad_prob - delta) * scale
        pair = jnp.concatenate([prob.astype(BF16), grad_score.astype(BF16)], axis=1)
        key_side = jnp.dot(pair, right, preferred_element_type=F32)
        for s in range(SLOTS):
            acc[named[s]] += key_side[s * BLK : (s + 1) * BLK]
        turned = jnp.concatenate([kvt[n] for n in named], axis=1)
        row_side = jnp.dot(turned, pair, preferred_element_type=F32)
        row_side = jnp.concatenate(
            [row_side[FEAT:, :BLK], row_side[:FEAT, BLK:], jnp.zeros((2 * FEAT, BLK), F32)],
            axis=0,
        )
        acc[r] += jnp.transpose(row_side)
        return c

    lax.fori_loop(0, nb, row_block, 0)

    def emit(b, c):
        out_ref[b] = acc[b].astype(BF16)
        return c

    lax.fori_loop(0, nb, emit, 0)


def return_kernel(
    nd, ns, ny, nz, tpd, ret_ref, w_ref, xt_ref, mix_ref, gn_ref, wg_ref,
    ret_in, w_vm, xt_vm, dq, wg_in, part, rs_y, mid, rs_z,
    load_sem, send_sem, recv_sem, own_sem, ts_sem, tr_sem, to_sem,
    ys_sem, yr_sem, zs_sem, zr_sem,
):
    me_d, me_s = lax.axis_index("dp"), lax.axis_index("seq")
    me_y, me_z = me_s // nz, me_s % nz
    ng = ns // 4
    hidden = ng * BLK
    load_w = pltpu.make_async_copy(w_ref, w_vm, load_sem.at[0])
    load_xt = pltpu.make_async_copy(xt_ref, xt_vm, load_sem.at[1])
    own = pltpu.make_async_copy(ret_ref.at[me_s], ret_in.at[me_s], own_sem.at[0])
    own.start()
    load_xt.start()
    load_w.start()
    barrier = greet(me_d, me_s, nd, ns)

    def back_copy(i, j):
        peer = peer_at(me_s, i, j, ng, 1)
        return pltpu.make_async_remote_copy(
            src_ref=ret_ref.at[peer],
            dst_ref=ret_in.at[me_s],
            send_sem=send_sem.at[i, j],
            recv_sem=recv_sem.at[i, j],
            device_id=(me_d, peer),
            device_id_type=MESH,
        )

    pl.semaphore_wait(barrier, ns + nd - 2)

    def back_start(i, c):
        @pl.when(i > 0)
        def _():
            back_copy(i, 0).start()

        for j in range(1, 4):
            back_copy(i, j).start()
        return c

    lax.fori_loop(0, ng, back_start, 0)

    def tile_rows(d):
        return pl.ds(pl.multiple_of(d * BLK, BLK), BLK)

    def lanes(t):
        return pl.ds(pl.multiple_of(t * BLK, BLK), BLK)

    def tile_own(t):
        return pltpu.make_async_copy(
            dq.at[:, lanes(t)], wg_in.at[t % tpd, tile_rows(me_d)], to_sem.at[t % tpd]
        )

    def tile_copy(t):
        return pltpu.make_async_remote_copy(
            src_ref=dq.at[:, lanes(t)],
            dst_ref=wg_in.at[t % tpd, tile_rows(me_d)],
            send_sem=ts_sem.at[t],
            recv_sem=tr_sem.at[me_d, t % tpd],
            device_id=(t // tpd, me_s),
            device_id_type=MESH,
        )

    def gather(i, c):
        g = lax.rem(me_s // 4 - i + ng, ng)

        @pl.when(i == 0)
        def _():
            own.wait()

        @pl.when(i > 0)
        def _():
            back_copy(i, 0).wait_recv()

        for j in range(1, 4):
            back_copy(i, j).wait_recv()
        mix, d_q, d_k, d_v = swap_quarters(tuple(ret_in[4 * g + j] for j in range(4)))
        mix_ref[:, lanes(g)] = mix
        for m, tile in enumerate((d_q, d_k, d_v)):
            t = m * ng + g
            dq[:, lanes(t)] = tile

            @pl.when(t // tpd == me_d)
            def _():
                tile_own(t).start()

            @pl.when(t // tpd != me_d)
            def _():
                tile_copy(t).start()

        return c

    lax.fori_loop(0, ng, gather, 0)
    load_xt.wait()

    def y_copy(t, k):
        to = lax.rem(me_y + k, ny)
        return pltpu.make_async_remote_copy(
            src_ref=part.at[t, pl.ds(pl.multiple_of(to * nz * FEAT, FEAT), nz * FEAT)],
            dst_ref=rs_y.at[t, k - 1],
            send_sem=ys_sem.at[t, k],
            recv_sem=yr_sem.at[t, k],
            device_id=(me_d, to * nz + me_z),
            device_id_type=MESH,
        )

    def z_copy(t, k):
        to = lax.rem(me_z + k, nz)
        return pltpu.make_async_remote_copy(
            src_ref=mid.at[t, pl.ds(pl.multiple_of(to * FEAT, FEAT), FEAT)],
            dst_ref=rs_z.at[t, k - 1],
            send_sem=zs_sem.at[t, k],
            recv_sem=zr_sem.at[t, k],
            device_id=(me_d, me_y * nz + to),
            device_id_type=MESH,
        )

    def tile_done(t, k):
        src = lax.rem(me_d + k, nd)
        return pltpu.make_async_remote_copy(
            src_ref=dq.at[:, lanes(0)],
            dst_ref=wg_in.at[t, tile_rows(src)],
            send_sem=ts_sem.at[0],
            recv_sem=tr_sem.at[src, t],
            device_id=(src, me_s),
            device_id_type=MESH,
        )

    for t in range(tpd):
        tile_own(me_d * tpd + t).wait()

        def arrived(k, c):
            tile_done(t, k).wait_recv()
            return c

        lax.fori_loop(1, nd, arrived, 0)
        part[t] = jnp.dot(xt_vm[...], wg_in[t], preferred_element_type=F32).astype(BF16)
        for k in range(1, ny):
            y_copy(t, k).start()

    load_w.wait()

    def node_cols(n, c):
        cols = pl.ds(pl.multiple_of(n * 2 * BLK, 2 * BLK), 2 * BLK)
        gn_ref[:, cols] = lax.dot_general(
            dq[...], w_vm[cols, :], (((1,), (1,)), ((), ())), preferred_element_type=F32
        ).astype(BF16)
        return c

    lax.fori_loop(0, hidden // (2 * BLK), node_cols, 0)

    for t in range(tpd):
        total = part[t, pl.ds(pl.multiple_of(me_y * nz * FEAT, FEAT), nz * FEAT)].astype(F32)
        for k in range(1, ny):
            y_copy(t, k).wait_recv()
            total += rs_y[t, k - 1].astype(F32)
        mid[t] = total.astype(BF16)
        for k in range(1, nz):
            z_copy(t, k).start()

    for t in range(tpd):
        total = mid[t, pl.ds(pl.multiple_of(me_z * FEAT, FEAT), FEAT)].astype(F32)
        for k in range(1, nz):
            z_copy(t, k).wait_recv()
            total += rs_z[t, k - 1].astype(F32)
        wg_ref[:, pl.ds(t * BLK, BLK)] = total

    def back_sent(i, c):
        @pl.when(i > 0)
        def _():
            back_copy(i, 0).wait_send()

        for j in range(1, 4):
            back_copy(i, j).wait_send()
        return c

    lax.fori_loop(0, ng, back_sent, 0)

    def tile_sent(t, c):
        @pl.when(t // tpd != me_d)
        def _():
            tile_copy(t).wait_send()

        return c

    lax.fori_loop(0, 3 * ng, tile_sent, 0)
    for t in range(tpd):
        for k in range(1, ny):
            y_copy(t, k).wait_send()
        for k in range(1, nz):
            z_copy(t, k).wait_send()


def per_device(nd, ns, nodes, w_qkv, incoming_adjoint, block_cols, block_counts):
    rows, hidden = nodes.shape[1:]
    ny, nz = 4, ns // 4
    ng = ns // 4
    tpd = 3 * ng // nd
    any_spec = pl.BlockSpec(memory_space=pl.ANY)
    vm_spec = pl.BlockSpec(memory_space=pltpu.VMEM)
    sm_spec = pl.BlockSpec(memory_space=pltpu.SMEM)
    dma = pltpu.SemaphoreType.DMA
    packed, xt_all = pl.pallas_call(
        functools.partial(spread_kernel, nd, ns),
        out_shape=(
            jax.ShapeDtypeStruct((ns, BLK, BLK), BF16),
            jax.ShapeDtypeStruct((hidden, nd * BLK), BF16),
        ),
        in_specs=[vm_spec, any_spec, vm_spec],
        out_specs=(any_spec, any_spec),
        scratch_shapes=[
            pltpu.VMEM((ng, hidden, 3 * BLK), BF16),
            pltpu.VMEM((ns, BLK, BLK), BF16),
            pltpu.VMEM((hidden, BLK), BF16),
            dma((ng, 3)),
            dma((ng, 4)),
            dma((ng, 4)),
            dma((nd,)),
            dma((nd,)),
            dma((2,)),
        ],
        compiler_params=pltpu.CompilerParams(
            collective_id=1, has_side_effects=True, vmem_limit_bytes=VMEM_LIMIT
        ),
        name="spread",
    )(nodes[0], w_qkv, incoming_adjoint[0])
    returned = pl.pallas_call(
        functools.partial(attend_kernel, ns),
        out_shape=jax.ShapeDtypeStruct((ns, BLK, BLK), BF16),
        in_specs=[sm_spec, sm_spec, vm_spec],
        out_specs=vm_spec,
        scratch_shapes=[
            pltpu.VMEM((ns, 2 * FEAT, BLK), BF16),
            pltpu.VMEM((ns, BLK, BLK), F32),
        ],
        compiler_params=pltpu.CompilerParams(vmem_limit_bytes=VMEM_LIMIT),
        name="attend",
    )(block_cols[0].reshape(-1), block_counts[0], packed)
    mixture, grad_nodes, weight_grad = pl.pallas_call(
        functools.partial(return_kernel, nd, ns, ny, nz, tpd),
        out_shape=(
            jax.ShapeDtypeStruct((rows, hidden), BF16),
            jax.ShapeDtypeStruct((rows, hidden), BF16),
            jax.ShapeDtypeStruct((FEAT, tpd * BLK), F32),
        ),
        in_specs=[any_spec, any_spec, any_spec],
        out_specs=(vm_spec, vm_spec, vm_spec),
        scratch_shapes=[
            pltpu.VMEM((ns, BLK, BLK), BF16),
            pltpu.VMEM((hidden, 3 * hidden), BF16),
            pltpu.VMEM((hidden, nd * BLK), BF16),
            pltpu.VMEM((rows, 3 * hidden), BF16),
            pltpu.VMEM((tpd, nd * BLK, BLK), BF16),
            pltpu.VMEM((tpd, hidden, BLK), BF16),
            pltpu.VMEM((tpd, ny - 1, nz * FEAT, BLK), BF16),
            pltpu.VMEM((tpd, nz * FEAT, BLK), BF16),
            pltpu.VMEM((tpd, nz - 1, FEAT, BLK), BF16),
            dma((2,)),
            dma((ng, 4)),
            dma((ng, 4)),
            dma((1,)),
            dma((3 * ng,)),
            dma((nd, tpd)),
            dma((tpd,)),
            dma((tpd, ny)),
            dma((tpd, ny)),
            dma((tpd, nz)),
            dma((tpd, nz)),
        ],
        compiler_params=pltpu.CompilerParams(
            collective_id=2, has_side_effects=True, vmem_limit_bytes=VMEM_LIMIT
        ),
        name="give_back",
    )(returned, w_qkv, xt_all)
    return (mixture[None], grad_nodes[None], jnp.transpose(weight_grad))


def solution(mesh):
    nd, ns = mesh.shape["dp"], mesh.shape["seq"]
    in_specs = (P("dp", "seq", None), P(), P("dp", "seq", None), P("dp", None, None), P("dp", None))
    out_specs = (P("dp", "seq", None), P("dp", "seq", None), P("dp", "seq"))
    return jax.shard_map(
        functools.partial(per_device, nd, ns),
        mesh=mesh,
        in_specs=in_specs,
        out_specs=out_specs,
        check_vma=False,
    )
```

time: 450 us -> 126 us (0.28)
  waiting for transfers between devices: 250 us -> 0 us
  Pallas kernels: 0 us -> 120 us
  local copies, waits for them, and re-layouts: 66.5 us -> 4.8 us
  blocking collectives: 45 us -> 0 us
  matrix products: 29.6 us -> 0 us
  other arithmetic: 23.9 us -> 0 us
  starting transfers between devices: 16.5 us -> 0 us
  between operations: 14.3 us -> 0.68 us
    reduce_scatter x1 -> x0, waiting for transfers between devices: 195 us -> none  [per_device(): lax.psum_scatter(partial_value.astype(jnp.bfloat16), 'seq', scatter_dimen...]
    pallas_call x0 -> x3, Pallas kernels: none -> 120 us  [the longest x1 51.9 us: per_device(): pl.pallas_call(functools.partial(return_kernel, nd, ns, ny, nz, tpd), out...]
    all_to_all x2 -> x0, blocking collectives: 45 us -> none  [the longest x1 26.4 us: per_device(): lax.all_to_all(head_grads, 'seq', split_axis=0, concat_axis=2, tiled=True)]
    all_to_all x2 -> x0, waiting for transfers between devices: 30.8 us -> none  [the longest x1 22.5 us: per_device(): lax.all_to_all(mapped_vectors, 'seq', split_axis=2, concat_axis=0, tiled=...]
    dot_general x15 -> x0, matrix products: 29.6 us -> none  [the longest x2 7.9 us: block_step(): jnp.einsum('rqhd,rkhd->rhqk', cot_now, values_now, preferred_element_type...]
    unnamed x3 -> x0, waiting for transfers between devices: 24 us -> none
    unnamed x23 -> x10, local copies, waits for them, and re-layouts: 21.7 us -> 4.7 us
    all_to_all x2 -> x0, starting transfers between devices: 16.2 us -> none  [the longest x1 11.5 us: per_device(): lax.all_to_all(mapped_vectors, 'seq', split_axis=2, concat_axis=0, tiled=...]
  transfers between devices with their start and end apart: 4 -> 0, of which waited for: 4 -> 0; matrix products, arithmetic and copies ran while one was open for 4% -> 0% of each run, Pallas kernels for 0% -> 0%
where the time goes in v1:
time: 126 us; the launch traced here: 125 us
  Pallas kernels  120 us (95%)
  local copies, waits for them, and re-layouts  4.8 us (4%)
    pallas_call x1, Pallas kernels, per_device(): pl.pallas_call(functools.partial(return_kernel, nd, ns, ny, nz, tpd), out...  51.9 us
    pallas_call x1, Pallas kernels, per_device(): pl.pallas_call(functools.partial(spread_kernel, nd, ns), out_shape=(jax.S...  34.5 us
    pallas_call x1, Pallas kernels, per_device(): pl.pallas_call(functools.partial(attend_kernel, ns), out_shape=jax.ShapeD...  33.4 us
    unnamed x10, local copies, waits for them, and re-layouts  4.7 us

profile of v1, /device:TPU:2, one launch (start us, length us, event | category | flops | bytes accessed | tf_op | source)
XLA Modules:
  0.0 125.3 jit_solution(9719001284570184733)
XLA Ops:
  0.6 0.0 copy-start.2
  0.6 0.8 copy.9
  1.4 0.1 reshape_squeeze.3.cols_ref
  1.5 0.0 copy-start
  1.5 0.9 copy-done
  2.5 0.0 copy-start.1
  2.5 0.9 copy-done.1
  3.4 34.5 %spread.1 = (bf16[32,128,128]{2,1,0:T(8,128)(2,1)S(1)}, bf16[1024,1024]{1,0:T(8,128)(2,1)S(1)}) custom-call(bf16[128,1024]{1,0:T(8,128)(2,1)S(1)} %bitcast.8, bf16[1024,3072]{1,0:T(8,128)(2,1)} %w_ref.3, bf16[128,1024]{1,0:T(8,128)(2,1)S(1)} %bitcast.9), custom_call_target="tpu_custom_call" | custom-call | tf_op jit(solution)/shard_map/spread/pallas_call | solution.py:443
  38.0 0.0 copy-done.2
  38.0 33.4 %attend.1.ret_ref = bf16[32,128,128]{2,1,0:T(8,128)(2,1)S(1)} custom-call(s32[128]{0:T(128)S(1)} %reshape_squeeze.3.cols_ref, s32[32]{0:T(128)S(1)} %bitcast.11, bf16[32,128,128]{2,1,0:T(8,128)(2,1)S(1)} %get-tuple-element.8.a_ref), custom_call_target="tpu_custom_call" | custom-call | tf_op jit(solution)/shard_map/attend/pallas_call | solution.py:467
  71.4 51.9 %give_back.1 = (bf16[128,1024]{1,0:T(8,128)(2,1)S(1)}, bf16[128,1024]{1,0:T(8,128)(2,1)S(1)}, f32[32,384]{1,0:T(8,128)S(1)}) custom-call(bf16[32,128,128]{2,1,0:T(8,128)(2,1)S(1)} %attend.1.ret_ref, bf16[1024,3072]{1,0:T(8,128)(2,1)} %w_ref.3, bf16[1024,1024]{1,0:T(8,128)(2,1)S(1)} %get-tuple-element.9.xt_ref), custom_call_target="tpu_custom_call" | custom-call | tf_op jit(solution)/shard_map/give_back/pallas_call | solution.py:479
  123.3 0.7 copy.13
  124.0 0.7 copy.14
  124.7 0.6 copy.15
Async XLA Ops:
  0.6 37.3 %copy-start.2 = (s32[1,32]{1,0:T(1,128)S(1)}, s32[1,32]{1,0:T(1,128)}, u32[]{:S(2)}) copy-start(s32[1,32]{1,0:T(1,128)} %param.9) | copy-start | bytes 388
  1.5 1.0 copy-start
  2.5 0.9 copy-start.1

commit v2 on v1

--- a/solution.py
+++ b/solution.py
@@ -14,7 +14,7 @@
 SLOTS = 4
 F32 = jnp.float32
 BF16 = jnp.bfloat16
-VMEM_LIMIT = 48 * 1024 * 1024
+VMEM_LIMIT = 62 * 1024 * 1024
 
 
 def lane_ids(shape):
@@ -64,7 +64,7 @@
 
 
 def spread_kernel(
-    nd, ns, x_ref, w_ref, do_ref, recv_ref, xt_all, w_vm, send_buf, xt_vm,
+    nd, ns, x_in, w_ref, do_in, recv_ref, xt_all, x_ref, do_ref, w_vm, send_buf, xt_vm,
     w_sem, send_sem, recv_sem, xs_sem, xr_sem, own_sem,
 ):
     me_d, me_s = lax.axis_index("dp"), lax.axis_index("seq")
@@ -84,8 +84,14 @@
             w_copy(i, m).start()
         return c
 
+    load_x = pltpu.make_async_copy(x_in.at[0], x_ref, own_sem.at[2])
+    load_do = pltpu.make_async_copy(do_in.at[0], do_ref, own_sem.at[3])
+    load_x.start()
+    load_do.start()
     lax.fori_loop(0, ng, w_start, 0)
     barrier = greet(me_d, me_s, nd, ns)
+    load_x.wait()
+    load_do.wait()
     xt_vm[...] = jnp.transpose(x_ref[...].astype(F32)).astype(BF16)
 
     def xt_slot(d):
@@ -169,73 +175,106 @@
     lax.fori_loop(1, nd, xt_wait, 0)
 
 
-def attend_kernel(nb, cols_ref, counts_ref, a_ref, out_ref, kvt, acc):
+def attend_kernel(
+    nb, cols_ref, counts_ref, a_ref, out_ref, turned_kv, left, right, col_acc, row_out,
+    raw_even, raw_odd, top_even, top_odd, pair_even, pair_odd,
+):
     scale = 1.0 / math.sqrt(FEAT)
     to_exp2 = scale * math.log2(math.e)
-    lane = lane_ids((BLK, BLK))
+    raw, top, pair = (raw_even, raw_odd), (top_even, top_odd), (pair_even, pair_odd)
+    quarter = lane_ids((BLK, BLK)) // FEAT
 
     def prepare(b, c):
-        kvt[b] = jnp.transpose(a_ref[b].astype(F32))[FEAT : 3 * FEAT].astype(BF16)
-        acc[b] = jnp.zeros((BLK, BLK), F32)
-        return c
-
-    lax.fori_loop(0, nb, prepare, 0)
-
-    def row_block(r, c):
-        mine = a_ref[r]
+        mine = a_ref[b]
         zero = jnp.zeros_like(mine)
-        quarter = lane // FEAT
-        left = jnp.concatenate(
-            [
-                jnp.where(quarter == 1, pltpu.roll(mine, 32, 1), zero),
-                jnp.where(quarter == 2, pltpu.roll(mine, 96, 1), zero),
-            ],
-            axis=0,
-        )
-        right = jnp.concatenate(
-            [
-                jnp.where(quarter == 3, mine, zero),
-                jnp.where(quarter == 2, pltpu.roll(mine, 64, 1), zero),
-            ],
-            axis=0,
-        )
-        count = counts_ref[r]
-        named = [cols_ref[r * SLOTS + s] for s in range(SLOTS)]
-        keys = jnp.concatenate([a_ref[n] for n in named], axis=0)
+        turned = jnp.transpose(mine.astype(F32)).astype(BF16)
+        empty = jnp.zeros((FEAT, BLK), BF16)
+        turned_kv[b] = turned[FEAT : 3 * FEAT]
+        left[b, :BLK] = jnp.where(quarter == 1, pltpu.roll(mine, 32, 1), zero)
+        left[b, BLK:] = jnp.where(quarter == 2, pltpu.roll(mine, 96, 1), zero)
+        right[b, :FEAT, :BLK] = empty
+        right[b, :FEAT, BLK:] = turned[:FEAT]
+        right[b, FEAT:, :BLK] = turned[3 * FEAT :]
+        right[b, FEAT:, BLK:] = empty
+        col_acc[b] = jnp.zeros((2 * FEAT, BLK), F32)
+        return c
+
+    lax.fori_loop(0, nb, prepare, 0, unroll=2)
+
+    def score_stage(r, p):
+        count = counts_ref[0, r]
+        keys = jnp.concatenate([a_ref[cols_ref[0, s, r]] for s in range(SLOTS)], axis=0)
         both = lax.dot_general(
-            keys, left, (((1,), (1,)), ((), ())), preferred_element_type=F32
-        )
-        scores = [
-            jnp.where(s < count, both[s * BLK : (s + 1) * BLK, :BLK], -jnp.inf)
-            for s in range(SLOTS)
-        ]
-        scores = jnp.concatenate(scores, axis=0)
-        grad_prob = both[:, BLK:]
-        top = jnp.max(scores, axis=0, keepdims=True)
-        weights = jnp.exp2((scores - top) * to_exp2)
-        prob = weights * (1.0 / jnp.sum(weights, axis=0, keepdims=True))
-        delta = jnp.sum(prob * grad_prob, axis=0, keepdims=True)
-        grad_score = prob * (grad_prob - delta) * scale
-        pair = jnp.concatenate([prob.astype(BF16), grad_score.astype(BF16)], axis=1)
-        key_side = jnp.dot(pair, right, preferred_element_type=F32)
+            keys, left[r], (((1,), (1,)), ((), ())), preferred_element_type=F32
+        )
+        best = None
         for s in range(SLOTS):
-            acc[named[s]] += key_side[s * BLK : (s + 1) * BLK]
-        turned = jnp.concatenate([kvt[n] for n in named], axis=1)
-        row_side = jnp.dot(turned, pair, preferred_element_type=F32)
-        row_side = jnp.concatenate(
-            [row_side[FEAT:, :BLK], row_side[:FEAT, BLK:], jnp.zeros((2 * FEAT, BLK), F32)],
-            axis=0,
-        )
-        acc[r] += jnp.transpose(row_side)
-        return c
-
-    lax.fori_loop(0, nb, row_block, 0)
+            block = both[s * BLK : (s + 1) * BLK]
+            scores = block[:, :BLK]
+            if s:
+                scores = jnp.where(s < count, scores, -jnp.inf)
+            raw[p][s, :, :BLK] = scores
+            raw[p][s, :, BLK:] = block[:, BLK:]
+            peak = jnp.max(scores, axis=0, keepdims=True)
+            best = peak if best is None else jnp.maximum(best, peak)
+        top[p][...] = best * to_exp2
+
+    def soft_stage(p):
+        peak = top[p][...]
+        total = mixed = None
+        for s in range(SLOTS):
+            weights = jnp.exp2(raw[p][s, :, :BLK] * to_exp2 - peak)
+            t = jnp.sum(weights, axis=0, keepdims=True)
+            m = jnp.sum(weights * raw[p][s, :, BLK:], axis=0, keepdims=True)
+            total = t if total is None else total + t
+            mixed = m if mixed is None else mixed + m
+            raw[p][s, :, :BLK] = weights
+        inverse = 1.0 / total
+        delta = mixed * inverse
+        for s in range(SLOTS):
+            prob = raw[p][s, :, :BLK] * inverse
+            rows = slice(s * BLK, (s + 1) * BLK)
+            pair[p][rows, :BLK] = prob.astype(BF16)
+            pair[p][rows, BLK:] = (prob * (raw[p][s, :, BLK:] - delta)).astype(BF16)
+
+    def grad_stage(r, p):
+        named = [cols_ref[0, s, r] for s in range(SLOTS)]
+        both = pair[p][...]
+        turned = jnp.concatenate([turned_kv[n] for n in named], axis=1)
+        row_side = jnp.dot(turned, both, preferred_element_type=F32)
+        row_out[r, :FEAT] = row_side[FEAT:, :BLK]
+        row_out[r, FEAT:] = row_side[:FEAT, BLK:]
+        key_side = lax.dot_general(
+            right[r], both, (((1,), (1,)), ((), ())), preferred_element_type=F32
+        )
+        for s in range(SLOTS):
+            col_acc[named[s]] += key_side[:, s * BLK : (s + 1) * BLK]
+
+    score_stage(0, 0)
+    score_stage(1, 1)
+    soft_stage(0)
+
+    def steps(i, c):
+        for u in range(2):
+            r, p = 1 + 2 * i + u, (1 + u) % 2
+            score_stage(r + 1, 1 - p)
+            soft_stage(p)
+            grad_stage(r - 1, 1 - p)
+        return c
+
+    lax.fori_loop(0, (nb - 2) // 2, steps, 0)
+    soft_stage(1)
+    grad_stage(nb - 2, 0)
+    grad_stage(nb - 1, 1)
+    part = lax.broadcasted_iota(jnp.int32, (BLK, BLK), 0) // FEAT
+    factor = jnp.where((part == 1) | (part == 2), scale, 1.0).astype(F32)
 
     def emit(b, c):
-        out_ref[b] = acc[b].astype(BF16)
-        return c
-
-    lax.fori_loop(0, nb, emit, 0)
+        whole = jnp.concatenate([row_out[b], col_acc[b]], axis=0) * factor
+        out_ref[b] = jnp.transpose(whole).astype(BF16)
+        return c
+
+    lax.fori_loop(0, nb, emit, 0, unroll=2)
 
 
 def return_kernel(
@@ -446,9 +485,11 @@
             jax.ShapeDtypeStruct((ns, BLK, BLK), BF16),
             jax.ShapeDtypeStruct((hidden, nd * BLK), BF16),
         ),
-        in_specs=[vm_spec, any_spec, vm_spec],
+        in_specs=[any_spec, any_spec, any_spec],
         out_specs=(any_spec, any_spec),
         scratch_shapes=[
+            pltpu.VMEM((rows, hidden), BF16),
+            pltpu.VMEM((rows, hidden), BF16),
             pltpu.VMEM((ng, hidden, 3 * BLK), BF16),
             pltpu.VMEM((ns, BLK, BLK), BF16),
             pltpu.VMEM((hidden, BLK), BF16),
@@ -457,13 +498,13 @@
             dma((ng, 4)),
             dma((nd,)),
             dma((nd,)),
-            dma((2,)),
+            dma((4,)),
         ],
         compiler_params=pltpu.CompilerParams(
             collective_id=1, has_side_effects=True, vmem_limit_bytes=VMEM_LIMIT
         ),
         name="spread",
-    )(nodes[0], w_qkv, incoming_adjoint[0])
+    )(nodes, w_qkv, incoming_adjoint)
     returned = pl.pallas_call(
         functools.partial(attend_kernel, ns),
         out_shape=jax.ShapeDtypeStruct((ns, BLK, BLK), BF16),
@@ -471,11 +512,20 @@
         out_specs=vm_spec,
         scratch_shapes=[
             pltpu.VMEM((ns, 2 * FEAT, BLK), BF16),
-            pltpu.VMEM((ns, BLK, BLK), F32),
+            pltpu.VMEM((ns, 2 * BLK, BLK), BF16),
+            pltpu.VMEM((ns, 2 * FEAT, 2 * BLK), BF16),
+            pltpu.VMEM((ns, 2 * FEAT, BLK), F32),
+            pltpu.VMEM((ns, 2 * FEAT, BLK), F32),
+            pltpu.VMEM((SLOTS, BLK, 2 * BLK), F32),
+            pltpu.VMEM((SLOTS, BLK, 2 * BLK), F32),
+            pltpu.VMEM((1, BLK), F32),
+            pltpu.VMEM((1, BLK), F32),
+            pltpu.VMEM((SLOTS * BLK, 2 * BLK), BF16),
+            pltpu.VMEM((SLOTS * BLK, 2 * BLK), BF16),
         ],
         compiler_params=pltpu.CompilerParams(vmem_limit_bytes=VMEM_LIMIT),
         name="attend",
-    )(block_cols[0].reshape(-1), block_counts[0], packed)
+    )(jnp.swapaxes(block_cols, 1, 2), block_counts, packed)
     mixture, grad_nodes, weight_grad = pl.pallas_call(
         functools.partial(return_kernel, nd, ns, ny, nz, tpd),
         out_shape=(

time: 126 us -> 108 us (0.86)
  Pallas kernels: 120 us -> 102 us
    pallas_call x1, Pallas kernels: 33.4 us -> 14.5 us  [per_device(): pl.pallas_call(functools.partial(attend_kernel, ns), out_shape=jax.ShapeD...]
    unnamed x10 -> x3, local copies, waits for them, and re-layouts: 4.7 us -> 4.76 us
where the time goes in v2:
time: 108 us; the launch traced here: 107 us
  Pallas kernels  102 us (94%)
  local copies, waits for them, and re-layouts  4.76 us (4%)
    pallas_call x1, Pallas kernels, per_device(): pl.pallas_call(functools.partial(return_kernel, nd, ns, ny, nz, tpd), out...  52.5 us
    pallas_call x1, Pallas kernels, per_device(): pl.pallas_call(functools.partial(spread_kernel, nd, ns), out_shape=(jax.S...  34.7 us
    pallas_call x1, Pallas kernels, per_device(): pl.pallas_call(functools.partial(attend_kernel, ns), out_shape=jax.ShapeD...  14.5 us
    unnamed x3, local copies, waits for them, and re-layouts  4.76 us

profile of v2, /device:TPU:2, one launch (start us, length us, event | category | flops | bytes accessed | tf_op | source)
XLA Modules:
  0.0 107.0 jit_solution(6036913341646313144)
XLA Ops:
  0.6 34.7 %spread.1 = (bf16[32,128,128]{2,1,0:T(8,128)(2,1)}, bf16[1024,1024]{1,0:T(8,128)(2,1)}) custom-call(bf16[1,128,1024]{2,1,0:T(8,128)(2,1)} %x_in.1, bf16[1024,3072]{1,0:T(8,128)(2,1)} %w_ref.3, bf16[1,128,1024]{2,1,0:T(8,128)(2,1)} %do_in.1), custom_call_target="tpu_custom_call" | custom-call | tf_op jit(solution)/shard_map/spread/pallas_call | solution.py:482
  35.3 14.5 %attend.1.ret_ref = bf16[32,128,128]{2,1,0:T(8,128)(2,1)} custom-call(s32[1,4,32]{2,1,0:T(4,128)} %bitcast.7, s32[1,32]{1,0:T(1,128)} %counts_ref.1, bf16[32,128,128]{2,1,0:T(8,128)(2,1)} %get-tuple-element.8.a_ref), custom_call_target="tpu_custom_call" | custom-call | tf_op jit(solution)/shard_map/attend/pallas_call | solution.py:508
  49.8 52.5 %give_back.1 = (bf16[128,1024]{1,0:T(8,128)(2,1)}, bf16[128,1024]{1,0:T(8,128)(2,1)}, f32[32,384]{1,0:T(8,128)}) custom-call(bf16[32,128,128]{2,1,0:T(8,128)(2,1)} %attend.1.ret_ref, bf16[1024,3072]{1,0:T(8,128)(2,1)} %w_ref.3, bf16[1024,1024]{1,0:T(8,128)(2,1)} %get-tuple-element.9.xt_ref), custom_call_target="tpu_custom_call" | custom-call | tf_op jit(solution)/shard_map/give_back/pallas_call | solution.py:529
  102.3 1.7 %copy.11 = bf16[1,128,1024]{2,1,0:T(8,128)(2,1)} copy(bf16[1,128,1024]{2,1,0:T(8,128)(2,1)} %bitcast.5) | data formatting | bytes 524288
  104.0 1.7 %copy.12 = bf16[1,128,1024]{2,1,0:T(8,128)(2,1)} copy(bf16[1,128,1024]{2,1,0:T(8,128)(2,1)} %bitcast.4) | data formatting | bytes 524288
  105.6 1.4 %copy.13 = f32[384,32]{0,1:T(8,128)} copy(f32[384,32]{0,1:T(8,128)} %bitcast.6) | data formatting | bytes 98304

commit v3 on v2

v3 whole, which is shorter than its diff:
```python
import functools
import math

import jax
import jax.numpy as jnp
from jax import lax
from jax.experimental import pallas as pl
from jax.experimental.pallas import tpu as pltpu
from jax.sharding import PartitionSpec as P

MESH = pl.DeviceIdType.MESH
BLK = 128
FEAT = 32
SLOTS = 4
F32 = jnp.float32
BF16 = jnp.bfloat16
VMEM_LIMIT = 62 * 1024 * 1024


def lane_ids(shape):
    return lax.broadcasted_iota(jnp.int32, shape, len(shape) - 1)


def swap_quarters(tiles):
    lane = lane_ids(tiles[0].shape)
    low = lane < 64
    even = (lane // 32) % 2 == 0
    a0, a1, a2, a3 = tiles
    b0 = jnp.where(low, a0, pltpu.roll(a2, 64, 1))
    b2 = jnp.where(low, pltpu.roll(a0, 64, 1), a2)
    b1 = jnp.where(low, a1, pltpu.roll(a3, 64, 1))
    b3 = jnp.where(low, pltpu.roll(a1, 64, 1), a3)
    return (
        jnp.where(even, b0, pltpu.roll(b1, 32, 1)),
        jnp.where(even, pltpu.roll(b0, 96, 1), b1),
        jnp.where(even, b2, pltpu.roll(b3, 32, 1)),
        jnp.where(even, pltpu.roll(b2, 96, 1), b3),
    )


def greet(me_d, me_s, nd, ns):
    barrier = pltpu.get_barrier_semaphore()

    def seq_hello(k, c):
        pl.semaphore_signal(
            barrier, inc=1, device_id=(me_d, lax.rem(me_s + k, ns)), device_id_type=MESH
        )
        return c

    def dp_hello(k, c):
        pl.semaphore_signal(
            barrier, inc=1, device_id=(lax.rem(me_d + k, nd), me_s), device_id_type=MESH
        )
        return c

    lax.fori_loop(1, ns, seq_hello, 0)
    lax.fori_loop(1, nd, dp_hello, 0)
    return barrier


def peer_at(me_s, i, j, ng, sign):
    group = lax.rem(me_s // 4 + sign * i + ng, ng)
    return 4 * group + lax.rem(me_s % 4 + sign * j + 4, 4)


def whole_kernel(
    nd, ns, ny, nz, tpd,
    x_in, w_in, cot_in, cols_ref, cols_vec, counts_ref,
    mix_ref, gn_ref, wg_ref,
    x_vm, cot_vm, w_vm, head_out, head_in, xt_own, xt_all,
    turned_kv, left, right, chain, row_out, col_out, row_in, col_in,
    raw_even, raw_odd, top_even, top_odd, pair_even, pair_odd,
    table_vm, table, dq, wg_in, part, relay, fold, mid, last_in,
    w_sem, load_sem, head_s, head_r, xt_s, xt_r, row_s, row_r, col_s, col_r,
    own_sem, tile_s, tile_r, tile_o, relay_s, relay_r, fold_s, fold_r, last_s, last_r,
):
    me_d, me_s = lax.axis_index("dp"), lax.axis_index("seq")
    me_y, me_z = me_s // nz, me_s % nz
    ng = ns // 4
    my_group = me_s // 4
    hidden = ng * BLK
    nb = ns
    scale = 1.0 / math.sqrt(FEAT)
    to_exp2 = scale * math.log2(math.e)

    def lanes(t):
        return pl.ds(pl.multiple_of(t * BLK, BLK), BLK)

    def sent_group(i):
        return lax.rem(my_group + i, ng)

    def got_group(i):
        return lax.rem(my_group - i + ng, ng)

    def row_at(k):
        return peer_at(me_s, k // 4, k % 4, ng, 1)

    def remote(src, dst, send_sem, recv_sem, d, s):
        return pltpu.make_async_remote_copy(
            src_ref=src, dst_ref=dst, send_sem=send_sem, recv_sem=recv_sem,
            device_id=(d, s), device_id_type=MESH,
        )

    load_x = pltpu.make_async_copy(x_in.at[0], x_vm, load_sem.at[0])
    load_cot = pltpu.make_async_copy(cot_in.at[0], cot_vm, load_sem.at[1])
    load_x.start()

    def w_copy(i, m):
        g = sent_group(i)
        return pltpu.make_async_copy(
            w_in.at[:, lanes(m * ng + g)],
            w_vm.at[g, :, pl.ds(m * BLK, BLK)],
            w_sem.at[i, m],
        )

    def w_start(i, c):
        for m in range(3):
            w_copy(i, m).start()
        return c

    w_start(0, 0)
    load_cot.start()
    lax.fori_loop(1, ng, w_start, 0)
    barrier = greet(me_d, me_s, nd, ns)
    load_x.wait()
    load_cot.wait()

    def head_copy(i, j):
        peer = peer_at(me_s, i, j, ng, 1)
        return remote(
            head_out.at[peer], head_in.at[me_s], head_s.at[i, j], head_r.at[i, j], me_d, peer
        )

    own_head = pltpu.make_async_copy(head_out.at[me_s], head_in.at[me_s], own_sem.at[0])

    def project(i, c):
        g = sent_group(i)
        for m in range(3):
            w_copy(i, m).wait()
        qkv = jnp.dot(x_vm[...], w_vm[g], preferred_element_type=F32).astype(BF16)
        packed = swap_quarters(
            (qkv[:, :BLK], qkv[:, BLK : 2 * BLK], qkv[:, 2 * BLK :], cot_vm[:, lanes(g)])
        )
        for j in range(4):
            head_out[4 * g + j] = packed[j]

        @pl.when(i == 0)
        def _():
            pl.semaphore_wait(barrier, ns + nd - 2)
            own_head.start()

        @pl.when(i > 0)
        def _():
            head_copy(i, 0).start()

        for j in range(1, 4):
            head_copy(i, j).start()
        return c

    lax.fori_loop(0, ng, project, 0)

    xt_own[...] = jnp.transpose(x_vm[...].astype(F32)).astype(BF16)
    xt_keep = pltpu.make_async_copy(xt_own, xt_all.at[:, lanes(me_d)], own_sem.at[1])
    xt_keep.start()

    def xt_copy(k):
        return remote(
            xt_own, xt_all.at[:, lanes(me_d)], xt_s.at[k], xt_r.at[k],
            lax.rem(me_d + k, nd), me_s,
        )

    def xt_start(k, c):
        xt_copy(k).start()
        return c

    lax.fori_loop(1, nd, xt_start, 0)

    named_now = cols_vec[...]
    row_ids = lane_ids((SLOTS, nb))
    place = 4 * lax.rem(row_ids // 4 - my_group + ng, ng) + lax.rem(
        row_ids % 4 - me_s % 4 + 4, 4
    )
    col_ids = lane_ids((1, nb))

    def link(k, carry):
        before, final = carry
        r = row_at(k)
        for s in range(SLOTS):
            name = cols_ref[0, s, r]
            before = jnp.where((named_now == name) & (place > k), 4 * k + s, before)
            final = jnp.where(col_ids == name, 4 * k + s, final)
        return before, final

    before, final = lax.fori_loop(
        0, nb, link,
        (jnp.full((SLOTS, nb), SLOTS * nb, jnp.int32), jnp.zeros((1, nb), jnp.int32)),
    )
    table_vm[...] = jnp.zeros_like(table_vm)
    table_vm[:SLOTS, :nb] = before
    table_vm[SLOTS : SLOTS + 1, :nb] = final
    table_copy = pltpu.make_async_copy(table_vm, table, own_sem.at[2])
    table_copy.start()
    chain[SLOTS * nb] = jnp.zeros((2 * FEAT, BLK), F32)

    raw, top, pair = (raw_even, raw_odd), (top_even, top_odd), (pair_even, pair_odd)
    quarter = lane_ids((BLK, BLK)) // FEAT

    def prepare(b):
        mine = head_in[b]
        zero = jnp.zeros_like(mine)
        turned = jnp.transpose(mine.astype(F32)).astype(BF16)
        empty = jnp.zeros((FEAT, BLK), BF16)
        turned_kv[b] = turned[FEAT : 3 * FEAT]
        left[b, :BLK] = jnp.where(quarter == 1, pltpu.roll(mine, 32, 1), zero)
        left[b, BLK:] = jnp.where(quarter == 2, pltpu.roll(mine, 96, 1), zero)
        right[b, :FEAT, :BLK] = empty
        right[b, :FEAT, BLK:] = turned[:FEAT]
        right[b, FEAT:, :BLK] = turned[3 * FEAT :]
        right[b, FEAT:, BLK:] = empty

    def arrive(i, c):
        for j in range(4):
            if j == 0:

                @pl.when(i == 0)
                def _():
                    own_head.wait()

                @pl.when(i > 0)
                def _():
                    head_copy(i, 0).wait_recv()

            else:
                head_copy(i, j).wait_recv()
            prepare(4 * got_group(i) + lax.rem(me_s % 4 - j + 4, 4))
        return c

    lax.fori_loop(0, ng, arrive, 0)
    table_copy.wait()

    def score_stage(k, p):
        r = row_at(k)
        count = counts_ref[0, r]
        keys = jnp.concatenate([head_in[cols_ref[0, s, r]] for s in range(SLOTS)], axis=0)
        both = lax.dot_general(
            keys, left[r], (((1,), (1,)), ((), ())), preferred_element_type=F32
        )
        best = None
        for s in range(SLOTS):
            block = both[s * BLK : (s + 1) * BLK]
            scores = block[:, :BLK]
            if s:
                scores = jnp.where(s < count, scores, -jnp.inf)
            raw[p][s, :, :BLK] = scores
            raw[p][s, :, BLK:] = block[:, BLK:]
            peak = jnp.max(scores, axis=0, keepdims=True)
            best = peak if best is None else jnp.maximum(best, peak)
        top[p][...] = best * to_exp2

    def soft_stage(p):
        peak = top[p][...]
        total = mixed = None
        for s in range(SLOTS):
            weights = jnp.exp2(raw[p][s, :, :BLK] * to_exp2 - peak)
            t = jnp.sum(weights, axis=0, keepdims=True)
            m = jnp.sum(weights * raw[p][s, :, BLK:], axis=0, keepdims=True)
            total = t if total is None else total + t
            mixed = m if mixed is None else mixed + m
            raw[p][s, :, :BLK] = weights
        inverse = 1.0 / total
        delta = mixed * inverse
        for s in range(SLOTS):
            prob = raw[p][s, :, :BLK] * inverse
            rows = slice(s * BLK, (s + 1) * BLK)
            pair[p][rows, :BLK] = prob.astype(BF16)
            pair[p][rows, BLK:] = (prob * (raw[p][s, :, BLK:] - delta)).astype(BF16)

    def grad_stage(k, p):
        r = row_at(k)
        named = [cols_ref[0, s, r] for s in range(SLOTS)]
        both = pair[p][...]
        turned = jnp.concatenate([turned_kv[n] for n in named], axis=1)
        row_side = jnp.dot(turned, both, preferred_element_type=F32)
        row_out[r, :FEAT] = row_side[FEAT:, :BLK].astype(BF16)
        row_out[r, FEAT:] = (row_side[:FEAT, BLK:] * scale).astype(BF16)
        key_side = lax.dot_general(
            right[r], both, (((1,), (1,)), ((), ())), preferred_element_type=F32
        )
        for s in range(SLOTS):
            chain[4 * k + s] = key_side[:, s * BLK : (s + 1) * BLK] + chain[table[s, r]]

    def row_copy(i, j):
        peer = peer_at(me_s, i, j, ng, 1)
        return remote(
            row_out.at[peer], row_in.at[me_s], row_s.at[i, j], row_r.at[i, j], me_d, peer
        )

    def col_copy(i, j):
        peer = peer_at(me_s, i, j, ng, 1)
        return remote(
            col_out.at[peer], col_in.at[me_s], col_s.at[i, j], col_r.at[i, j], me_d, peer
        )

    own_row = pltpu.make_async_copy(row_out.at[me_s], row_in.at[me_s], own_sem.at[3])
    own_col = pltpu.make_async_copy(col_out.at[me_s], col_in.at[me_s], own_sem.at[4])
    score_stage(0, 0)
    score_stage(1, 1)
    soft_stage(0)

    def steps(i, c):
        @pl.when(i > 1)
        def _():
            row_copy((i - 1) // 2, 2 * ((i - 1) % 2)).start()

        @pl.when(i > 0)
        def _():
            row_copy((i - 1) // 2, 2 * ((i - 1) % 2) + 1).start()

        for u in range(2):
            k, p = 1 + 2 * i + u, (1 + u) % 2
            score_stage(k + 1, 1 - p)
            soft_stage(p)
            grad_stage(k - 1, 1 - p)
        return c

    lax.fori_loop(0, (nb - 2) // 2, steps, 0)
    own_row.start()
    row_copy(ng - 1, 0).start()
    row_copy(ng - 1, 1).start()
    soft_stage(1)
    grad_stage(nb - 2, 0)
    grad_stage(nb - 1, 1)
    row_copy(ng - 1, 2).start()
    row_copy(ng - 1, 3).start()

    def col_send(i, c):
        for j in range(4):
            peer = peer_at(me_s, i, j, ng, 1)
            total = chain[table[SLOTS, peer]]
            col_out[peer, :FEAT] = (total[:FEAT] * scale).astype(BF16)
            col_out[peer, FEAT:] = total[FEAT:].astype(BF16)
            if j == 0:

                @pl.when(i == 0)
                def _():
                    own_col.start()

                @pl.when(i > 0)
                def _():
                    col_copy(i, 0).start()

            else:
                col_copy(i, j).start()
        return c

    lax.fori_loop(0, ng, col_send, 0)

    def tile_own(g, m):
        t = m * ng + g
        return pltpu.make_async_copy(
            dq.at[g, pl.ds(m * BLK, BLK)], wg_in.at[t % tpd, :, lanes(me_d)],
            tile_o.at[t % tpd],
        )

    def tile_copy(g, m):
        t = m * ng + g
        return remote(
            dq.at[g, pl.ds(m * BLK, BLK)], wg_in.at[t % tpd, :, lanes(me_d)],
            tile_s.at[g, m], tile_r.at[me_d, t % tpd], t // tpd, me_s,
        )

    def tile_send(g, m):
        t = m * ng + g

        @pl.when(t // tpd == me_d)
        def _():
            tile_own(g, m).start()

        @pl.when(t // tpd != me_d)
        def _():
            tile_copy(g, m).start()

    def await_group(i, own, copy):
        @pl.when(i == 0)
        def _():
            own.wait()

        @pl.when(i > 0)
        def _():
            copy(i, 0).wait_recv()

        for j in range(1, 4):
            copy(i, j).wait_recv()

    def take_rows(i, c):
        g = got_group(i)
        await_group(i, own_row, row_copy)
        mix = jnp.concatenate([row_in[4 * g + j, :FEAT] for j in range(4)], axis=0)
        mix_ref[:, lanes(g)] = jnp.transpose(mix.astype(F32)).astype(BF16)
        for j in range(4):
            dq[g, j * FEAT : (j + 1) * FEAT] = row_in[4 * g + j, FEAT:]
        tile_send(g, 0)
        return c

    def take_cols(i, c):
        g = got_group(i)
        await_group(i, own_col, col_copy)
        for j in range(4):
            dq[g, BLK + j * FEAT : BLK + (j + 1) * FEAT] = col_in[4 * g + j, :FEAT]
            dq[g, 2 * BLK + j * FEAT : 2 * BLK + (j + 1) * FEAT] = col_in[4 * g + j, FEAT:]
        tile_send(g, 1)
        tile_send(g, 2)
        return c

    lax.fori_loop(0, ng, take_rows, 0)
    lax.fori_loop(0, ng, take_cols, 0)
    xt_keep.wait()

    def xt_wait(k, c):
        xt_copy(k).wait()
        return c

    lax.fori_loop(1, nd, xt_wait, 0)

    chunk = nz * FEAT
    half = chunk // 2
    up, down = lax.rem(me_y + 1, ny), lax.rem(me_y + ny - 1, ny)
    across = lax.rem(me_y + 2, ny)

    def rows_of(y, which):
        return pl.ds(pl.multiple_of(y * chunk + which * half, half), half)

    def relay_copy(t, way):
        return remote(
            part.at[t, rows_of(across, way)], relay.at[t, way],
            relay_s.at[t, way], relay_r.at[t, way], me_d, (up, down)[way] * nz + me_z,
        )

    def fold_copy(t, way, which):
        return remote(
            part.at[t, rows_of((up, down)[way], which)], fold.at[t, way, which],
            fold_s.at[t, way, which], fold_r.at[t, way, which],
            me_d, (up, down)[way] * nz + me_z,
        )

    def last_copy(t, k):
        to = lax.rem(me_z + k, nz)
        return remote(
            mid.at[t, pl.ds(pl.multiple_of(to * FEAT, FEAT), FEAT)], last_in.at[t, k - 1],
            last_s.at[t, k], last_r.at[t, k], me_d, me_y * nz + to,
        )

    def tile_done(t, k):
        src = lax.rem(me_d + k, nd)
        return remote(
            dq.at[0, pl.ds(0, BLK)], wg_in.at[t, :, lanes(src)],
            tile_s.at[0, 0], tile_r.at[src, t], src, me_s,
        )

    for t in range(tpd):
        pltpu.make_async_copy(
            dq.at[0, pl.ds(0, BLK)], wg_in.at[t, :, lanes(me_d)], tile_o.at[t]
        ).wait()

        def arrived(k, c):
            tile_done(t, k).wait_recv()
            return c

        lax.fori_loop(1, nd, arrived, 0)
        part[t] = lax.dot_general(
            xt_all[...], wg_in[t], (((1,), (1,)), ((), ())), preferred_element_type=F32
        ).astype(BF16)
        for way in range(2):
            relay_copy(t, way).start()
            fold_copy(t, way, 1 - way).start()

    def node_cols(n, c):
        width = 2 * BLK
        cols = pl.ds(pl.multiple_of(n * width, width), width)
        total = jnp.zeros((width, BLK), F32)
        for g in range(ng):
            total += jnp.dot(w_vm[g, cols], dq[g], preferred_element_type=F32)
        gn_ref[:, cols] = jnp.transpose(total).astype(BF16)
        return c

    steps_gn = hidden // (2 * BLK)
    lax.fori_loop(0, steps_gn // 2, node_cols, 0)
    for t in range(tpd):
        for way in range(2):
            relay_copy(t, way).wait_recv()
            rows = rows_of((up, down)[way], way)
            part[t, rows] = (
                part[t, rows].astype(F32) + relay[t, way].astype(F32)
            ).astype(BF16)
            fold_copy(t, way, way).start()
    lax.fori_loop(steps_gn // 2, steps_gn, node_cols, 0)
    for t in range(tpd):
        for which in range(2):
            total = part[t, rows_of(me_y, which)].astype(F32)
            for way in range(2):
                fold_copy(t, way, which).wait_recv()
                total += fold[t, way, which].astype(F32)
            mid[t, which * half : (which + 1) * half] = total.astype(BF16)
        for k in range(1, nz):
            last_copy(t, k).start()
    for t in range(tpd):
        total = mid[t, pl.ds(pl.multiple_of(me_z * FEAT, FEAT), FEAT)].astype(F32)
        for k in range(1, nz):
            last_copy(t, k).wait_recv()
            total += last_in[t, k - 1].astype(F32)
        wg_ref[:, t * BLK : (t + 1) * BLK] = total

    def sent(i, c):
        for copy in (head_copy, row_copy, col_copy):

            @pl.when(i > 0)
            def _():
                copy(i, 0).wait_send()

            for j in range(1, 4):
                copy(i, j).wait_send()
        for m in range(3):

            @pl.when((m * ng + i) // tpd != me_d)
            def _():
                tile_copy(i, m).wait_send()

        return c

    lax.fori_loop(0, ng, sent, 0)
    for t in range(tpd):
        for way in range(2):
            relay_copy(t, way).wait_send()
            for which in range(2):
                fold_copy(t, way, which).wait_send()
        for k in range(1, nz):
            last_copy(t, k).wait_send()


def per_device(nd, ns, nodes, w_qkv, incoming_adjoint, block_cols, block_counts):
    rows, hidden = nodes.shape[1:]
    ny, nz = 4, ns // 4
    ng = ns // 4
    tpd = 3 * ng // nd
    chunk = nz * FEAT
    hbm = pl.BlockSpec(memory_space=pltpu.HBM)
    vm_spec = pl.BlockSpec(memory_space=pltpu.VMEM)
    sm_spec = pl.BlockSpec(memory_space=pltpu.SMEM)
    dma = pltpu.SemaphoreType.DMA
    slots_first = jnp.swapaxes(block_cols, 1, 2)
    mixture, grad_nodes, weight_grad = pl.pallas_call(
        functools.partial(whole_kernel, nd, ns, ny, nz, tpd),
        out_shape=(
            jax.ShapeDtypeStruct((rows, hidden), BF16),
            jax.ShapeDtypeStruct((rows, hidden), BF16),
            jax.ShapeDtypeStruct((FEAT, tpd * BLK), F32),
        ),
        in_specs=[hbm, hbm, hbm, sm_spec, vm_spec, sm_spec],
        out_specs=(vm_spec, vm_spec, vm_spec),
        scratch_shapes=[
            pltpu.VMEM((rows, hidden), BF16),
            pltpu.VMEM((rows, hidden), BF16),
            pltpu.VMEM((ng, hidden, 3 * BLK), BF16),
            pltpu.VMEM((ns, BLK, BLK), BF16),
            pltpu.VMEM((ns, BLK, BLK), BF16),
            pltpu.VMEM((hidden, BLK), BF16),
            pltpu.VMEM((hidden, nd * BLK), BF16),
            pltpu.VMEM((ns, 2 * FEAT, BLK), BF16),
            pltpu.VMEM((ns, 2 * BLK, BLK), BF16),
            pltpu.VMEM((ns, 2 * FEAT, 2 * BLK), BF16),
            pltpu.VMEM((SLOTS * ns + 1, 2 * FEAT, BLK), F32),
            pltpu.VMEM((ns, 2 * FEAT, BLK), BF16),
            pltpu.VMEM((ns, 2 * FEAT, BLK), BF16),
            pltpu.VMEM((ns, 2 * FEAT, BLK), BF16),
            pltpu.VMEM((ns, 2 * FEAT, BLK), BF16),
            pltpu.VMEM((SLOTS, BLK, 2 * BLK), F32),
            pltpu.VMEM((SLOTS, BLK, 2 * BLK), F32),
            pltpu.VMEM((1, BLK), F32),
            pltpu.VMEM((1, BLK), F32),
            pltpu.VMEM((SLOTS * BLK, 2 * BLK), BF16),
            pltpu.VMEM((SLOTS * BLK, 2 * BLK), BF16),
            pltpu.VMEM((8, BLK), jnp.int32),
            pltpu.SMEM((8, BLK), jnp.int32),
            pltpu.VMEM((ng, 3 * BLK, BLK), BF16),
            pltpu.VMEM((tpd, BLK, nd * BLK), BF16),
            pltpu.VMEM((tpd, hidden, BLK), BF16),
            pltpu.VMEM((tpd, 2, chunk // 2, BLK), BF16),
            pltpu.VMEM((tpd, 2, 2, chunk // 2, BLK), BF16),
            pltpu.VMEM((tpd, chunk, BLK), BF16),
            pltpu.VMEM((tpd, nz - 1, FEAT, BLK), BF16),
            dma((ng, 3)),
            dma((2,)),
            dma((ng, 4)),
            dma((ng, 4)),
            dma((nd,)),
            dma((nd,)),
            dma((ng, 4)),
            dma((ng, 4)),
            dma((ng, 4)),
            dma((ng, 4)),
            dma((5,)),
            dma((ng, 3)),
            dma((nd, tpd)),
            dma((tpd,)),
            dma((tpd, 2)),
            dma((tpd, 2)),
            dma((tpd, 2, 2)),
            dma((tpd, 2, 2)),
            dma((tpd, nz)),
            dma((tpd, nz)),
        ],
        compiler_params=pltpu.CompilerParams(
            collective_id=1, has_side_effects=True, vmem_limit_bytes=VMEM_LIMIT
        ),
        name="whole",
    )(nodes, w_qkv, incoming_adjoint, slots_first, slots_first[0], block_counts)
    return (mixture[None], grad_nodes[None], jnp.transpose(weight_grad))


def solution(mesh):
    nd, ns = mesh.shape["dp"], mesh.shape["seq"]
    in_specs = (P("dp", "seq", None), P(), P("dp", "seq", None), P("dp", None, None), P("dp", None))
    out_specs = (P("dp", "seq", None), P("dp", "seq", None), P("dp", "seq"))
    return jax.shard_map(
        functools.partial(per_device, nd, ns),
        mesh=mesh,
        in_specs=in_specs,
        out_specs=out_specs,
        check_vma=False,
    )
```

time: 108 us -> 92.9 us (0.86)
  Pallas kernels: 102 us -> 87 us
    pallas_call x3 -> x1, Pallas kernels: 102 us -> 87 us  [per_device(): pl.pallas_call(functools.partial(whole_kernel, nd, ns, ny, nz, tpd), out_...]
where the time goes in v3:
time: 92.9 us; the launch traced here: 92.4 us
  Pallas kernels  87 us (94%)
  local copies, waits for them, and re-layouts  4.76 us (5%)
    pallas_call x1, Pallas kernels, per_device(): pl.pallas_call(functools.partial(whole_kernel, nd, ns, ny, nz, tpd), out_...  87 us
    unnamed x3, local copies, waits for them, and re-layouts  4.76 us

profile of v3, /device:TPU:2, one launch (start us, length us, event | category | flops | bytes accessed | tf_op | source)
XLA Modules:
  0.0 92.4 jit_solution(6504607642427900188)
XLA Ops:
  0.6 87.0 %whole.1 = (bf16[128,1024]{1,0:T(8,128)(2,1)}, bf16[128,1024]{1,0:T(8,128)(2,1)}, f32[32,384]{1,0:T(8,128)}) custom-call(bf16[1,128,1024]{2,1,0:T(8,128)(2,1)} %x_in.1, bf16[1024,3072]{1,0:T(8,128)(2,1)} %w_in.1, bf16[1,128,1024]{2,1,0:T(8,128)(2,1)} %cot_in.1, s32[1,4,32]{2,1,0:T(4,128)} %bitcast.9, s32[4,32]{1,0:T(4,128)} %bitcast.10, s32[1,32]{1,0:T(1,128)} %counts_ref.1), custom_call_target="tpu_custom_call" | custom-call | tf_op jit(solution)/shard_map/whole/pallas_call | solution.py:551
  87.7 1.7 %copy.11 = bf16[1,128,1024]{2,1,0:T(8,128)(2,1)} copy(bf16[1,128,1024]{2,1,0:T(8,128)(2,1)} %bitcast.7) | data formatting | bytes 524288
  89.3 1.7 %copy.12 = bf16[1,128,1024]{2,1,0:T(8,128)(2,1)} copy(bf16[1,128,1024]{2,1,0:T(8,128)(2,1)} %bitcast.6) | data formatting | bytes 524288
  91.0 1.4 %copy.13 = f32[384,32]{0,1:T(8,128)} copy(f32[384,32]{0,1:T(8,128)} %bitcast.8) | data formatting | bytes 98304

commit v4 on v3

v4 whole, which is shorter than its diff:
```python
import functools
import math

import jax
import jax.numpy as jnp
from jax import lax
from jax.experimental import pallas as pl
from jax.experimental.pallas import tpu as pltpu
from jax.sharding import PartitionSpec as P

MESH = pl.DeviceIdType.MESH
BLK = 128
FEAT = 32
SLOTS = 4
F32 = jnp.float32
BF16 = jnp.bfloat16
VMEM_LIMIT = 62 * 1024 * 1024


def lane_ids(shape):
    return lax.broadcasted_iota(jnp.int32, shape, len(shape) - 1)


def peer_at(me_s, i, j, ng, sign):
    group = lax.rem(me_s // 4 + sign * i + ng, ng)
    return 4 * group + lax.rem(me_s % 4 + sign * j + 4, 4)


def flip(tile):
    return jnp.transpose(tile.astype(F32)).astype(BF16)


def whole_kernel(
    nd, ns, ny, nz,
    x_in, w_in, cot_in, cols_ref, cols_vec, counts_ref,
    mix_out, gn_out, wg_ref,
    x_vm, cot_vm, cot_t, w_vm, head_out, head_in, natural, xt_own, xt_all,
    left, right, chain, row_out, col_out, row_in, col_in,
    raw_even, raw_odd, top_even, top_odd, pair_even, pair_odd,
    table_vm, table, dq, wg_in, part, y_in, mid, last_in, mix_vm, gn_acc, gn_vm,
    w_sem, load_sem, cot_s, cot_r, head_s, head_r, xt_s, xt_r, share_s, share_r,
    row_s, row_r, col_s, col_r, own_sem, tile_s, tile_r, tile_o,
    ys_sem, yr_sem, last_s, last_r, last_o, out_sem,
):
    me_d, me_s = lax.axis_index("dp"), lax.axis_index("seq")
    me_y, me_z = me_s // nz, me_s % nz
    ng = ns // 4
    my_group = me_s // 4
    hidden = ng * BLK
    nb = ns
    scale = 1.0 / math.sqrt(FEAT)
    to_exp2 = scale * math.log2(math.e)

    def lanes(t):
        return pl.ds(pl.multiple_of(t * BLK, BLK), BLK)

    def sent_group(i):
        return lax.rem(my_group + i, ng)

    def got_group(i):
        return lax.rem(my_group - i + ng, ng)

    def row_at(k):
        return peer_at(me_s, k // 4, k % 4, ng, 1)

    def remote(src, dst, send_sem, recv_sem, d, s):
        return pltpu.make_async_remote_copy(
            src_ref=src, dst_ref=dst, send_sem=send_sem, recv_sem=recv_sem,
            device_id=(d, s), device_id_type=MESH,
        )

    def owner(m):
        return (m * ng + me_d) // 3, (m * ng + me_d) % 3

    def source(u):
        return lax.rem(3 * me_d + u, ng)

    barrier = pltpu.get_barrier_semaphore()

    def hello(d, s):
        pl.semaphore_signal(barrier, inc=1, device_id=(d, s), device_id_type=MESH)

    def seq_hello(k, c):
        hello(me_d, lax.rem(me_s + k, ns))
        return c

    def dp_hello(k, c):
        hello(lax.rem(me_d + k, nd), me_s)
        return c

    lax.fori_loop(1, ns, seq_hello, 0)
    lax.fori_loop(1, nd, dp_hello, 0)
    greeted = ns + nd - 2
    for u in range(3):

        @pl.when(source(u) != me_d)
        def _():
            def z_hello(z, c):
                hello(source(u), me_y * nz + z)
                return c

            lax.fori_loop(0, nz, z_hello, 0)

        greeted += nz * (owner(u)[0] != me_d).astype(jnp.int32)

    load_x = pltpu.make_async_copy(x_in.at[0], x_vm, load_sem.at[0])
    load_cot = pltpu.make_async_copy(cot_in.at[0], cot_vm, load_sem.at[1])
    load_cot.start()
    load_x.start()

    def w_copy(i, m):
        g = sent_group(i)
        return pltpu.make_async_copy(
            w_in.at[:, lanes(m * ng + g)], w_vm.at[m, :, lanes(g)], w_sem.at[i, m]
        )

    def w_start(i, c):
        for m in range(3):
            w_copy(i, m).start()
        return c

    lax.fori_loop(0, ng, w_start, 0)
    load_cot.wait()

    def cot_flip(g, c):
        cot_t[lanes(g)] = flip(cot_vm[:, lanes(g)])
        return c

    lax.fori_loop(0, ng, cot_flip, 0)

    def cot_rows(s):
        return cot_t.at[pl.ds(pl.multiple_of(s * FEAT, FEAT), FEAT)]

    def cot_copy(i, j):
        peer = peer_at(me_s, i, j, ng, 1)
        return remote(
            cot_rows(peer), head_in.at[me_s, pl.ds(3 * FEAT, FEAT)],
            cot_s.at[i, j], cot_r.at[i, j], me_d, peer,
        )

    def head_copy(i, j):
        peer = peer_at(me_s, i, j, ng, 1)
        return remote(
            head_out.at[peer], head_in.at[me_s, pl.ds(0, 3 * FEAT)],
            head_s.at[i, j], head_r.at[i, j], me_d, peer,
        )

    own_cot = pltpu.make_async_copy(
        cot_rows(me_s), head_in.at[me_s, pl.ds(3 * FEAT, FEAT)], own_sem.at[5]
    )
    own_head = pltpu.make_async_copy(
        head_out.at[me_s], head_in.at[me_s, pl.ds(0, 3 * FEAT)], own_sem.at[0]
    )

    def start_group(i, own, copy):
        @pl.when(i == 0)
        def _():
            own.start()

        @pl.when(i > 0)
        def _():
            copy(i, 0).start()

        for j in range(1, 4):
            copy(i, j).start()

    def await_group(i, own, copy):
        @pl.when(i == 0)
        def _():
            own.wait()

        @pl.when(i > 0)
        def _():
            copy(i, 0).wait_recv()

        for j in range(1, 4):
            copy(i, j).wait_recv()

    pl.semaphore_wait(barrier, greeted)

    def cot_send(i, c):
        start_group(i, own_cot, cot_copy)
        return c

    lax.fori_loop(0, ng, cot_send, 0)
    load_x.wait()

    def project(i, c):
        g = sent_group(i)
        for m in range(3):
            w_copy(i, m).wait()
            flat = jnp.dot(x_vm[...], w_vm[m, :, lanes(g)], preferred_element_type=F32)
            turned = jnp.transpose(flat).astype(BF16)
            for j in range(4):
                head_out[4 * g + j, m * FEAT : (m + 1) * FEAT] = turned[
                    j * FEAT : (j + 1) * FEAT
                ]
        start_group(i, own_head, head_copy)
        return c

    lax.fori_loop(0, ng, project, 0)

    xt_own[...] = flip(x_vm[...])
    xt_keep = pltpu.make_async_copy(xt_own, xt_all.at[:, lanes(me_d)], own_sem.at[1])
    xt_keep.start()
    sibling = me_d + 1 - 2 * (me_d % 2)

    def xt_copy(k):
        return remote(
            xt_own, xt_all.at[:, lanes(me_d)], xt_s.at[k], xt_r.at[k],
            lax.rem(me_d + 2 * k, nd), me_s,
        )

    def share_copy(k):
        here = lanes(lax.rem(me_d - 2 * k + nd, nd))
        return remote(
            xt_all.at[:, here] if k else xt_own, xt_all.at[:, here],
            share_s.at[k], share_r.at[k], sibling, me_s,
        )

    for k in range(1, nd // 2):
        xt_copy(k).start()
    share_copy(0).start()

    named_now = cols_vec[...]
    row_ids = lane_ids((SLOTS, nb))
    place = 4 * lax.rem(row_ids // 4 - my_group + ng, ng) + lax.rem(
        row_ids % 4 - me_s % 4 + 4, 4
    )
    col_ids = lane_ids((1, nb))

    def link(k, carry):
        before, final = carry
        r = row_at(k)
        for s in range(SLOTS):
            name = cols_ref[0, s, r]
            before = jnp.where((named_now == name) & (place > k), 4 * k + s, before)
            final = jnp.where(col_ids == name, 4 * k + s, final)
        return before, final

    before, final = lax.fori_loop(
        0, nb, link,
        (jnp.full((SLOTS, nb), SLOTS * nb, jnp.int32), jnp.zeros((1, nb), jnp.int32)),
    )
    table_vm[...] = jnp.zeros_like(table_vm)
    table_vm[:SLOTS, :nb] = before
    table_vm[SLOTS : SLOTS + 1, :nb] = final
    table_copy = pltpu.make_async_copy(table_vm, table, own_sem.at[2])
    table_copy.start()
    chain[SLOTS * nb] = jnp.zeros((2 * FEAT, BLK), F32)

    def blank(b, c):
        left[b] = jnp.zeros((BLK, 2 * BLK), BF16)
        right[b] = jnp.zeros((2 * FEAT, 2 * BLK), BF16)
        return c

    lax.fori_loop(0, nb, blank, 0)

    raw, top, pair = (raw_even, raw_odd), (top_even, top_odd), (pair_even, pair_odd)

    def arrive(i, c):
        await_group(i, own_cot, cot_copy)
        await_group(i, own_head, head_copy)
        for j in range(4):
            b = 4 * got_group(i) + lax.rem(me_s % 4 - j + 4, 4)
            turned = head_in[b]
            queries, cot = turned[:FEAT], turned[3 * FEAT :]
            natural[b] = flip(turned)
            left[b, FEAT : 2 * FEAT, :BLK] = queries
            left[b, 2 * FEAT : 3 * FEAT, BLK:] = cot
            right[b, :FEAT, BLK:] = queries
            right[b, FEAT:, :BLK] = cot
        return c

    lax.fori_loop(0, ng, arrive, 0)
    table_copy.wait()
    for k in range(1, nd // 2):
        xt_copy(k).wait_recv()
        share_copy(k).start()

    def score_stage(k, p):
        r = row_at(k)
        count = counts_ref[0, r]
        keys = jnp.concatenate([natural[cols_ref[0, s, r]] for s in range(SLOTS)], axis=0)
        both = jnp.dot(keys, left[r], preferred_element_type=F32)
        best = None
        for s in range(SLOTS):
            block = both[s * BLK : (s + 1) * BLK]
            scores = block[:, :BLK]
            if s:
                scores = jnp.where(s < count, scores, -jnp.inf)
            raw[p][s, :, :BLK] = scores
            raw[p][s, :, BLK:] = block[:, BLK:]
            peak = jnp.max(scores, axis=0, keepdims=True)
            best = peak if best is None else jnp.maximum(best, peak)
        top[p][...] = best * to_exp2

    def soft_stage(p):
        peak = top[p][...]
        total = mixed = None
        for s in range(SLOTS):
            weights = jnp.exp2(raw[p][s, :, :BLK] * to_exp2 - peak)
            t = jnp.sum(weights, axis=0, keepdims=True)
            m = jnp.sum(weights * raw[p][s, :, BLK:], axis=0, keepdims=True)
            total = t if total is None else total + t
            mixed = m if mixed is None else mixed + m
            raw[p][s, :, :BLK] = weights
        inverse = 1.0 / total
        delta = mixed * inverse
        for s in range(SLOTS):
            prob = raw[p][s, :, :BLK] * inverse
            rows = slice(s * BLK, (s + 1) * BLK)
            pair[p][rows, :BLK] = prob.astype(BF16)
            pair[p][rows, BLK:] = (prob * (raw[p][s, :, BLK:] - delta)).astype(BF16)

    def grad_stage(k, p):
        r = row_at(k)
        named = [cols_ref[0, s, r] for s in range(SLOTS)]
        both = pair[p][...]
        turned = jnp.concatenate([head_in[n, FEAT : 3 * FEAT] for n in named], axis=1)
        row_side = jnp.dot(turned, both, preferred_element_type=F32)
        row_out[r, :FEAT] = row_side[FEAT:, :BLK].astype(BF16)
        row_out[r, FEAT:] = (row_side[:FEAT, BLK:] * scale).astype(BF16)
        key_side = lax.dot_general(
            right[r], both, (((1,), (1,)), ((), ())), preferred_element_type=F32
        )
        for s in range(SLOTS):
            chain[4 * k + s] = key_side[:, s * BLK : (s + 1) * BLK] + chain[table[s, r]]

    def row_copy(i, j):
        peer = peer_at(me_s, i, j, ng, 1)
        return remote(
            row_out.at[peer], row_in.at[me_s], row_s.at[i, j], row_r.at[i, j], me_d, peer
        )

    def col_copy(i, j):
        peer = peer_at(me_s, i, j, ng, 1)
        return remote(
            col_out.at[peer], col_in.at[me_s], col_s.at[i, j], col_r.at[i, j], me_d, peer
        )

    own_row = pltpu.make_async_copy(row_out.at[me_s], row_in.at[me_s], own_sem.at[3])
    own_col = pltpu.make_async_copy(col_out.at[me_s], col_in.at[me_s], own_sem.at[4])
    score_stage(0, 0)
    score_stage(1, 1)
    soft_stage(0)

    def steps(i, c):
        @pl.when(i > 1)
        def _():
            row_copy((i - 1) // 2, 2 * ((i - 1) % 2)).start()

        @pl.when(i > 0)
        def _():
            row_copy((i - 1) // 2, 2 * ((i - 1) % 2) + 1).start()

        for u in range(2):
            k, p = 1 + 2 * i + u, (1 + u) % 2
            score_stage(k + 1, 1 - p)
            soft_stage(p)
            grad_stage(k - 1, 1 - p)
        return c

    lax.fori_loop(0, (nb - 2) // 2, steps, 0)
    own_row.start()
    row_copy(ng - 1, 0).start()
    row_copy(ng - 1, 1).start()
    soft_stage(1)
    grad_stage(nb - 2, 0)
    grad_stage(nb - 1, 1)
    row_copy(ng - 1, 2).start()
    row_copy(ng - 1, 3).start()

    def col_send(i, c):
        for j in range(4):
            peer = peer_at(me_s, i, j, ng, 1)
            total = chain[table[SLOTS, peer]]
            col_out[peer, :FEAT] = (total[:FEAT] * scale).astype(BF16)
            col_out[peer, FEAT:] = total[FEAT:].astype(BF16)
        start_group(i, own_col, col_copy)
        return c

    lax.fori_loop(0, ng, col_send, 0)

    def tile_own(m):
        return pltpu.make_async_copy(
            dq.at[m, lanes(me_d)], wg_in.at[m, :, lanes(me_d)], tile_o.at[m]
        )

    def tile_copy(m, g):
        return remote(
            dq.at[m, lanes(g)], wg_in.at[m, :, lanes(me_d)],
            tile_s.at[m, g], tile_r.at[m, me_d], g, me_s,
        )

    def tile_send(m, g):
        @pl.when(g == me_d)
        def _():
            tile_own(m).start()

        @pl.when(g != me_d)
        def _():
            tile_copy(m, g).start()

    def tile_rows(g, j):
        return pl.ds(pl.multiple_of(g * BLK + j * FEAT, FEAT), FEAT)

    def take_rows(i, c):
        g = got_group(i)
        await_group(i, own_row, row_copy)
        for j in range(4):
            dq[0, tile_rows(g, j)] = row_in[4 * g + j, FEAT:]
        tile_send(0, g)
        mix = jnp.concatenate([row_in[4 * g + j, :FEAT] for j in range(4)], axis=0)
        mix_vm[:, lanes(g)] = flip(mix)
        return c

    def take_cols(i, c):
        g = got_group(i)
        await_group(i, own_col, col_copy)
        for j in range(4):
            dq[1, tile_rows(g, j)] = col_in[4 * g + j, :FEAT]
            dq[2, tile_rows(g, j)] = col_in[4 * g + j, FEAT:]
        tile_send(1, g)
        tile_send(2, g)
        return c

    chunk = nz * FEAT

    def chunk_rows(y):
        return pl.ds(pl.multiple_of(y * chunk, chunk), chunk)

    def y_copy(m, k):
        to = lax.rem(me_y + k, ny)
        return remote(
            part.at[m, chunk_rows(to)], y_in.at[m, k - 1],
            ys_sem.at[m, k], yr_sem.at[m, k], me_d, to * nz + me_z,
        )

    def z_rows(z):
        return pl.ds(pl.multiple_of(z * FEAT, FEAT), FEAT)

    def last_copy(m, k):
        to = lax.rem(me_z + k, nz)
        d, u = owner(m)
        return remote(
            mid.at[m, z_rows(to)], last_in.at[u, k],
            last_s.at[m, k], last_r.at[u, k], d, me_y * nz + to,
        )

    def last_own(m):
        u = owner(m)[1]
        return pltpu.make_async_copy(mid.at[m, z_rows(me_z)], last_in.at[u, 0], last_o.at[u])

    def contract(m):
        tile_own(m).wait()

        def arrived(k, c):
            src = lax.rem(me_d + k, nd)
            remote(
                dq.at[m, lanes(0)], wg_in.at[m, :, lanes(src)],
                tile_s.at[m, 0], tile_r.at[m, src], src, me_s,
            ).wait_recv()
            return c

        lax.fori_loop(1, nd, arrived, 0)
        part[m] = lax.dot_general(
            xt_all[...], wg_in[m], (((1,), (1,)), ((), ())), preferred_element_type=F32
        ).astype(BF16)
        for k in range(1, ny):
            y_copy(m, k).start()

    def sum_y(m):
        total = part[m, chunk_rows(me_y)].astype(F32)
        for k in range(1, ny):
            y_copy(m, k).wait_recv()
            total += y_in[m, k - 1].astype(F32)
        mid[m] = total.astype(BF16)

        @pl.when(owner(m)[0] == me_d)
        def _():
            last_own(m).start()

        @pl.when(owner(m)[0] != me_d)
        def _():
            last_copy(m, 0).start()

        for k in range(1, nz):
            last_copy(m, k).start()

    width = 2 * BLK

    def node_part(n, m):
        rows = pl.ds(pl.multiple_of(n * width, width), width)
        return rows, jnp.dot(w_vm[m, rows], dq[m], preferred_element_type=F32)

    def nodes_early(n, c):
        rows, value = node_part(n, 0)
        gn_acc[rows] = value
        return c

    def nodes_late(n, c):
        rows, keys = node_part(n, 1)
        total = gn_acc[rows] + keys + node_part(n, 2)[1]
        gn_vm[:, rows] = jnp.transpose(total).astype(BF16)
        return c

    lax.fori_loop(0, ng, take_rows, 0)
    mix_done = pltpu.make_async_copy(mix_vm, mix_out, out_sem.at[0])
    mix_done.start()
    xt_keep.wait()
    for k in range(nd // 2):
        share_copy(k).wait_recv()
    contract(0)
    lax.fori_loop(0, hidden // width, nodes_early, 0)
    lax.fori_loop(0, ng // 4, take_cols, 0)
    sum_y(0)
    lax.fori_loop(ng // 4, ng, take_cols, 0)
    contract(1)
    contract(2)
    lax.fori_loop(0, hidden // width // 2, nodes_late, 0)
    sum_y(1)
    sum_y(2)
    lax.fori_loop(hidden // width // 2, hidden // width, nodes_late, 0)
    gn_done = pltpu.make_async_copy(gn_vm, gn_out, out_sem.at[1])
    gn_done.start()
    for u in range(3):

        @pl.when(source(u) == me_d)
        def _():
            pltpu.make_async_copy(mid.at[0, z_rows(0)], last_in.at[u, 0], last_o.at[u]).wait()

        for k in range(nz):
            arrival = remote(
                mid.at[0, z_rows(0)], last_in.at[u, k], last_s.at[0, 0], last_r.at[u, k],
                source(u), me_s,
            )
            if k:
                arrival.wait_recv()
            else:

                @pl.when(source(u) != me_d)
                def _():
                    arrival.wait_recv()

        total = last_in[u, 0].astype(F32)
        for k in range(1, nz):
            total += last_in[u, k].astype(F32)
        wg_ref[:, u * BLK : (u + 1) * BLK] = total

    def sent(i, c):
        for copy in (cot_copy, head_copy, row_copy, col_copy):

            @pl.when(i > 0)
            def _():
                copy(i, 0).wait_send()

            for j in range(1, 4):
                copy(i, j).wait_send()
        for m in range(3):

            @pl.when(i != me_d)
            def _():
                tile_copy(m, i).wait_send()

        return c

    lax.fori_loop(0, ng, sent, 0)
    for k in range(1, nd // 2):
        xt_copy(k).wait_send()
    for k in range(nd // 2):
        share_copy(k).wait_send()
    for m in range(3):
        for k in range(1, ny):
            y_copy(m, k).wait_send()

        @pl.when(owner(m)[0] != me_d)
        def _():
            last_copy(m, 0).wait_send()

        for k in range(1, nz):
            last_copy(m, k).wait_send()
    mix_done.wait()
    gn_done.wait()


def settle_kernel(mix_in, gn_in, wg_in, mix_out, gn_out, wg_out, sem):
    copies = [
        pltpu.make_async_copy(src, dst, sem.at[n])
        for n, (src, dst) in enumerate(((mix_in, mix_out), (gn_in, gn_out), (wg_in, wg_out)))
    ]
    for copy in copies:
        copy.start()
    for copy in copies:
        copy.wait()


def per_device(nd, ns, nodes, w_qkv, incoming_adjoint, block_cols, block_counts):
    rows, hidden = nodes.shape[1:]
    ny, nz = 4, ns // 4
    ng = ns // 4
    chunk = nz * FEAT
    any_spec = pl.BlockSpec(memory_space=pl.ANY)
    vm_spec = pl.BlockSpec(memory_space=pltpu.VMEM)
    sm_spec = pl.BlockSpec(memory_space=pltpu.SMEM)
    dma = pltpu.SemaphoreType.DMA
    slots_first = jnp.swapaxes(block_cols, 1, 2)
    out_shape = (
        jax.ShapeDtypeStruct((rows, hidden), BF16),
        jax.ShapeDtypeStruct((rows, hidden), BF16),
        jax.ShapeDtypeStruct((FEAT, 3 * BLK), F32),
    )
    results = pl.pallas_call(
        functools.partial(whole_kernel, nd, ns, ny, nz),
        out_shape=out_shape,
        in_specs=[any_spec, any_spec, any_spec, sm_spec, vm_spec, sm_spec],
        out_specs=(any_spec, any_spec, vm_spec),
        scratch_shapes=[
            pltpu.VMEM((rows, hidden), BF16),
            pltpu.VMEM((rows, hidden), BF16),
            pltpu.VMEM((hidden, BLK), BF16),
            pltpu.VMEM((3, hidden, hidden), BF16),
            pltpu.VMEM((ns, 3 * FEAT, BLK), BF16),
            pltpu.VMEM((ns, BLK, BLK), BF16),
            pltpu.VMEM((ns, BLK, BLK), BF16),
            pltpu.VMEM((hidden, BLK), BF16),
            pltpu.VMEM((hidden, nd * BLK), BF16),
            pltpu.VMEM((ns, BLK, 2 * BLK), BF16),
            pltpu.VMEM((ns, 2 * FEAT, 2 * BLK), BF16),
            pltpu.VMEM((SLOTS * ns + 1, 2 * FEAT, BLK), F32),
            pltpu.VMEM((ns, 2 * FEAT, BLK), BF16),
            pltpu.VMEM((ns, 2 * FEAT, BLK), BF16),
            pltpu.VMEM((ns, 2 * FEAT, BLK), BF16),
            pltpu.VMEM((ns, 2 * FEAT, BLK), BF16),
            pltpu.VMEM((SLOTS, BLK, 2 * BLK), F32),
            pltpu.VMEM((SLOTS, BLK, 2 * BLK), F32),
            pltpu.VMEM((1, BLK), F32),
            pltpu.VMEM((1, BLK), F32),
            pltpu.VMEM((SLOTS * BLK, 2 * BLK), BF16),
            pltpu.VMEM((SLOTS * BLK, 2 * BLK), BF16),
            pltpu.VMEM((8, BLK), jnp.int32),
            pltpu.SMEM((8, BLK), jnp.int32),
            pltpu.VMEM((3, hidden, BLK), BF16),
            pltpu.VMEM((3, BLK, nd * BLK), BF16),
            pltpu.VMEM((3, hidden, BLK), BF16),
            pltpu.VMEM((3, ny - 1, chunk, BLK), BF16),
            pltpu.VMEM((3, chunk, BLK), BF16),
            pltpu.VMEM((3, nz, FEAT, BLK), BF16),
            pltpu.VMEM((rows, hidden), BF16),
            pltpu.VMEM((hidden, BLK), F32),
            pltpu.VMEM((rows, hidden), BF16),
            dma((ng, 3)),
            dma((2,)),
            dma((ng, 4)),
            dma((ng, 4)),
            dma((ng, 4)),
            dma((ng, 4)),
            dma((nd // 2,)),
            dma((nd // 2,)),
            dma((nd // 2,)),
            dma((nd // 2,)),
            dma((ng, 4)),
            dma((ng, 4)),
            dma((ng, 4)),
            dma((ng, 4)),
            dma((6,)),
            dma((3, ng)),
            dma((3, nd)),
            dma((3,)),
            dma((3, ny)),
            dma((3, ny)),
            dma((3, nz)),
            dma((3, nz)),
            dma((3,)),
            dma((2,)),
        ],
        compiler_params=pltpu.CompilerParams(
            collective_id=1, has_side_effects=True, vmem_limit_bytes=VMEM_LIMIT
        ),
        name="whole",
    )(nodes, w_qkv, incoming_adjoint, slots_first, slots_first[0], block_counts)
    mixture, grad_nodes, weight_grad = pl.pallas_call(
        settle_kernel,
        out_shape=out_shape,
        in_specs=[any_spec] * 3,
        out_specs=(any_spec,) * 3,
        scratch_shapes=[dma((3,))],
        compiler_params=pltpu.CompilerParams(vmem_limit_bytes=VMEM_LIMIT),
        name="settle",
    )(*results)
    return (mixture[None], grad_nodes[None], jnp.transpose(weight_grad))


def solution(mesh):
    nd, ns = mesh.shape["dp"], mesh.shape["seq"]
    in_specs = (P("dp", "seq", None), P(), P("dp", "seq", None), P("dp", None, None), P("dp", None))
    out_specs = (P("dp", "seq", None), P("dp", "seq", None), P("dp", "seq"))
    return jax.shard_map(
        functools.partial(per_device, nd, ns),
        mesh=mesh,
        in_specs=in_specs,
        out_specs=out_specs,
        check_vma=False,
    )
```

time: 92.9 us -> 111 us (1.19); the launches traced: 92.4 us -> 109 us
  Pallas kernels: 87 us -> 108 us
  local copies, waits for them, and re-layouts: 4.76 us -> 0 us
    pallas_call x1 -> x2, Pallas kernels: 87 us -> 108 us  [the longest x1 89.8 us: per_device(): pl.pallas_call(functools.partial(whole_kernel, nd, ns, ny, nz), out_shape...]
    unnamed x3 -> x0, local copies, waits for them, and re-layouts: 4.76 us -> none
where the time goes in v4:
time: 111 us; the launch traced here: 109 us
  Pallas kernels  108 us (97%)
    pallas_call x1, Pallas kernels, per_device(): pl.pallas_call(functools.partial(whole_kernel, nd, ns, ny, nz), out_shape...  89.8 us
    pallas_call x1, Pallas kernels, per_device(): pl.pallas_call(settle_kernel, out_shape=out_shape, in_specs=[any_spec] *...  18.5 us

profile of v4, /device:TPU:2, one launch (start us, length us, event | category | flops | bytes accessed | tf_op | source)
XLA Modules:
  0.0 108.9 jit_solution(17889426246665160629)
XLA Ops:
  0.6 89.8 %whole.1 = (bf16[128,1024]{1,0:T(8,128)(2,1)}, bf16[128,1024]{1,0:T(8,128)(2,1)}, f32[32,384]{1,0:T(8,128)}) custom-call(bf16[1,128,1024]{2,1,0:T(8,128)(2,1)} %x_in.1, bf16[1024,3072]{1,0:T(8,128)(2,1)} %w_in.1, bf16[1,128,1024]{2,1,0:T(8,128)(2,1)} %cot_in.1, s32[1,4,32]{2,1,0:T(4,128)} %bitcast.6, s32[4,32]{1,0:T(4,128)} %bitcast.7, s32[1,32]{1,0:T(1,128)} %counts_ref.1), custom_call_target="tpu_custom_call" | custom-call | tf_op jit(solution)/shard_map/whole/pallas_call | solution.py:613
  90.4 18.5 %settle.1 = (bf16[128,1024]{1,0:T(8,128)(2,1)}, bf16[128,1024]{1,0:T(8,128)(2,1)}, f32[32,384]{1,0:T(8,128)}) custom-call(bf16[128,1024]{1,0:T(8,128)(2,1)} %get-tuple-element.9.mix_in, bf16[128,1024]{1,0:T(8,128)(2,1)} %get-tuple-element.10.gn_in, f32[32,384]{1,0:T(8,128)} %get-tuple-element.11.wg_in), custom_call_target="tpu_custom_call" | custom-call | tf_op jit(solution)/shard_map/settle/pallas_call | solution.py:682

commit v5 on v3

--- a/solution.py
+++ b/solution.py
@@ -65,14 +65,14 @@
 
 def whole_kernel(
     nd, ns, ny, nz, tpd,
-    x_in, w_in, cot_in, cols_ref, cols_vec, counts_ref,
-    mix_ref, gn_ref, wg_ref,
-    x_vm, cot_vm, w_vm, head_out, head_in, xt_own, xt_all,
+    x_in, w_in, cot_in, cols_in, counts_in,
+    mix_out, gn_out, wg_out,
+    cols_ref, cols_vec, counts_ref, mix_ref, gn_ref, wg_ref, x_vm, cot_vm, w_vm, head_out, head_in, xt_own, xt_all,
     turned_kv, left, right, chain, row_out, col_out, row_in, col_in,
     raw_even, raw_odd, top_even, top_odd, pair_even, pair_odd,
     table_vm, table, dq, wg_in, part, relay, fold, mid, last_in,
     w_sem, load_sem, head_s, head_r, xt_s, xt_r, row_s, row_r, col_s, col_r,
-    own_sem, tile_s, tile_r, tile_o, relay_s, relay_r, fold_s, fold_r, last_s, last_r,
+    own_sem, tile_s, tile_r, tile_o, relay_s, relay_r, fold_s, fold_r, last_s, last_r, late_s, late_r, share_s, share_r, out_sem,
 ):
     me_d, me_s = lax.axis_index("dp"), lax.axis_index("seq")
     me_y, me_z = me_s // nz, me_s % nz
@@ -101,6 +101,7 @@
             device_id=(d, s), device_id_type=MESH,
         )
 
+    barrier = greet(me_d, me_s, nd, ns)
     load_x = pltpu.make_async_copy(x_in.at[0], x_vm, load_sem.at[0])
     load_cot = pltpu.make_async_copy(cot_in.at[0], cot_vm, load_sem.at[1])
     load_x.start()
@@ -118,10 +119,17 @@
             w_copy(i, m).start()
         return c
 
+    small_loads = [
+        pltpu.make_async_copy(src, dst, load_sem.at[2 + n])
+        for n, (src, dst) in enumerate(
+            ((cols_in, cols_ref), (cols_in.at[0], cols_vec), (counts_in, counts_ref))
+        )
+    ]
     w_start(0, 0)
     load_cot.start()
     lax.fori_loop(1, ng, w_start, 0)
-    barrier = greet(me_d, me_s, nd, ns)
+    for load in small_loads:
+        load.start()
     load_x.wait()
     load_cot.wait()
 
@@ -163,18 +171,27 @@
     xt_keep = pltpu.make_async_copy(xt_own, xt_all.at[:, lanes(me_d)], own_sem.at[1])
     xt_keep.start()
 
+    sibling = me_d + 1 - 2 * (me_d % 2)
+
     def xt_copy(k):
         return remote(
             xt_own, xt_all.at[:, lanes(me_d)], xt_s.at[k], xt_r.at[k],
-            lax.rem(me_d + k, nd), me_s,
-        )
-
-    def xt_start(k, c):
+            lax.rem(me_d + 2 * k, nd), me_s,
+        )
+
+    def share_copy(k):
+        here = lanes(lax.rem(me_d - 2 * k + nd, nd))
+        return remote(
+            xt_all.at[:, here] if k else xt_own, xt_all.at[:, here],
+            share_s.at[k], share_r.at[k], sibling, me_s,
+        )
+
+    for k in range(1, nd // 2):
         xt_copy(k).start()
-        return c
-
-    lax.fori_loop(1, nd, xt_start, 0)
-
+    share_copy(0).start()
+
+    for load in small_loads:
+        load.wait()
     named_now = cols_vec[...]
     row_ids = lane_ids((SLOTS, nb))
     place = 4 * lax.rem(row_ids // 4 - my_group + ng, ng) + lax.rem(
@@ -235,7 +252,11 @@
             prepare(4 * got_group(i) + lax.rem(me_s % 4 - j + 4, 4))
         return c
 
-    lax.fori_loop(0, ng, arrive, 0)
+    lax.fori_loop(0, ng - 1, arrive, 0)
+    for k in range(1, nd // 2):
+        xt_copy(k).wait_recv()
+        share_copy(k).start()
+    lax.fori_loop(ng - 1, ng, arrive, 0)
     table_copy.wait()
 
     def score_stage(k, p):
@@ -289,11 +310,22 @@
         for s in range(SLOTS):
             chain[4 * k + s] = key_side[:, s * BLK : (s + 1) * BLK] + chain[table[s, r]]
 
-    def row_copy(i, j):
-        peer = peer_at(me_s, i, j, ng, 1)
-        return remote(
-            row_out.at[peer], row_in.at[me_s], row_s.at[i, j], row_r.at[i, j], me_d, peer
-        )
+    early = ng // 2
+
+    def piece_copy(lo, hi, send_sem, recv_sem):
+        def copy(i, j):
+            peer = peer_at(me_s, i, j, ng, 1)
+            part_of = pl.ds(lo, hi - lo)
+            return remote(
+                row_out.at[peer, part_of], row_in.at[me_s, part_of],
+                send_sem.at[i, j], recv_sem.at[i, j], me_d, peer,
+            )
+
+        return copy
+
+    row_copy = piece_copy(0, 2 * FEAT, row_s, row_r)
+    query_copy = piece_copy(FEAT, 2 * FEAT, row_s, row_r)
+    late_copy = piece_copy(0, FEAT, late_s, late_r)
 
     def col_copy(i, j):
         peer = peer_at(me_s, i, j, ng, 1)
@@ -307,14 +339,14 @@
     score_stage(1, 1)
     soft_stage(0)
 
-    def steps(i, c):
+    def steps(copy, i, c):
         @pl.when(i > 1)
         def _():
-            row_copy((i - 1) // 2, 2 * ((i - 1) % 2)).start()
+            copy((i - 1) // 2, 2 * ((i - 1) % 2)).start()
 
         @pl.when(i > 0)
         def _():
-            row_copy((i - 1) // 2, 2 * ((i - 1) % 2) + 1).start()
+            copy((i - 1) // 2, 2 * ((i - 1) % 2) + 1).start()
 
         for u in range(2):
             k, p = 1 + 2 * i + u, (1 + u) % 2
@@ -323,15 +355,17 @@
             grad_stage(k - 1, 1 - p)
         return c
 
-    lax.fori_loop(0, (nb - 2) // 2, steps, 0)
+    turn = 2 * early + 1
+    lax.fori_loop(0, turn, functools.partial(steps, row_copy), 0)
+    lax.fori_loop(turn, (nb - 2) // 2, functools.partial(steps, query_copy), 0)
     own_row.start()
-    row_copy(ng - 1, 0).start()
-    row_copy(ng - 1, 1).start()
+    query_copy(ng - 1, 0).start()
+    query_copy(ng - 1, 1).start()
     soft_stage(1)
     grad_stage(nb - 2, 0)
     grad_stage(nb - 1, 1)
-    row_copy(ng - 1, 2).start()
-    row_copy(ng - 1, 3).start()
+    query_copy(ng - 1, 2).start()
+    query_copy(ng - 1, 3).start()
 
     def col_send(i, c):
         for j in range(4):
@@ -355,6 +389,13 @@
 
     lax.fori_loop(0, ng, col_send, 0)
 
+    def late_send(i, c):
+        for j in range(4):
+            late_copy(i, j).start()
+        return c
+
+    lax.fori_loop(early, ng, late_send, 0)
+
     def tile_own(g, m):
         t = m * ng + g
         return pltpu.make_async_copy(
@@ -392,14 +433,31 @@
         for j in range(1, 4):
             copy(i, j).wait_recv()
 
-    def take_rows(i, c):
-        g = got_group(i)
-        await_group(i, own_row, row_copy)
-        mix = jnp.concatenate([row_in[4 * g + j, :FEAT] for j in range(4)], axis=0)
-        mix_ref[:, lanes(g)] = jnp.transpose(mix.astype(F32)).astype(BF16)
+    def take_queries(g):
         for j in range(4):
             dq[g, j * FEAT : (j + 1) * FEAT] = row_in[4 * g + j, FEAT:]
         tile_send(g, 0)
+
+    def take_mix(g):
+        mix = jnp.concatenate([row_in[4 * g + j, :FEAT] for j in range(4)], axis=0)
+        mix_ref[:, lanes(g)] = jnp.transpose(mix.astype(F32)).astype(BF16)
+
+    def take_early(i, c):
+        await_group(i, own_row, row_copy)
+        take_queries(got_group(i))
+        take_mix(got_group(i))
+        return c
+
+    def take_later(i, c):
+        for j in range(4):
+            query_copy(i, j).wait_recv()
+        take_queries(got_group(i))
+        return c
+
+    def take_late(i, c):
+        for j in range(4):
+            late_copy(i, j).wait_recv()
+        take_mix(got_group(i))
         return c
 
     def take_cols(i, c):
@@ -412,15 +470,12 @@
         tile_send(g, 2)
         return c
 
-    lax.fori_loop(0, ng, take_rows, 0)
+    lax.fori_loop(0, early, take_early, 0)
+    lax.fori_loop(early, ng, take_later, 0)
     lax.fori_loop(0, ng, take_cols, 0)
     xt_keep.wait()
-
-    def xt_wait(k, c):
-        xt_copy(k).wait()
-        return c
-
-    lax.fori_loop(1, nd, xt_wait, 0)
+    for k in range(nd // 2):
+        share_copy(k).wait_recv()
 
     chunk = nz * FEAT
     half = chunk // 2
@@ -493,7 +548,12 @@
                 part[t, rows].astype(F32) + relay[t, way].astype(F32)
             ).astype(BF16)
             fold_copy(t, way, way).start()
+    lax.fori_loop(early, ng, take_late, 0)
+    mix_done = pltpu.make_async_copy(mix_ref, mix_out, out_sem.at[0])
+    mix_done.start()
     lax.fori_loop(steps_gn // 2, steps_gn, node_cols, 0)
+    gn_done = pltpu.make_async_copy(gn_ref, gn_out, out_sem.at[1])
+    gn_done.start()
     for t in range(tpd):
         for which in range(2):
             total = part[t, rows_of(me_y, which)].astype(F32)
@@ -501,7 +561,7 @@
                 fold_copy(t, way, which).wait_recv()
                 total += fold[t, way, which].astype(F32)
             mid[t, which * half : (which + 1) * half] = total.astype(BF16)
-        for k in range(1, nz):
+        for k in sorted(range(1, nz), key=lambda k: -min(k, nz - k)):
             last_copy(t, k).start()
     for t in range(tpd):
         total = mid[t, pl.ds(pl.multiple_of(me_z * FEAT, FEAT), FEAT)].astype(F32)
@@ -509,9 +569,11 @@
             last_copy(t, k).wait_recv()
             total += last_in[t, k - 1].astype(F32)
         wg_ref[:, t * BLK : (t + 1) * BLK] = total
+    wg_done = pltpu.make_async_copy(wg_ref, wg_out, out_sem.at[2])
+    wg_done.start()
 
     def sent(i, c):
-        for copy in (head_copy, row_copy, col_copy):
+        for copy in (head_copy, col_copy):
 
             @pl.when(i > 0)
             def _():
@@ -519,6 +581,22 @@
 
             for j in range(1, 4):
                 copy(i, j).wait_send()
+
+        @pl.when((i > 0) & (i < early))
+        def _():
+            row_copy(i, 0).wait_send()
+
+        @pl.when(i < early)
+        def _():
+            for j in range(1, 4):
+                row_copy(i, j).wait_send()
+
+        @pl.when(i >= early)
+        def _():
+            for j in range(4):
+                query_copy(i, j).wait_send()
+                late_copy(i, j).wait_send()
+
         for m in range(3):
 
             @pl.when((m * ng + i) // tpd != me_d)
@@ -528,6 +606,10 @@
         return c
 
     lax.fori_loop(0, ng, sent, 0)
+    for k in range(1, nd // 2):
+        xt_copy(k).wait_send()
+    for k in range(nd // 2):
+        share_copy(k).wait_send()
     for t in range(tpd):
         for way in range(2):
             relay_copy(t, way).wait_send()
@@ -535,6 +617,22 @@
                 fold_copy(t, way, which).wait_send()
         for k in range(1, nz):
             last_copy(t, k).wait_send()
+    mix_done.wait()
+    gn_done.wait()
+    wg_done.wait()
+
+
+def settle_kernel(mix_in, gn_in, wg_in, mix_out, gn_out, wg_out, mix_vm, gn_vm, wg_vm, sem):
+    triples = ((mix_in, mix_vm, mix_out), (gn_in, gn_vm, gn_out), (wg_in, wg_vm, wg_out))
+    loads = [pltpu.make_async_copy(a, b, sem.at[0, n]) for n, (a, b, _) in enumerate(triples)]
+    stores = [pltpu.make_async_copy(b, c, sem.at[1, n]) for n, (_, b, c) in enumerate(triples)]
+    for load in loads:
+        load.start()
+    for load, store in zip(loads, stores):
+        load.wait()
+        store.start()
+    for store in stores:
+        store.wait()
 
 
 def per_device(nd, ns, nodes, w_qkv, incoming_adjoint, block_cols, block_counts):
@@ -543,21 +641,25 @@
     ng = ns // 4
     tpd = 3 * ng // nd
     chunk = nz * FEAT
-    hbm = pl.BlockSpec(memory_space=pltpu.HBM)
-    vm_spec = pl.BlockSpec(memory_space=pltpu.VMEM)
-    sm_spec = pl.BlockSpec(memory_space=pltpu.SMEM)
+    any_spec = pl.BlockSpec(memory_space=pl.ANY)
     dma = pltpu.SemaphoreType.DMA
     slots_first = jnp.swapaxes(block_cols, 1, 2)
-    mixture, grad_nodes, weight_grad = pl.pallas_call(
+    out_shape = (
+        jax.ShapeDtypeStruct((rows, hidden), BF16),
+        jax.ShapeDtypeStruct((rows, hidden), BF16),
+        jax.ShapeDtypeStruct((FEAT, tpd * BLK), F32),
+    )
+    out_buffers = [pltpu.VMEM(out.shape, out.dtype) for out in out_shape]
+    results = pl.pallas_call(
         functools.partial(whole_kernel, nd, ns, ny, nz, tpd),
-        out_shape=(
-            jax.ShapeDtypeStruct((rows, hidden), BF16),
-            jax.ShapeDtypeStruct((rows, hidden), BF16),
-            jax.ShapeDtypeStruct((FEAT, tpd * BLK), F32),
-        ),
-        in_specs=[hbm, hbm, hbm, sm_spec, vm_spec, sm_spec],
-        out_specs=(vm_spec, vm_spec, vm_spec),
+        out_shape=out_shape,
+        in_specs=[any_spec] * 5,
+        out_specs=(any_spec,) * 3,
         scratch_shapes=[
+            pltpu.SMEM((1, SLOTS, ns), jnp.int32),
+            pltpu.VMEM((SLOTS, ns), jnp.int32),
+            pltpu.SMEM((1, ns), jnp.int32),
+            *out_buffers,
             pltpu.VMEM((rows, hidden), BF16),
             pltpu.VMEM((rows, hidden), BF16),
             pltpu.VMEM((ng, hidden, 3 * BLK), BF16),
@@ -589,7 +691,7 @@
             pltpu.VMEM((tpd, chunk, BLK), BF16),
             pltpu.VMEM((tpd, nz - 1, FEAT, BLK), BF16),
             dma((ng, 3)),
-            dma((2,)),
+            dma((5,)),
             dma((ng, 4)),
             dma((ng, 4)),
             dma((nd,)),
@@ -608,12 +710,26 @@
             dma((tpd, 2, 2)),
             dma((tpd, nz)),
             dma((tpd, nz)),
+            dma((ng, 4)),
+            dma((ng, 4)),
+            dma((nd // 2,)),
+            dma((nd // 2,)),
+            dma((3,)),
         ],
         compiler_params=pltpu.CompilerParams(
             collective_id=1, has_side_effects=True, vmem_limit_bytes=VMEM_LIMIT
         ),
         name="whole",
-    )(nodes, w_qkv, incoming_adjoint, slots_first, slots_first[0], block_counts)
+    )(nodes, w_qkv, incoming_adjoint, slots_first, block_counts)
+    mixture, grad_nodes, weight_grad = pl.pallas_call(
+        settle_kernel,
+        out_shape=out_shape,
+        in_specs=[any_spec] * 3,
+        out_specs=(any_spec,) * 3,
+        scratch_shapes=[*out_buffers, dma((2, 3))],
+        compiler_params=pltpu.CompilerParams(vmem_limit_bytes=VMEM_LIMIT),
+        name="settle",
+    )(*results)
     return (mixture[None], grad_nodes[None], jnp.transpose(weight_grad))
 
 

time: 92.9 us -> 86.9 us (0.935)
  local copies, waits for them, and re-layouts: 4.76 us -> 0 us
  Pallas kernels: 87 us -> 85.9 us
    unnamed x3 -> x0, local copies, waits for them, and re-layouts: 4.76 us -> none
    pallas_call x1, Pallas kernels: 87 us -> 84.1 us  [per_device(): pl.pallas_call(functools.partial(whole_kernel, nd, ns, ny, nz, tpd), out_...]
    pallas_call x0 -> x1, Pallas kernels: none -> 1.79 us  [per_device(): pl.pallas_call(settle_kernel, out_shape=out_shape, in_specs=[any_spec] *...]
where the time goes in v5:
time: 86.9 us; the launch traced here: 86.5 us
  Pallas kernels  85.9 us (99%)
    pallas_call x1, Pallas kernels, per_device(): pl.pallas_call(functools.partial(whole_kernel, nd, ns, ny, nz, tpd), out_...  84.1 us
    pallas_call x1, Pallas kernels, per_device(): pl.pallas_call(settle_kernel, out_shape=out_shape, in_specs=[any_spec] *...  1.79 us

profile of v5, /device:TPU:2, one launch (start us, length us, event | category | flops | bytes accessed | tf_op | source)
XLA Modules:
  0.0 86.5 jit_solution(16501324090387300845)
XLA Ops:
  0.6 84.1 %whole.1 = (bf16[128,1024]{1,0:T(8,128)(2,1)}, bf16[128,1024]{1,0:T(8,128)(2,1)}, f32[32,384]{1,0:T(8,128)}) custom-call(bf16[1,128,1024]{2,1,0:T(8,128)(2,1)} %x_in.1, bf16[1024,3072]{1,0:T(8,128)(2,1)} %w_in.1, bf16[1,128,1024]{2,1,0:T(8,128)(2,1)} %cot_in.1, s32[1,4,32]{2,1,0:T(4,128)} %bitcast.4, s32[1,32]{1,0:T(1,128)} %counts_in.1), custom_call_target="tpu_custom_call" | custom-call | tf_op jit(solution)/shard_map/whole/pallas_call | solution.py:653
  84.7 1.8 %settle.1 = (bf16[128,1024]{1,0:T(8,128)(2,1)}, bf16[128,1024]{1,0:T(8,128)(2,1)}, f32[32,384]{1,0:T(8,128)}) custom-call(bf16[128,1024]{1,0:T(8,128)(2,1)} %get-tuple-element.9.mix_in, bf16[128,1024]{1,0:T(8,128)(2,1)} %get-tuple-element.10.gn_in, f32[32,384]{1,0:T(8,128)} %get-tuple-element.11.wg_in), custom_call_target="tpu_custom_call" | custom-call | tf_op jit(solution)/shard_map/settle/pallas_call | solution.py:724

commit v6 on v5

--- a/solution.py
+++ b/solution.py
@@ -310,22 +310,19 @@
         for s in range(SLOTS):
             chain[4 * k + s] = key_side[:, s * BLK : (s + 1) * BLK] + chain[table[s, r]]
 
-    early = ng // 2
-
-    def piece_copy(lo, hi, send_sem, recv_sem):
+    def piece_copy(lo, send_sem, recv_sem):
         def copy(i, j):
             peer = peer_at(me_s, i, j, ng, 1)
-            part_of = pl.ds(lo, hi - lo)
+            piece = pl.ds(lo, FEAT)
             return remote(
-                row_out.at[peer, part_of], row_in.at[me_s, part_of],
+                row_out.at[peer, piece], row_in.at[me_s, piece],
                 send_sem.at[i, j], recv_sem.at[i, j], me_d, peer,
             )
 
         return copy
 
-    row_copy = piece_copy(0, 2 * FEAT, row_s, row_r)
-    query_copy = piece_copy(FEAT, 2 * FEAT, row_s, row_r)
-    late_copy = piece_copy(0, FEAT, late_s, late_r)
+    late_copy = piece_copy(0, late_s, late_r)
+    row_copy = piece_copy(FEAT, row_s, row_r)
 
     def col_copy(i, j):
         peer = peer_at(me_s, i, j, ng, 1)
@@ -339,15 +336,7 @@
     score_stage(1, 1)
     soft_stage(0)
 
-    def steps(copy, i, c):
-        @pl.when(i > 1)
-        def _():
-            copy((i - 1) // 2, 2 * ((i - 1) % 2)).start()
-
-        @pl.when(i > 0)
-        def _():
-            copy((i - 1) // 2, 2 * ((i - 1) % 2) + 1).start()
-
+    def steps(i, c):
         for u in range(2):
             k, p = 1 + 2 * i + u, (1 + u) % 2
             score_stage(k + 1, 1 - p)
@@ -355,17 +344,23 @@
             grad_stage(k - 1, 1 - p)
         return c
 
-    turn = 2 * early + 1
-    lax.fori_loop(0, turn, functools.partial(steps, row_copy), 0)
-    lax.fori_loop(turn, (nb - 2) // 2, functools.partial(steps, query_copy), 0)
+    def send_steps(i, c):
+        row_copy((i - 1) // 2, 2 * ((i - 1) % 2)).start()
+        row_copy((i - 1) // 2, 2 * ((i - 1) % 2) + 1).start()
+        return steps(i, c)
+
+    steps(0, 0)
+    row_copy(0, 1).start()
+    steps(1, 0)
+    lax.fori_loop(2, (nb - 2) // 2, send_steps, 0)
     own_row.start()
-    query_copy(ng - 1, 0).start()
-    query_copy(ng - 1, 1).start()
+    row_copy(ng - 1, 0).start()
+    row_copy(ng - 1, 1).start()
     soft_stage(1)
     grad_stage(nb - 2, 0)
     grad_stage(nb - 1, 1)
-    query_copy(ng - 1, 2).start()
-    query_copy(ng - 1, 3).start()
+    row_copy(ng - 1, 2).start()
+    row_copy(ng - 1, 3).start()
 
     def col_send(i, c):
         for j in range(4):
@@ -389,24 +384,43 @@
 
     lax.fori_loop(0, ng, col_send, 0)
 
+    def depart(i, *copies):
+        @pl.when(i > 0)
+        def _():
+            for copy in copies:
+                copy(i, 0).wait_send()
+
+        for copy in copies:
+            for j in range(1, 4):
+                copy(i, j).wait_send()
+
     def late_send(i, c):
-        for j in range(4):
+        @pl.when(i > 0)
+        def _():
+            late_copy(i, 0).start()
+
+        for j in range(1, 4):
             late_copy(i, j).start()
-        return c
-
-    lax.fori_loop(early, ng, late_send, 0)
+        depart(i, head_copy)
+        return c
+
+    lax.fori_loop(0, ng, late_send, 0)
+    for k in range(1, nd // 2):
+        xt_copy(k).wait_send()
+    for k in range(nd // 2):
+        share_copy(k).wait_send()
 
     def tile_own(g, m):
         t = m * ng + g
         return pltpu.make_async_copy(
-            dq.at[g, pl.ds(m * BLK, BLK)], wg_in.at[t % tpd, :, lanes(me_d)],
+            dq.at[g, pl.ds(m * BLK, BLK)], wg_in.at[lanes(t % tpd), lanes(me_d)],
             tile_o.at[t % tpd],
         )
 
     def tile_copy(g, m):
         t = m * ng + g
         return remote(
-            dq.at[g, pl.ds(m * BLK, BLK)], wg_in.at[t % tpd, :, lanes(me_d)],
+            dq.at[g, pl.ds(m * BLK, BLK)], wg_in.at[lanes(t % tpd), lanes(me_d)],
             tile_s.at[g, m], tile_r.at[me_d, t % tpd], t // tpd, me_s,
         )
 
@@ -433,31 +447,26 @@
         for j in range(1, 4):
             copy(i, j).wait_recv()
 
-    def take_queries(g):
+    def take_rows(i, c):
+        g = got_group(i)
+        await_group(i, own_row, row_copy)
         for j in range(4):
             dq[g, j * FEAT : (j + 1) * FEAT] = row_in[4 * g + j, FEAT:]
         tile_send(g, 0)
-
-    def take_mix(g):
+        depart(i, row_copy)
+        return c
+
+    def take_late(i, c):
+        g = got_group(i)
+
+        @pl.when(i > 0)
+        def _():
+            late_copy(i, 0).wait_recv()
+
+        for j in range(1, 4):
+            late_copy(i, j).wait_recv()
         mix = jnp.concatenate([row_in[4 * g + j, :FEAT] for j in range(4)], axis=0)
         mix_ref[:, lanes(g)] = jnp.transpose(mix.astype(F32)).astype(BF16)
-
-    def take_early(i, c):
-        await_group(i, own_row, row_copy)
-        take_queries(got_group(i))
-        take_mix(got_group(i))
-        return c
-
-    def take_later(i, c):
-        for j in range(4):
-            query_copy(i, j).wait_recv()
-        take_queries(got_group(i))
-        return c
-
-    def take_late(i, c):
-        for j in range(4):
-            late_copy(i, j).wait_recv()
-        take_mix(got_group(i))
         return c
 
     def take_cols(i, c):
@@ -470,8 +479,7 @@
         tile_send(g, 2)
         return c
 
-    lax.fori_loop(0, early, take_early, 0)
-    lax.fori_loop(early, ng, take_later, 0)
+    lax.fori_loop(0, ng, take_rows, 0)
     lax.fori_loop(0, ng, take_cols, 0)
     xt_keep.wait()
     for k in range(nd // 2):
@@ -508,26 +516,30 @@
     def tile_done(t, k):
         src = lax.rem(me_d + k, nd)
         return remote(
-            dq.at[0, pl.ds(0, BLK)], wg_in.at[t, :, lanes(src)],
+            dq.at[0, pl.ds(0, BLK)], wg_in.at[pl.ds(t * BLK, BLK), lanes(src)],
             tile_s.at[0, 0], tile_r.at[src, t], src, me_s,
         )
 
-    for t in range(tpd):
-        pltpu.make_async_copy(
-            dq.at[0, pl.ds(0, BLK)], wg_in.at[t, :, lanes(me_d)], tile_o.at[t]
-        ).wait()
-
-        def arrived(k, c):
-            tile_done(t, k).wait_recv()
-            return c
-
-        lax.fori_loop(1, nd, arrived, 0)
-        part[t] = lax.dot_general(
-            xt_all[...], wg_in[t], (((1,), (1,)), ((), ())), preferred_element_type=F32
+    for first, last in ((0, tpd - 1), (tpd - 1, tpd)):
+        for t in range(first, last):
+            pltpu.make_async_copy(
+                dq.at[0, pl.ds(0, BLK)], wg_in.at[pl.ds(t * BLK, BLK), lanes(me_d)], tile_o.at[t]
+            ).wait()
+
+            def arrived(k, c):
+                tile_done(t, k).wait_recv()
+                return c
+
+            lax.fori_loop(1, nd, arrived, 0)
+        partial_sum = lax.dot_general(
+            xt_all[...], wg_in[first * BLK : last * BLK], (((1,), (1,)), ((), ())),
+            preferred_element_type=F32,
         ).astype(BF16)
-        for way in range(2):
-            relay_copy(t, way).start()
-            fold_copy(t, way, 1 - way).start()
+        for t in range(first, last):
+            part[t] = partial_sum[:, (t - first) * BLK : (t - first + 1) * BLK]
+            for way in range(2):
+                relay_copy(t, way).start()
+                fold_copy(t, way, 1 - way).start()
 
     def node_cols(n, c):
         width = 2 * BLK
@@ -536,6 +548,16 @@
         for g in range(ng):
             total += jnp.dot(w_vm[g, cols], dq[g], preferred_element_type=F32)
         gn_ref[:, cols] = jnp.transpose(total).astype(BF16)
+        return c
+
+    def sent(i, c):
+        depart(i, col_copy, late_copy)
+        for m in range(3):
+
+            @pl.when((m * ng + i) // tpd != me_d)
+            def _():
+                tile_copy(i, m).wait_send()
+
         return c
 
     steps_gn = hidden // (2 * BLK)
@@ -548,12 +570,13 @@
                 part[t, rows].astype(F32) + relay[t, way].astype(F32)
             ).astype(BF16)
             fold_copy(t, way, way).start()
-    lax.fori_loop(early, ng, take_late, 0)
+    lax.fori_loop(0, ng, take_late, 0)
     mix_done = pltpu.make_async_copy(mix_ref, mix_out, out_sem.at[0])
     mix_done.start()
     lax.fori_loop(steps_gn // 2, steps_gn, node_cols, 0)
     gn_done = pltpu.make_async_copy(gn_ref, gn_out, out_sem.at[1])
     gn_done.start()
+    lax.fori_loop(0, ng, sent, 0)
     for t in range(tpd):
         for which in range(2):
             total = part[t, rows_of(me_y, which)].astype(F32)
@@ -572,44 +595,6 @@
     wg_done = pltpu.make_async_copy(wg_ref, wg_out, out_sem.at[2])
     wg_done.start()
 
-    def sent(i, c):
-        for copy in (head_copy, col_copy):
-
-            @pl.when(i > 0)
-            def _():
-                copy(i, 0).wait_send()
-
-            for j in range(1, 4):
-                copy(i, j).wait_send()
-
-        @pl.when((i > 0) & (i < early))
-        def _():
-            row_copy(i, 0).wait_send()
-
-        @pl.when(i < early)
-        def _():
-            for j in range(1, 4):
-                row_copy(i, j).wait_send()
-
-        @pl.when(i >= early)
-        def _():
-            for j in range(4):
-                query_copy(i, j).wait_send()
-                late_copy(i, j).wait_send()
-
-        for m in range(3):
-
-            @pl.when((m * ng + i) // tpd != me_d)
-            def _():
-                tile_copy(i, m).wait_send()
-
-        return c
-
-    lax.fori_loop(0, ng, sent, 0)
-    for k in range(1, nd // 2):
-        xt_copy(k).wait_send()
-    for k in range(nd // 2):
-        share_copy(k).wait_send()
     for t in range(tpd):
         for way in range(2):
             relay_copy(t, way).wait_send()
@@ -684,7 +669,7 @@
             pltpu.VMEM((8, BLK), jnp.int32),
             pltpu.SMEM((8, BLK), jnp.int32),
             pltpu.VMEM((ng, 3 * BLK, BLK), BF16),
-            pltpu.VMEM((tpd, BLK, nd * BLK), BF16),
+            pltpu.VMEM((tpd * BLK, nd * BLK), BF16),
             pltpu.VMEM((tpd, hidden, BLK), BF16),
             pltpu.VMEM((tpd, 2, chunk // 2, BLK), BF16),
             pltpu.VMEM((tpd, 2, 2, chunk // 2, BLK), BF16),

time: 86.9 us -> 87.4 us (level)
  no operation moved by 1% of the time
where the time goes in v6:
time: 87.4 us; the launch traced here: 86.6 us
  Pallas kernels  86 us (98%)
    pallas_call x1, Pallas kernels, per_device(): pl.pallas_call(functools.partial(whole_kernel, nd, ns, ny, nz, tpd), out_...  84.2 us
    pallas_call x1, Pallas kernels, per_device(): pl.pallas_call(settle_kernel, out_shape=out_shape, in_specs=[any_spec] *...  1.79 us

profile of v6, /device:TPU:2, one launch (start us, length us, event | category | flops | bytes accessed | tf_op | source)
XLA Modules:
  0.0 86.6 jit_solution(8049818978806622465)
XLA Ops:
  0.6 84.2 %whole.1 = (bf16[128,1024]{1,0:T(8,128)(2,1)}, bf16[128,1024]{1,0:T(8,128)(2,1)}, f32[32,384]{1,0:T(8,128)}) custom-call(bf16[1,128,1024]{2,1,0:T(8,128)(2,1)} %x_in.1, bf16[1024,3072]{1,0:T(8,128)(2,1)} %w_in.1, bf16[1,128,1024]{2,1,0:T(8,128)(2,1)} %cot_in.1, s32[1,4,32]{2,1,0:T(4,128)} %bitcast.4, s32[1,32]{1,0:T(1,128)} %counts_in.1), custom_call_target="tpu_custom_call" | custom-call | tf_op jit(solution)/shard_map/whole/pallas_call | solution.py:638
  84.8 1.8 %settle.1 = (bf16[128,1024]{1,0:T(8,128)(2,1)}, bf16[128,1024]{1,0:T(8,128)(2,1)}, f32[32,384]{1,0:T(8,128)}) custom-call(bf16[128,1024]{1,0:T(8,128)(2,1)} %get-tuple-element.9.mix_in, bf16[128,1024]{1,0:T(8,128)(2,1)} %get-tuple-element.10.gn_in, f32[32,384]{1,0:T(8,128)} %get-tuple-element.11.wg_in), custom_call_target="tpu_custom_call" | custom-call | tf_op jit(solution)/shard_map/settle/pallas_call | solution.py:709

commit v7 on v6

--- a/solution.py
+++ b/solution.py
@@ -72,7 +72,7 @@
     raw_even, raw_odd, top_even, top_odd, pair_even, pair_odd,
     table_vm, table, dq, wg_in, part, relay, fold, mid, last_in,
     w_sem, load_sem, head_s, head_r, xt_s, xt_r, row_s, row_r, col_s, col_r,
-    own_sem, tile_s, tile_r, tile_o, relay_s, relay_r, fold_s, fold_r, last_s, last_r, late_s, late_r, share_s, share_r, out_sem,
+    own_sem, tile_s, tile_r, relay_s, relay_r, fold_s, fold_r, last_s, last_r, late_s, late_r, share_s, share_r, out_sem,
 ):
     me_d, me_s = lax.axis_index("dp"), lax.axis_index("seq")
     me_y, me_z = me_s // nz, me_s % nz
@@ -101,6 +101,9 @@
             device_id=(d, s), device_id_type=MESH,
         )
 
+    def landed(ref, sem):
+        pltpu.make_async_copy(ref, ref, sem).wait()
+
     barrier = greet(me_d, me_s, nd, ns)
     load_x = pltpu.make_async_copy(x_in.at[0], x_vm, load_sem.at[0])
     load_cot = pltpu.make_async_copy(cot_in.at[0], cot_vm, load_sem.at[1])
@@ -111,7 +114,7 @@
         return pltpu.make_async_copy(
             w_in.at[:, lanes(m * ng + g)],
             w_vm.at[g, :, pl.ds(m * BLK, BLK)],
-            w_sem.at[i, m],
+            w_sem.at[i],
         )
 
     def w_start(i, c):
@@ -136,15 +139,14 @@
     def head_copy(i, j):
         peer = peer_at(me_s, i, j, ng, 1)
         return remote(
-            head_out.at[peer], head_in.at[me_s], head_s.at[i, j], head_r.at[i, j], me_d, peer
-        )
-
-    own_head = pltpu.make_async_copy(head_out.at[me_s], head_in.at[me_s], own_sem.at[0])
+            head_out.at[peer], head_in.at[me_s], head_s, head_r.at[i], me_d, peer
+        )
+
+    own_head = pltpu.make_async_copy(head_out.at[me_s], head_in.at[me_s], head_r.at[0])
 
     def project(i, c):
         g = sent_group(i)
-        for m in range(3):
-            w_copy(i, m).wait()
+        landed(w_vm.at[g], w_sem.at[i])
         qkv = jnp.dot(x_vm[...], w_vm[g], preferred_element_type=F32).astype(BF16)
         packed = swap_quarters(
             (qkv[:, :BLK], qkv[:, BLK : 2 * BLK], qkv[:, 2 * BLK :], cot_vm[:, lanes(g)])
@@ -168,14 +170,14 @@
     lax.fori_loop(0, ng, project, 0)
 
     xt_own[...] = jnp.transpose(x_vm[...].astype(F32)).astype(BF16)
-    xt_keep = pltpu.make_async_copy(xt_own, xt_all.at[:, lanes(me_d)], own_sem.at[1])
+    xt_keep = pltpu.make_async_copy(xt_own, xt_all.at[:, lanes(me_d)], own_sem.at[0])
     xt_keep.start()
 
     sibling = me_d + 1 - 2 * (me_d % 2)
 
     def xt_copy(k):
         return remote(
-            xt_own, xt_all.at[:, lanes(me_d)], xt_s.at[k], xt_r.at[k],
+            xt_own, xt_all.at[:, lanes(me_d)], xt_s, xt_r,
             lax.rem(me_d + 2 * k, nd), me_s,
         )
 
@@ -183,7 +185,7 @@
         here = lanes(lax.rem(me_d - 2 * k + nd, nd))
         return remote(
             xt_all.at[:, here] if k else xt_own, xt_all.at[:, here],
-            share_s.at[k], share_r.at[k], sibling, me_s,
+            share_s, share_r, sibling, me_s,
         )
 
     for k in range(1, nd // 2):
@@ -215,7 +217,7 @@
     table_vm[...] = jnp.zeros_like(table_vm)
     table_vm[:SLOTS, :nb] = before
     table_vm[SLOTS : SLOTS + 1, :nb] = final
-    table_copy = pltpu.make_async_copy(table_vm, table, own_sem.at[2])
+    table_copy = pltpu.make_async_copy(table_vm, table, own_sem.at[1])
     table_copy.start()
     chain[SLOTS * nb] = jnp.zeros((2 * FEAT, BLK), F32)
 
@@ -236,25 +238,16 @@
         right[b, FEAT:, BLK:] = empty
 
     def arrive(i, c):
+        landed(head_in.at[pl.ds(0, 4)], head_r.at[i])
         for j in range(4):
-            if j == 0:
-
-                @pl.when(i == 0)
-                def _():
-                    own_head.wait()
-
-                @pl.when(i > 0)
-                def _():
-                    head_copy(i, 0).wait_recv()
-
-            else:
-                head_copy(i, j).wait_recv()
             prepare(4 * got_group(i) + lax.rem(me_s % 4 - j + 4, 4))
         return c
 
     lax.fori_loop(0, ng - 1, arrive, 0)
+    others = nd // 2 - 1
+    if others:
+        landed(xt_all.at[:, pl.ds(0, others * BLK)], xt_r)
     for k in range(1, nd // 2):
-        xt_copy(k).wait_recv()
         share_copy(k).start()
     lax.fori_loop(ng - 1, ng, arrive, 0)
     table_copy.wait()
@@ -316,22 +309,27 @@
             piece = pl.ds(lo, FEAT)
             return remote(
                 row_out.at[peer, piece], row_in.at[me_s, piece],
-                send_sem.at[i, j], recv_sem.at[i, j], me_d, peer,
+                send_sem, recv_sem(i), me_d, peer,
             )
 
         return copy
 
-    late_copy = piece_copy(0, late_s, late_r)
-    row_copy = piece_copy(FEAT, row_s, row_r)
+    late_copy = piece_copy(0, late_s, lambda i: late_r)
+    row_copy = piece_copy(FEAT, row_s, lambda i: row_r.at[i])
 
     def col_copy(i, j):
         peer = peer_at(me_s, i, j, ng, 1)
         return remote(
-            col_out.at[peer], col_in.at[me_s], col_s.at[i, j], col_r.at[i, j], me_d, peer
-        )
-
-    own_row = pltpu.make_async_copy(row_out.at[me_s], row_in.at[me_s], own_sem.at[3])
-    own_col = pltpu.make_async_copy(col_out.at[me_s], col_in.at[me_s], own_sem.at[4])
+            col_out.at[peer], col_in.at[me_s], col_s, col_r.at[i], me_d, peer
+        )
+
+    def own_piece(lo, sem):
+        piece = pl.ds(lo, FEAT)
+        return pltpu.make_async_copy(row_out.at[me_s, piece], row_in.at[me_s, piece], sem)
+
+    own_late = own_piece(0, late_r)
+    own_row = own_piece(FEAT, row_r.at[0])
+    own_col = pltpu.make_async_copy(col_out.at[me_s], col_in.at[me_s], col_r.at[0])
     score_stage(0, 0)
     score_stage(1, 1)
     soft_stage(0)
@@ -354,6 +352,7 @@
     steps(1, 0)
     lax.fori_loop(2, (nb - 2) // 2, send_steps, 0)
     own_row.start()
+    own_late.start()
     row_copy(ng - 1, 0).start()
     row_copy(ng - 1, 1).start()
     soft_stage(1)
@@ -384,16 +383,6 @@
 
     lax.fori_loop(0, ng, col_send, 0)
 
-    def depart(i, *copies):
-        @pl.when(i > 0)
-        def _():
-            for copy in copies:
-                copy(i, 0).wait_send()
-
-        for copy in copies:
-            for j in range(1, 4):
-                copy(i, j).wait_send()
-
     def late_send(i, c):
         @pl.when(i > 0)
         def _():
@@ -401,27 +390,26 @@
 
         for j in range(1, 4):
             late_copy(i, j).start()
-        depart(i, head_copy)
         return c
 
     lax.fori_loop(0, ng, late_send, 0)
-    for k in range(1, nd // 2):
-        xt_copy(k).wait_send()
-    for k in range(nd // 2):
-        share_copy(k).wait_send()
+    landed(head_out.at[pl.ds(0, ns - 1)], head_s)
+    if others:
+        landed(xt_all.at[:, pl.ds(0, others * BLK)], xt_s)
+    landed(xt_all.at[:, pl.ds(0, nd // 2 * BLK)], share_s)
 
     def tile_own(g, m):
         t = m * ng + g
         return pltpu.make_async_copy(
             dq.at[g, pl.ds(m * BLK, BLK)], wg_in.at[lanes(t % tpd), lanes(me_d)],
-            tile_o.at[t % tpd],
+            tile_r.at[t % tpd],
         )
 
     def tile_copy(g, m):
         t = m * ng + g
         return remote(
             dq.at[g, pl.ds(m * BLK, BLK)], wg_in.at[lanes(t % tpd), lanes(me_d)],
-            tile_s.at[g, m], tile_r.at[me_d, t % tpd], t // tpd, me_s,
+            tile_s, tile_r.at[t % tpd], t // tpd, me_s,
         )
 
     def tile_send(g, m):
@@ -435,43 +423,22 @@
         def _():
             tile_copy(g, m).start()
 
-    def await_group(i, own, copy):
-        @pl.when(i == 0)
-        def _():
-            own.wait()
-
-        @pl.when(i > 0)
-        def _():
-            copy(i, 0).wait_recv()
-
-        for j in range(1, 4):
-            copy(i, j).wait_recv()
-
     def take_rows(i, c):
         g = got_group(i)
-        await_group(i, own_row, row_copy)
+        landed(row_in.at[pl.ds(0, 4), pl.ds(FEAT, FEAT)], row_r.at[i])
         for j in range(4):
             dq[g, j * FEAT : (j + 1) * FEAT] = row_in[4 * g + j, FEAT:]
         tile_send(g, 0)
-        depart(i, row_copy)
-        return c
-
-    def take_late(i, c):
-        g = got_group(i)
-
-        @pl.when(i > 0)
-        def _():
-            late_copy(i, 0).wait_recv()
-
-        for j in range(1, 4):
-            late_copy(i, j).wait_recv()
+        return c
+
+    def take_late(g, c):
         mix = jnp.concatenate([row_in[4 * g + j, :FEAT] for j in range(4)], axis=0)
         mix_ref[:, lanes(g)] = jnp.transpose(mix.astype(F32)).astype(BF16)
         return c
 
     def take_cols(i, c):
         g = got_group(i)
-        await_group(i, own_col, col_copy)
+        landed(col_in.at[pl.ds(0, 4)], col_r.at[i])
         for j in range(4):
             dq[g, BLK + j * FEAT : BLK + (j + 1) * FEAT] = col_in[4 * g + j, :FEAT]
             dq[g, 2 * BLK + j * FEAT : 2 * BLK + (j + 1) * FEAT] = col_in[4 * g + j, FEAT:]
@@ -482,8 +449,7 @@
     lax.fori_loop(0, ng, take_rows, 0)
     lax.fori_loop(0, ng, take_cols, 0)
     xt_keep.wait()
-    for k in range(nd // 2):
-        share_copy(k).wait_recv()
+    landed(xt_all.at[:, pl.ds(0, nd // 2 * BLK)], share_r)
 
     chunk = nz * FEAT
     half = chunk // 2
@@ -496,41 +462,26 @@
     def relay_copy(t, way):
         return remote(
             part.at[t, rows_of(across, way)], relay.at[t, way],
-            relay_s.at[t, way], relay_r.at[t, way], me_d, (up, down)[way] * nz + me_z,
+            relay_s, relay_r.at[t], me_d, (up, down)[way] * nz + me_z,
         )
 
     def fold_copy(t, way, which):
         return remote(
             part.at[t, rows_of((up, down)[way], which)], fold.at[t, way, which],
-            fold_s.at[t, way, which], fold_r.at[t, way, which],
+            fold_s, fold_r.at[t],
             me_d, (up, down)[way] * nz + me_z,
         )
 
-    def last_copy(t, k):
+    def last_copy(k):
         to = lax.rem(me_z + k, nz)
         return remote(
-            mid.at[t, pl.ds(pl.multiple_of(to * FEAT, FEAT), FEAT)], last_in.at[t, k - 1],
-            last_s.at[t, k], last_r.at[t, k], me_d, me_y * nz + to,
-        )
-
-    def tile_done(t, k):
-        src = lax.rem(me_d + k, nd)
-        return remote(
-            dq.at[0, pl.ds(0, BLK)], wg_in.at[pl.ds(t * BLK, BLK), lanes(src)],
-            tile_s.at[0, 0], tile_r.at[src, t], src, me_s,
+            mid.at[pl.ds(pl.multiple_of(to * FEAT, FEAT), FEAT)], last_in.at[k - 1],
+            last_s, last_r, me_d, me_y * nz + to,
         )
 
     for first, last in ((0, tpd - 1), (tpd - 1, tpd)):
         for t in range(first, last):
-            pltpu.make_async_copy(
-                dq.at[0, pl.ds(0, BLK)], wg_in.at[pl.ds(t * BLK, BLK), lanes(me_d)], tile_o.at[t]
-            ).wait()
-
-            def arrived(k, c):
-                tile_done(t, k).wait_recv()
-                return c
-
-            lax.fori_loop(1, nd, arrived, 0)
+            landed(wg_in.at[pl.ds(t * BLK, BLK)], tile_r.at[t])
         partial_sum = lax.dot_general(
             xt_all[...], wg_in[first * BLK : last * BLK], (((1,), (1,)), ((), ())),
             preferred_element_type=F32,
@@ -550,58 +501,47 @@
         gn_ref[:, cols] = jnp.transpose(total).astype(BF16)
         return c
 
-    def sent(i, c):
-        depart(i, col_copy, late_copy)
-        for m in range(3):
-
-            @pl.when((m * ng + i) // tpd != me_d)
-            def _():
-                tile_copy(i, m).wait_send()
-
-        return c
-
     steps_gn = hidden // (2 * BLK)
     lax.fori_loop(0, steps_gn // 2, node_cols, 0)
     for t in range(tpd):
+        landed(relay.at[t], relay_r.at[t])
         for way in range(2):
-            relay_copy(t, way).wait_recv()
             rows = rows_of((up, down)[way], way)
             part[t, rows] = (
                 part[t, rows].astype(F32) + relay[t, way].astype(F32)
             ).astype(BF16)
             fold_copy(t, way, way).start()
+    lax.fori_loop(steps_gn // 2, steps_gn, node_cols, 0)
+    gn_done = pltpu.make_async_copy(gn_ref, gn_out, out_sem.at[1])
+    gn_done.start()
+    for t in range(tpd):
+        landed(fold.at[t], fold_r.at[t])
+        for which in range(2):
+            total = part[t, rows_of(me_y, which)].astype(F32)
+            for way in range(2):
+                total += fold[t, way, which].astype(F32)
+            mid[which * half : (which + 1) * half, t * BLK : (t + 1) * BLK] = total.astype(BF16)
+    for k in sorted(range(1, nz), key=lambda k: -min(k, nz - k)):
+        last_copy(k).start()
+
+    landed(row_in.at[:, pl.ds(0, FEAT)], late_r)
     lax.fori_loop(0, ng, take_late, 0)
     mix_done = pltpu.make_async_copy(mix_ref, mix_out, out_sem.at[0])
     mix_done.start()
-    lax.fori_loop(steps_gn // 2, steps_gn, node_cols, 0)
-    gn_done = pltpu.make_async_copy(gn_ref, gn_out, out_sem.at[1])
-    gn_done.start()
-    lax.fori_loop(0, ng, sent, 0)
-    for t in range(tpd):
-        for which in range(2):
-            total = part[t, rows_of(me_y, which)].astype(F32)
-            for way in range(2):
-                fold_copy(t, way, which).wait_recv()
-                total += fold[t, way, which].astype(F32)
-            mid[t, which * half : (which + 1) * half] = total.astype(BF16)
-        for k in sorted(range(1, nz), key=lambda k: -min(k, nz - k)):
-            last_copy(t, k).start()
-    for t in range(tpd):
-        total = mid[t, pl.ds(pl.multiple_of(me_z * FEAT, FEAT), FEAT)].astype(F32)
-        for k in range(1, nz):
-            last_copy(t, k).wait_recv()
-            total += last_in[t, k - 1].astype(F32)
-        wg_ref[:, t * BLK : (t + 1) * BLK] = total
+    landed(row_out.at[pl.ds(0, ns - 1), pl.ds(FEAT, FEAT)], row_s)
+    landed(row_out.at[pl.ds(0, ns - 1), pl.ds(0, FEAT)], late_s)
+    landed(col_out.at[pl.ds(0, ns - 1)], col_s)
+    landed(dq.at[pl.ds(0, ng - 1)], tile_s)
+    landed(relay, relay_s)
+    landed(fold, fold_s)
+    landed(last_in, last_r)
+    total = mid[pl.ds(pl.multiple_of(me_z * FEAT, FEAT), FEAT)].astype(F32)
+    for k in range(1, nz):
+        total += last_in[k - 1].astype(F32)
+    wg_ref[...] = total
     wg_done = pltpu.make_async_copy(wg_ref, wg_out, out_sem.at[2])
     wg_done.start()
-
-    for t in range(tpd):
-        for way in range(2):
-            relay_copy(t, way).wait_send()
-            for which in range(2):
-                fold_copy(t, way, which).wait_send()
-        for k in range(1, nz):
-            last_copy(t, k).wait_send()
+    landed(last_in, last_s)
     mix_done.wait()
     gn_done.wait()
     wg_done.wait()
@@ -673,32 +613,31 @@
             pltpu.VMEM((tpd, hidden, BLK), BF16),
             pltpu.VMEM((tpd, 2, chunk // 2, BLK), BF16),
             pltpu.VMEM((tpd, 2, 2, chunk // 2, BLK), BF16),
-            pltpu.VMEM((tpd, chunk, BLK), BF16),
-            pltpu.VMEM((tpd, nz - 1, FEAT, BLK), BF16),
-            dma((ng, 3)),
+            pltpu.VMEM((chunk, tpd * BLK), BF16),
+            pltpu.VMEM((nz - 1, FEAT, tpd * BLK), BF16),
+            dma((ng,)),
             dma((5,)),
-            dma((ng, 4)),
-            dma((ng, 4)),
-            dma((nd,)),
-            dma((nd,)),
-            dma((ng, 4)),
-            dma((ng, 4)),
-            dma((ng, 4)),
-            dma((ng, 4)),
-            dma((5,)),
-            dma((ng, 3)),
-            dma((nd, tpd)),
+            dma,
+            dma((ng,)),
+            dma,
+            dma,
+            dma,
+            dma((ng,)),
+            dma,
+            dma((ng,)),
+            dma((2,)),
+            dma,
             dma((tpd,)),
-            dma((tpd, 2)),
-            dma((tpd, 2)),
-            dma((tpd, 2, 2)),
-            dma((tpd, 2, 2)),
-            dma((tpd, nz)),
-            dma((tpd, nz)),
-            dma((ng, 4)),
-            dma((ng, 4)),
-            dma((nd // 2,)),
-            dma((nd // 2,)),
+            dma,
+            dma((tpd,)),
+            dma,
+            dma((tpd,)),
+            dma,
+            dma,
+            dma,
+            dma,
+            dma,
+            dma,
             dma((3,)),
         ],
         compiler_params=pltpu.CompilerParams(

time: 87.4 us -> 84.1 us (0.962)
  Pallas kernels: 86 us -> 82.8 us
    pallas_call x1, Pallas kernels: 84.2 us -> 81 us  [per_device(): pl.pallas_call(functools.partial(whole_kernel, nd, ns, ny, nz, tpd), out_...]
where the time goes in v7:
time: 84.1 us; the launch traced here: 83.4 us
  Pallas kernels  82.8 us (98%)
    pallas_call x1, Pallas kernels, per_device(): pl.pallas_call(functools.partial(whole_kernel, nd, ns, ny, nz, tpd), out_...  81 us
    pallas_call x1, Pallas kernels, per_device(): pl.pallas_call(settle_kernel, out_shape=out_shape, in_specs=[any_spec] *...  1.79 us

profile of v7, /device:TPU:2, one launch (start us, length us, event | category | flops | bytes accessed | tf_op | source)
XLA Modules:
  0.0 83.4 jit_solution(14636763466081636081)
XLA Ops:
  0.6 81.0 %whole.1 = (bf16[128,1024]{1,0:T(8,128)(2,1)}, bf16[128,1024]{1,0:T(8,128)(2,1)}, f32[32,384]{1,0:T(8,128)}) custom-call(bf16[1,128,1024]{2,1,0:T(8,128)(2,1)} %x_in.1, bf16[1024,3072]{1,0:T(8,128)(2,1)} %w_in.1, bf16[1,128,1024]{2,1,0:T(8,128)(2,1)} %cot_in.1, s32[1,4,32]{2,1,0:T(4,128)} %bitcast.4, s32[1,32]{1,0:T(1,128)} %counts_in.1), custom_call_target="tpu_custom_call" | custom-call | tf_op jit(solution)/shard_map/whole/pallas_call | solution.py:578
  81.6 1.8 %settle.1 = (bf16[128,1024]{1,0:T(8,128)(2,1)}, bf16[128,1024]{1,0:T(8,128)(2,1)}, f32[32,384]{1,0:T(8,128)}) custom-call(bf16[128,1024]{1,0:T(8,128)(2,1)} %get-tuple-element.9.mix_in, bf16[128,1024]{1,0:T(8,128)(2,1)} %get-tuple-element.10.gn_in, f32[32,384]{1,0:T(8,128)} %get-tuple-element.11.wg_in), custom_call_target="tpu_custom_call" | custom-call | tf_op jit(solution)/shard_map/settle/pallas_call | solution.py:648

commit v8 on v7

--- a/solution.py
+++ b/solution.py
@@ -21,23 +21,6 @@
     return lax.broadcasted_iota(jnp.int32, shape, len(shape) - 1)
 
 
-def swap_quarters(tiles):
-    lane = lane_ids(tiles[0].shape)
-    low = lane < 64
-    even = (lane // 32) % 2 == 0
-    a0, a1, a2, a3 = tiles
-    b0 = jnp.where(low, a0, pltpu.roll(a2, 64, 1))
-    b2 = jnp.where(low, pltpu.roll(a0, 64, 1), a2)
-    b1 = jnp.where(low, a1, pltpu.roll(a3, 64, 1))
-    b3 = jnp.where(low, pltpu.roll(a1, 64, 1), a3)
-    return (
-        jnp.where(even, b0, pltpu.roll(b1, 32, 1)),
-        jnp.where(even, pltpu.roll(b0, 96, 1), b1),
-        jnp.where(even, b2, pltpu.roll(b3, 32, 1)),
-        jnp.where(even, pltpu.roll(b2, 96, 1), b3),
-    )
-
-
 def greet(me_d, me_s, nd, ns):
     barrier = pltpu.get_barrier_semaphore()
 
@@ -67,11 +50,11 @@
     nd, ns, ny, nz, tpd,
     x_in, w_in, cot_in, cols_in, counts_in,
     mix_out, gn_out, wg_out,
-    cols_ref, cols_vec, counts_ref, mix_ref, gn_ref, wg_ref, x_vm, cot_vm, w_vm, head_out, head_in, xt_own, xt_all,
-    turned_kv, left, right, chain, row_out, col_out, row_in, col_in,
+    cols_ref, cols_vec, counts_ref, mix_ref, gn_ref, wg_ref, x_vm, cot_vm, w_vm, kv_out, kv_in, qd_out, qd_in, natural, xt_own, xt_all,
+    chain, row_out, col_out, row_in, col_in,
     raw_even, raw_odd, top_even, top_odd, pair_even, pair_odd,
     table_vm, table, dq, wg_in, part, relay, fold, mid, last_in,
-    w_sem, load_sem, head_s, head_r, xt_s, xt_r, row_s, row_r, col_s, col_r,
+    w_sem, load_sem, kv_s, kv_r, qd_s, qd_r, xt_s, xt_r, row_s, row_r, col_s, col_r,
     own_sem, tile_s, tile_r, relay_s, relay_r, fold_s, fold_r, last_s, last_r, late_s, late_r, share_s, share_r, out_sem,
 ):
     me_d, me_s = lax.axis_index("dp"), lax.axis_index("seq")
@@ -93,7 +76,7 @@
         return lax.rem(my_group - i + ng, ng)
 
     def row_at(k):
-        return peer_at(me_s, k // 4, k % 4, ng, 1)
+        return peer_at(me_s, k // 4, k % 4, ng, -1)
 
     def remote(src, dst, send_sem, recv_sem, d, s):
         return pltpu.make_async_remote_copy(
@@ -109,17 +92,21 @@
     load_cot = pltpu.make_async_copy(cot_in.at[0], cot_vm, load_sem.at[1])
     load_x.start()
 
-    def w_copy(i, m):
+    def w_start(part, i):
         g = sent_group(i)
-        return pltpu.make_async_copy(
-            w_in.at[:, lanes(m * ng + g)],
-            w_vm.at[g, :, pl.ds(m * BLK, BLK)],
-            w_sem.at[i],
-        )
-
-    def w_start(i, c):
-        for m in range(3):
-            w_copy(i, m).start()
+        for m in ((1, 2), (0,))[part]:
+            pltpu.make_async_copy(
+                w_in.at[:, lanes(m * ng + g)],
+                w_vm.at[g, :, pl.ds(m * BLK, BLK)],
+                w_sem.at[part, i],
+            ).start()
+
+    def kv_weights(i, c):
+        w_start(0, i)
+        return c
+
+    def q_weights(i, c):
+        w_start(1, i)
         return c
 
     small_loads = [
@@ -128,46 +115,69 @@
             ((cols_in, cols_ref), (cols_in.at[0], cols_vec), (counts_in, counts_ref))
         )
     ]
-    w_start(0, 0)
+    lax.fori_loop(0, ng, kv_weights, 0)
     load_cot.start()
-    lax.fori_loop(1, ng, w_start, 0)
+    lax.fori_loop(0, ng, q_weights, 0)
     for load in small_loads:
         load.start()
     load_x.wait()
-    load_cot.wait()
-
-    def head_copy(i, j):
-        peer = peer_at(me_s, i, j, ng, 1)
-        return remote(
-            head_out.at[peer], head_in.at[me_s], head_s, head_r.at[i], me_d, peer
-        )
-
-    own_head = pltpu.make_async_copy(head_out.at[me_s], head_in.at[me_s], head_r.at[0])
-
-    def project(i, c):
+
+    def pieces_copy(out, into, send_sem, recv_sem):
+        def copy(i, j):
+            peer = peer_at(me_s, i, j, ng, 1)
+            return remote(out.at[peer], into.at[me_s], send_sem, recv_sem.at[i], me_d, peer)
+
+        return copy, pltpu.make_async_copy(out.at[me_s], into.at[me_s], recv_sem.at[0])
+
+    kv_copy, own_kv = pieces_copy(kv_out, kv_in, kv_s, kv_r)
+    qd_copy, own_qd = pieces_copy(qd_out, qd_in, qd_s, qd_r)
+
+    def start_group(i, own, copy):
+        @pl.when(i == 0)
+        def _():
+            own.start()
+
+        @pl.when(i > 0)
+        def _():
+            copy(i, 0).start()
+
+        for j in range(1, 4):
+            copy(i, j).start()
+
+    def project_kv(i, c):
         g = sent_group(i)
-        landed(w_vm.at[g], w_sem.at[i])
-        qkv = jnp.dot(x_vm[...], w_vm[g], preferred_element_type=F32).astype(BF16)
-        packed = swap_quarters(
-            (qkv[:, :BLK], qkv[:, BLK : 2 * BLK], qkv[:, 2 * BLK :], cot_vm[:, lanes(g)])
-        )
-        for j in range(4):
-            head_out[4 * g + j] = packed[j]
+        landed(w_vm.at[g, :, pl.ds(BLK, 2 * BLK)], w_sem.at[0, i])
+        flat = jnp.dot(x_vm[...], w_vm[g, :, BLK:], preferred_element_type=F32)
+        for m in range(2):
+            turned = jnp.transpose(flat[:, m * BLK : (m + 1) * BLK]).astype(BF16)
+            for j in range(4):
+                kv_out[4 * g + j, m * FEAT : (m + 1) * FEAT] = turned[
+                    j * FEAT : (j + 1) * FEAT
+                ]
 
         @pl.when(i == 0)
         def _():
             pl.semaphore_wait(barrier, ns + nd - 2)
-            own_head.start()
-
-        @pl.when(i > 0)
-        def _():
-            head_copy(i, 0).start()
-
-        for j in range(1, 4):
-            head_copy(i, j).start()
-        return c
-
-    lax.fori_loop(0, ng, project, 0)
+
+        start_group(i, own_kv, kv_copy)
+        return c
+
+    def project_q(i, c):
+        g = sent_group(i)
+        landed(w_vm.at[g, :, pl.ds(0, BLK)], w_sem.at[1, i])
+        flat = jnp.dot(x_vm[...], w_vm[g, :, :BLK], preferred_element_type=F32)
+        for m, piece in enumerate((flat, cot_vm[:, lanes(g)].astype(F32))):
+            turned = jnp.transpose(piece).astype(BF16)
+            for j in range(4):
+                qd_out[4 * g + j, m * FEAT : (m + 1) * FEAT] = turned[
+                    j * FEAT : (j + 1) * FEAT
+                ]
+        start_group(i, own_qd, qd_copy)
+        return c
+
+    lax.fori_loop(0, ng, project_kv, 0)
+    load_cot.wait()
+    lax.fori_loop(0, ng, project_q, 0)
 
     xt_own[...] = jnp.transpose(x_vm[...].astype(F32)).astype(BF16)
     xt_keep = pltpu.make_async_copy(xt_own, xt_all.at[:, lanes(me_d)], own_sem.at[0])
@@ -196,8 +206,8 @@
         load.wait()
     named_now = cols_vec[...]
     row_ids = lane_ids((SLOTS, nb))
-    place = 4 * lax.rem(row_ids // 4 - my_group + ng, ng) + lax.rem(
-        row_ids % 4 - me_s % 4 + 4, 4
+    place = 4 * lax.rem(my_group - row_ids // 4 + ng, ng) + lax.rem(
+        me_s % 4 - row_ids % 4 + 4, 4
     )
     col_ids = lane_ids((1, nb))
 
@@ -222,43 +232,32 @@
     chain[SLOTS * nb] = jnp.zeros((2 * FEAT, BLK), F32)
 
     raw, top, pair = (raw_even, raw_odd), (top_even, top_odd), (pair_even, pair_odd)
-    quarter = lane_ids((BLK, BLK)) // FEAT
-
-    def prepare(b):
-        mine = head_in[b]
-        zero = jnp.zeros_like(mine)
-        turned = jnp.transpose(mine.astype(F32)).astype(BF16)
+
+    def arrive(i, c):
+        landed(kv_in.at[pl.ds(0, 4)], kv_r.at[i])
+        for j in range(4):
+            b = row_at(4 * i + j)
+            natural[b] = jnp.transpose(kv_in[b].astype(F32)).astype(BF16)
+        return c
+
+    lax.fori_loop(0, ng, arrive, 0)
+    table_copy.wait()
+
+    def spread_pieces(r, side):
+        queries, cot = qd_in[r, :FEAT], qd_in[r, FEAT:]
         empty = jnp.zeros((FEAT, BLK), BF16)
-        turned_kv[b] = turned[FEAT : 3 * FEAT]
-        left[b, :BLK] = jnp.where(quarter == 1, pltpu.roll(mine, 32, 1), zero)
-        left[b, BLK:] = jnp.where(quarter == 2, pltpu.roll(mine, 96, 1), zero)
-        right[b, :FEAT, :BLK] = empty
-        right[b, :FEAT, BLK:] = turned[:FEAT]
-        right[b, FEAT:, :BLK] = turned[3 * FEAT :]
-        right[b, FEAT:, BLK:] = empty
-
-    def arrive(i, c):
-        landed(head_in.at[pl.ds(0, 4)], head_r.at[i])
-        for j in range(4):
-            prepare(4 * got_group(i) + lax.rem(me_s % 4 - j + 4, 4))
-        return c
-
-    lax.fori_loop(0, ng - 1, arrive, 0)
-    others = nd // 2 - 1
-    if others:
-        landed(xt_all.at[:, pl.ds(0, others * BLK)], xt_r)
-    for k in range(1, nd // 2):
-        share_copy(k).start()
-    lax.fori_loop(ng - 1, ng, arrive, 0)
-    table_copy.wait()
+        upper, lower = [queries, empty], [empty, cot]
+        if side:
+            upper, lower = upper[::-1], lower[::-1]
+        return jnp.concatenate(
+            [jnp.concatenate(upper, axis=1), jnp.concatenate(lower, axis=1)], axis=0
+        )
 
     def score_stage(k, p):
         r = row_at(k)
         count = counts_ref[0, r]
-        keys = jnp.concatenate([head_in[cols_ref[0, s, r]] for s in range(SLOTS)], axis=0)
-        both = lax.dot_general(
-            keys, left[r], (((1,), (1,)), ((), ())), preferred_element_type=F32
-        )
+        keys = jnp.concatenate([natural[cols_ref[0, s, r]] for s in range(SLOTS)], axis=0)
+        both = jnp.dot(keys, spread_pieces(r, 0), preferred_element_type=F32)
         best = None
         for s in range(SLOTS):
             block = both[s * BLK : (s + 1) * BLK]
@@ -293,19 +292,19 @@
         r = row_at(k)
         named = [cols_ref[0, s, r] for s in range(SLOTS)]
         both = pair[p][...]
-        turned = jnp.concatenate([turned_kv[n] for n in named], axis=1)
+        turned = jnp.concatenate([kv_in[n] for n in named], axis=1)
         row_side = jnp.dot(turned, both, preferred_element_type=F32)
         row_out[r, :FEAT] = row_side[FEAT:, :BLK].astype(BF16)
         row_out[r, FEAT:] = (row_side[:FEAT, BLK:] * scale).astype(BF16)
         key_side = lax.dot_general(
-            right[r], both, (((1,), (1,)), ((), ())), preferred_element_type=F32
+            spread_pieces(r, 1), both, (((1,), (1,)), ((), ())), preferred_element_type=F32
         )
         for s in range(SLOTS):
             chain[4 * k + s] = key_side[:, s * BLK : (s + 1) * BLK] + chain[table[s, r]]
 
     def piece_copy(lo, send_sem, recv_sem):
         def copy(i, j):
-            peer = peer_at(me_s, i, j, ng, 1)
+            peer = row_at(4 * i + j)
             piece = pl.ds(lo, FEAT)
             return remote(
                 row_out.at[peer, piece], row_in.at[me_s, piece],
@@ -330,36 +329,35 @@
     own_late = own_piece(0, late_r)
     own_row = own_piece(FEAT, row_r.at[0])
     own_col = pltpu.make_async_copy(col_out.at[me_s], col_in.at[me_s], col_r.at[0])
+    def one_step(k, p, grad=True):
+        score_stage(k + 1, 1 - p)
+        soft_stage(p)
+        if grad:
+            grad_stage(k - 1, 1 - p)
+
+    landed(qd_in.at[pl.ds(0, 4)], qd_r.at[0])
     score_stage(0, 0)
-    score_stage(1, 1)
-    soft_stage(0)
-
-    def steps(i, c):
-        for u in range(2):
-            k, p = 1 + 2 * i + u, (1 + u) % 2
-            score_stage(k + 1, 1 - p)
-            soft_stage(p)
-            grad_stage(k - 1, 1 - p)
-        return c
-
-    def send_steps(i, c):
-        row_copy((i - 1) // 2, 2 * ((i - 1) % 2)).start()
-        row_copy((i - 1) // 2, 2 * ((i - 1) % 2) + 1).start()
-        return steps(i, c)
-
-    steps(0, 0)
-    row_copy(0, 1).start()
-    steps(1, 0)
-    lax.fori_loop(2, (nb - 2) // 2, send_steps, 0)
-    own_row.start()
-    own_late.start()
-    row_copy(ng - 1, 0).start()
-    row_copy(ng - 1, 1).start()
+    one_step(0, 0, grad=False)
+    one_step(1, 1)
+    one_step(2, 0)
+
+    def four_rows(i, c):
+        @pl.when(i > 0)
+        def _():
+            start_group(i - 1, own_row, row_copy)
+
+        landed(qd_in.at[pl.ds(0, 4)], qd_r.at[i + 1])
+        for u in range(4):
+            one_step(3 + 4 * i + u, (1 + u) % 2)
+        return c
+
+    lax.fori_loop(0, ng - 1, four_rows, 0)
+    start_group(ng - 2, own_row, row_copy)
     soft_stage(1)
     grad_stage(nb - 2, 0)
     grad_stage(nb - 1, 1)
-    row_copy(ng - 1, 2).start()
-    row_copy(ng - 1, 3).start()
+    start_group(ng - 1, own_row, row_copy)
+    own_late.start()
 
     def col_send(i, c):
         for j in range(4):
@@ -367,21 +365,15 @@
             total = chain[table[SLOTS, peer]]
             col_out[peer, :FEAT] = (total[:FEAT] * scale).astype(BF16)
             col_out[peer, FEAT:] = total[FEAT:].astype(BF16)
-            if j == 0:
-
-                @pl.when(i == 0)
-                def _():
-                    own_col.start()
-
-                @pl.when(i > 0)
-                def _():
-                    col_copy(i, 0).start()
-
-            else:
-                col_copy(i, j).start()
+        start_group(i, own_col, col_copy)
         return c
 
     lax.fori_loop(0, ng, col_send, 0)
+    others = nd // 2 - 1
+    if others:
+        landed(xt_all.at[:, pl.ds(0, others * BLK)], xt_r)
+    for k in range(1, nd // 2):
+        share_copy(k).start()
 
     def late_send(i, c):
         @pl.when(i > 0)
@@ -393,7 +385,8 @@
         return c
 
     lax.fori_loop(0, ng, late_send, 0)
-    landed(head_out.at[pl.ds(0, ns - 1)], head_s)
+    landed(kv_out.at[pl.ds(0, ns - 1)], kv_s)
+    landed(qd_out.at[pl.ds(0, ns - 1)], qd_s)
     if others:
         landed(xt_all.at[:, pl.ds(0, others * BLK)], xt_s)
     landed(xt_all.at[:, pl.ds(0, nd // 2 * BLK)], share_s)
@@ -424,7 +417,7 @@
             tile_copy(g, m).start()
 
     def take_rows(i, c):
-        g = got_group(i)
+        g = sent_group(i)
         landed(row_in.at[pl.ds(0, 4), pl.ds(FEAT, FEAT)], row_r.at[i])
         for j in range(4):
             dq[g, j * FEAT : (j + 1) * FEAT] = row_in[4 * g + j, FEAT:]
@@ -588,13 +581,13 @@
             pltpu.VMEM((rows, hidden), BF16),
             pltpu.VMEM((rows, hidden), BF16),
             pltpu.VMEM((ng, hidden, 3 * BLK), BF16),
-            pltpu.VMEM((ns, BLK, BLK), BF16),
-            pltpu.VMEM((ns, BLK, BLK), BF16),
+            pltpu.VMEM((ns, 2 * FEAT, BLK), BF16),
+            pltpu.VMEM((ns, 2 * FEAT, BLK), BF16),
+            pltpu.VMEM((ns, 2 * FEAT, BLK), BF16),
+            pltpu.VMEM((ns, 2 * FEAT, BLK), BF16),
+            pltpu.VMEM((ns, BLK, 2 * FEAT), BF16),
             pltpu.VMEM((hidden, BLK), BF16),
             pltpu.VMEM((hidden, nd * BLK), BF16),
-            pltpu.VMEM((ns, 2 * FEAT, BLK), BF16),
-            pltpu.VMEM((ns, 2 * BLK, BLK), BF16),
-            pltpu.VMEM((ns, 2 * FEAT, 2 * BLK), BF16),
             pltpu.VMEM((SLOTS * ns + 1, 2 * FEAT, BLK), F32),
             pltpu.VMEM((ns, 2 * FEAT, BLK), BF16),
             pltpu.VMEM((ns, 2 * FEAT, BLK), BF16),
@@ -615,8 +608,10 @@
             pltpu.VMEM((tpd, 2, 2, chunk // 2, BLK), BF16),
             pltpu.VMEM((chunk, tpd * BLK), BF16),
             pltpu.VMEM((nz - 1, FEAT, tpd * BLK), BF16),
+            dma((2, ng)),
+            dma((5,)),
+            dma,
             dma((ng,)),
-            dma((5,)),
             dma,
             dma((ng,)),
             dma,

time: 84.1 us -> 78.5 us (0.933)
  Pallas kernels: 82.8 us -> 77.5 us
    pallas_call x1, Pallas kernels: 81 us -> 75.7 us  [per_device(): pl.pallas_call(functools.partial(whole_kernel, nd, ns, ny, nz, tpd), out_...]
where the time goes in v8:
time: 78.5 us; the launch traced here: 78.1 us
  Pallas kernels  77.5 us (99%)
    pallas_call x1, Pallas kernels, per_device(): pl.pallas_call(functools.partial(whole_kernel, nd, ns, ny, nz, tpd), out_...  75.7 us
    pallas_call x1, Pallas kernels, per_device(): pl.pallas_call(settle_kernel, out_shape=out_shape, in_specs=[any_spec] *...  1.79 us

profile of v8, /device:TPU:2, one launch (start us, length us, event | category | flops | bytes accessed | tf_op | source)
XLA Modules:
  0.0 78.1 jit_solution(16724136094199649683)
XLA Ops:
  0.6 75.7 %whole.1 = (bf16[128,1024]{1,0:T(8,128)(2,1)}, bf16[128,1024]{1,0:T(8,128)(2,1)}, f32[32,384]{1,0:T(8,128)}) custom-call(bf16[1,128,1024]{2,1,0:T(8,128)(2,1)} %x_in.1, bf16[1024,3072]{1,0:T(8,128)(2,1)} %w_in.1, bf16[1,128,1024]{2,1,0:T(8,128)(2,1)} %cot_in.1, s32[1,4,32]{2,1,0:T(4,128)} %bitcast.4, s32[1,32]{1,0:T(1,128)} %counts_in.1), custom_call_target="tpu_custom_call" | custom-call | tf_op jit(solution)/shard_map/whole/pallas_call | solution.py:571
  76.3 1.8 %settle.1 = (bf16[128,1024]{1,0:T(8,128)(2,1)}, bf16[128,1024]{1,0:T(8,128)(2,1)}, f32[32,384]{1,0:T(8,128)}) custom-call(bf16[128,1024]{1,0:T(8,128)(2,1)} %get-tuple-element.9.mix_in, bf16[128,1024]{1,0:T(8,128)(2,1)} %get-tuple-element.10.gn_in, f32[32,384]{1,0:T(8,128)} %get-tuple-element.11.wg_in), custom_call_target="tpu_custom_call" | custom-call | tf_op jit(solution)/shard_map/settle/pallas_call | solution.py:643

commit v9 on v8

--- a/solution.py
+++ b/solution.py
@@ -56,6 +56,7 @@
     table_vm, table, dq, wg_in, part, relay, fold, mid, last_in,
     w_sem, load_sem, kv_s, kv_r, qd_s, qd_r, xt_s, xt_r, row_s, row_r, col_s, col_r,
     own_sem, tile_s, tile_r, relay_s, relay_r, fold_s, fold_r, last_s, last_r, late_s, late_r, share_s, share_r, out_sem,
+    zpart, z_in, z_mid, y_in, z_s, z_r, y_s, y_r,
 ):
     me_d, me_s = lax.axis_index("dp"), lax.axis_index("seq")
     me_y, me_z = me_s // nz, me_s % nz
@@ -472,18 +473,35 @@
             last_s, last_r, me_d, me_y * nz + to,
         )
 
-    for first, last in ((0, tpd - 1), (tpd - 1, tpd)):
+    def z_copy(k):
+        to = lax.rem(me_z + k, nz)
+        return remote(zpart.at[:, to], z_in.at[k - 1], z_s, z_r, me_d, me_y * nz + to)
+
+    def y_copy(k):
+        to = lax.rem(me_y + k, ny)
+        return remote(z_mid.at[to], y_in.at[k - 1], y_s, y_r, me_d, to * nz + me_z)
+
+    def contract(first, last):
         for t in range(first, last):
             landed(wg_in.at[pl.ds(t * BLK, BLK)], tile_r.at[t])
-        partial_sum = lax.dot_general(
+        return lax.dot_general(
             xt_all[...], wg_in[first * BLK : last * BLK], (((1,), (1,)), ((), ())),
             preferred_element_type=F32,
         ).astype(BF16)
-        for t in range(first, last):
-            part[t] = partial_sum[:, (t - first) * BLK : (t - first + 1) * BLK]
-            for way in range(2):
-                relay_copy(t, way).start()
-                fold_copy(t, way, 1 - way).start()
+
+    far_first = sorted(range(1, nz), key=lambda k: -min(k, nz - k))
+    pairs = tpd - 1
+    zpart[...] = contract(pairs, tpd).reshape(ny, nz, FEAT, BLK)
+    for k in far_first:
+        z_copy(k).start()
+    partial_sum = contract(0, pairs)
+    for t in range(pairs):
+        part[t] = partial_sum[:, t * BLK : (t + 1) * BLK]
+        for way in range(2):
+            relay_copy(t, way).start()
+    for t in range(pairs):
+        for way in range(2):
+            fold_copy(t, way, 1 - way).start()
 
     def node_cols(n, c):
         width = 2 * BLK
@@ -496,7 +514,7 @@
 
     steps_gn = hidden // (2 * BLK)
     lax.fori_loop(0, steps_gn // 2, node_cols, 0)
-    for t in range(tpd):
+    for t in range(pairs):
         landed(relay.at[t], relay_r.at[t])
         for way in range(2):
             rows = rows_of((up, down)[way], way)
@@ -507,15 +525,22 @@
     lax.fori_loop(steps_gn // 2, steps_gn, node_cols, 0)
     gn_done = pltpu.make_async_copy(gn_ref, gn_out, out_sem.at[1])
     gn_done.start()
-    for t in range(tpd):
+    for t in range(pairs):
         landed(fold.at[t], fold_r.at[t])
         for which in range(2):
             total = part[t, rows_of(me_y, which)].astype(F32)
             for way in range(2):
                 total += fold[t, way, which].astype(F32)
             mid[which * half : (which + 1) * half, t * BLK : (t + 1) * BLK] = total.astype(BF16)
-    for k in sorted(range(1, nz), key=lambda k: -min(k, nz - k)):
+    for k in far_first:
         last_copy(k).start()
+    landed(z_in, z_r)
+    total = zpart[:, me_z].astype(F32)
+    for k in range(1, nz):
+        total += z_in[k - 1].astype(F32)
+    z_mid[...] = total.astype(BF16)
+    for k in range(1, ny):
+        y_copy(k).start()
 
     landed(row_in.at[:, pl.ds(0, FEAT)], late_r)
     lax.fori_loop(0, ng, take_late, 0)
@@ -531,10 +556,17 @@
     total = mid[pl.ds(pl.multiple_of(me_z * FEAT, FEAT), FEAT)].astype(F32)
     for k in range(1, nz):
         total += last_in[k - 1].astype(F32)
-    wg_ref[...] = total
+    wg_ref[:, : pairs * BLK] = total
+    landed(y_in, y_r)
+    total = z_mid[me_y].astype(F32)
+    for k in range(1, ny):
+        total += y_in[k - 1].astype(F32)
+    wg_ref[:, pairs * BLK :] = total
     wg_done = pltpu.make_async_copy(wg_ref, wg_out, out_sem.at[2])
     wg_done.start()
     landed(last_in, last_s)
+    landed(z_in, z_s)
+    landed(y_in, y_s)
     mix_done.wait()
     gn_done.wait()
     wg_done.wait()
@@ -603,11 +635,11 @@
             pltpu.SMEM((8, BLK), jnp.int32),
             pltpu.VMEM((ng, 3 * BLK, BLK), BF16),
             pltpu.VMEM((tpd * BLK, nd * BLK), BF16),
-            pltpu.VMEM((tpd, hidden, BLK), BF16),
-            pltpu.VMEM((tpd, 2, chunk // 2, BLK), BF16),
-            pltpu.VMEM((tpd, 2, 2, chunk // 2, BLK), BF16),
-            pltpu.VMEM((chunk, tpd * BLK), BF16),
-            pltpu.VMEM((nz - 1, FEAT, tpd * BLK), BF16),
+            pltpu.VMEM((tpd - 1, hidden, BLK), BF16),
+            pltpu.VMEM((tpd - 1, 2, chunk // 2, BLK), BF16),
+            pltpu.VMEM((tpd - 1, 2, 2, chunk // 2, BLK), BF16),
+            pltpu.VMEM((chunk, (tpd - 1) * BLK), BF16),
+            pltpu.VMEM((nz - 1, FEAT, (tpd - 1) * BLK), BF16),
             dma((2, ng)),
             dma((5,)),
             dma,
@@ -634,6 +666,14 @@
             dma,
             dma,
             dma((3,)),
+            pltpu.VMEM((ny, nz, FEAT, BLK), BF16),
+            pltpu.VMEM((nz - 1, ny, FEAT, BLK), BF16),
+            pltpu.VMEM((ny, FEAT, BLK), BF16),
+            pltpu.VMEM((ny - 1, FEAT, BLK), BF16),
+            dma,
+            dma,
+            dma,
+            dma,
         ],
         compiler_params=pltpu.CompilerParams(
             collective_id=1, has_side_effects=True, vmem_limit_bytes=VMEM_LIMIT

time: 78.5 us -> 77.7 us (0.990)
  Pallas kernels: 77.5 us -> 76.4 us
    pallas_call x1, Pallas kernels: 75.7 us -> 74.6 us  [per_device(): pl.pallas_call(functools.partial(whole_kernel, nd, ns, ny, nz, tpd), out_...]
where the time goes in v9:
time: 77.7 us; the launch traced here: 77 us
  Pallas kernels  76.4 us (98%)
    pallas_call x1, Pallas kernels, per_device(): pl.pallas_call(functools.partial(whole_kernel, nd, ns, ny, nz, tpd), out_...  74.6 us
    pallas_call x1, Pallas kernels, per_device(): pl.pallas_call(settle_kernel, out_shape=out_shape, in_specs=[any_spec] *...  1.79 us

profile of v9, /device:TPU:2, one launch (start us, length us, event | category | flops | bytes accessed | tf_op | source)
XLA Modules:
  0.0 77.0 jit_solution(192134438708058539)
XLA Ops:
  0.6 74.6 %whole.1 = (bf16[128,1024]{1,0:T(8,128)(2,1)}, bf16[128,1024]{1,0:T(8,128)(2,1)}, f32[32,384]{1,0:T(8,128)}) custom-call(bf16[1,128,1024]{2,1,0:T(8,128)(2,1)} %x_in.1, bf16[1024,3072]{1,0:T(8,128)(2,1)} %w_in.1, bf16[1,128,1024]{2,1,0:T(8,128)(2,1)} %cot_in.1, s32[1,4,32]{2,1,0:T(4,128)} %bitcast.4, s32[1,32]{1,0:T(1,128)} %counts_in.1), custom_call_target="tpu_custom_call" | custom-call | tf_op jit(solution)/shard_map/whole/pallas_call | solution.py:603
  75.2 1.8 %settle.1 = (bf16[128,1024]{1,0:T(8,128)(2,1)}, bf16[128,1024]{1,0:T(8,128)(2,1)}, f32[32,384]{1,0:T(8,128)}) custom-call(bf16[128,1024]{1,0:T(8,128)(2,1)} %get-tuple-element.9.mix_in, bf16[128,1024]{1,0:T(8,128)(2,1)} %get-tuple-element.10.gn_in, f32[32,384]{1,0:T(8,128)} %get-tuple-element.11.wg_in), custom_call_target="tpu_custom_call" | custom-call | tf_op jit(solution)/shard_map/settle/pallas_call | solution.py:683

commit v10 on v9

--- a/solution.py
+++ b/solution.py
@@ -385,12 +385,6 @@
             late_copy(i, j).start()
         return c
 
-    lax.fori_loop(0, ng, late_send, 0)
-    landed(kv_out.at[pl.ds(0, ns - 1)], kv_s)
-    landed(qd_out.at[pl.ds(0, ns - 1)], qd_s)
-    if others:
-        landed(xt_all.at[:, pl.ds(0, others * BLK)], xt_s)
-    landed(xt_all.at[:, pl.ds(0, nd // 2 * BLK)], share_s)
 
     def tile_own(g, m):
         t = m * ng + g
@@ -440,8 +434,12 @@
         tile_send(g, 2)
         return c
 
-    lax.fori_loop(0, ng, take_rows, 0)
-    lax.fori_loop(0, ng, take_cols, 0)
+    def bring_home(i, c):
+        late_send(i, 0)
+        take_rows(i, 0)
+        return take_cols(i, c)
+
+    lax.fori_loop(0, ng, bring_home, 0)
     xt_keep.wait()
     landed(xt_all.at[:, pl.ds(0, nd // 2 * BLK)], share_r)
 
@@ -481,27 +479,36 @@
         to = lax.rem(me_y + k, ny)
         return remote(z_mid.at[to], y_in.at[k - 1], y_s, y_r, me_d, to * nz + me_z)
 
-    def contract(first, last):
-        for t in range(first, last):
-            landed(wg_in.at[pl.ds(t * BLK, BLK)], tile_r.at[t])
+    far_first = sorted(range(1, nz), key=lambda k: -min(k, nz - k))
+    pairs = tpd - 1
+    for t in range(tpd):
+        landed(wg_in.at[pl.ds(t * BLK, BLK)], tile_r.at[t])
+
+    def contract(rows, first, last):
         return lax.dot_general(
-            xt_all[...], wg_in[first * BLK : last * BLK], (((1,), (1,)), ((), ())),
+            xt_all[rows, :], wg_in[first * BLK : last * BLK], (((1,), (1,)), ((), ())),
             preferred_element_type=F32,
         ).astype(BF16)
 
-    far_first = sorted(range(1, nz), key=lambda k: -min(k, nz - k))
-    pairs = tpd - 1
-    zpart[...] = contract(pairs, tpd).reshape(ny, nz, FEAT, BLK)
+    def fill(y):
+        rows = pl.ds(pl.multiple_of(y * chunk, chunk), chunk)
+        value = contract(rows, 0, pairs)
+        for t in range(pairs):
+            part[t, rows] = value[:, t * BLK : (t + 1) * BLK]
+
+    fill(across)
+    for t in range(pairs):
+        for way in range(2):
+            relay_copy(t, way).start()
+    zpart[...] = contract(slice(None), pairs, tpd).reshape(ny, nz, FEAT, BLK)
     for k in far_first:
         z_copy(k).start()
-    partial_sum = contract(0, pairs)
-    for t in range(pairs):
-        part[t] = partial_sum[:, t * BLK : (t + 1) * BLK]
-        for way in range(2):
-            relay_copy(t, way).start()
+    fill(up)
+    fill(down)
     for t in range(pairs):
         for way in range(2):
             fold_copy(t, way, 1 - way).start()
+    fill(me_y)
 
     def node_cols(n, c):
         width = 2 * BLK
@@ -513,7 +520,7 @@
         return c
 
     steps_gn = hidden // (2 * BLK)
-    lax.fori_loop(0, steps_gn // 2, node_cols, 0)
+    lax.fori_loop(0, steps_gn // 4, node_cols, 0)
     for t in range(pairs):
         landed(relay.at[t], relay_r.at[t])
         for way in range(2):
@@ -522,9 +529,7 @@
                 part[t, rows].astype(F32) + relay[t, way].astype(F32)
             ).astype(BF16)
             fold_copy(t, way, way).start()
-    lax.fori_loop(steps_gn // 2, steps_gn, node_cols, 0)
-    gn_done = pltpu.make_async_copy(gn_ref, gn_out, out_sem.at[1])
-    gn_done.start()
+    lax.fori_loop(steps_gn // 4, steps_gn // 2, node_cols, 0)
     for t in range(pairs):
         landed(fold.at[t], fold_r.at[t])
         for which in range(2):
@@ -534,6 +539,9 @@
             mid[which * half : (which + 1) * half, t * BLK : (t + 1) * BLK] = total.astype(BF16)
     for k in far_first:
         last_copy(k).start()
+    lax.fori_loop(steps_gn // 2, steps_gn, node_cols, 0)
+    gn_done = pltpu.make_async_copy(gn_ref, gn_out, out_sem.at[1])
+    gn_done.start()
     landed(z_in, z_r)
     total = zpart[:, me_z].astype(F32)
     for k in range(1, nz):
@@ -546,6 +554,11 @@
     lax.fori_loop(0, ng, take_late, 0)
     mix_done = pltpu.make_async_copy(mix_ref, mix_out, out_sem.at[0])
     mix_done.start()
+    landed(kv_out.at[pl.ds(0, ns - 1)], kv_s)
+    landed(qd_out.at[pl.ds(0, ns - 1)], qd_s)
+    if others:
+        landed(xt_all.at[:, pl.ds(0, others * BLK)], xt_s)
+    landed(xt_all.at[:, pl.ds(0, nd // 2 * BLK)], share_s)
     landed(row_out.at[pl.ds(0, ns - 1), pl.ds(FEAT, FEAT)], row_s)
     landed(row_out.at[pl.ds(0, ns - 1), pl.ds(0, FEAT)], late_s)
     landed(col_out.at[pl.ds(0, ns - 1)], col_s)

time: 77.7 us -> 76.4 us (0.983)
  Pallas kernels: 76.4 us -> 75.4 us
    pallas_call x1, Pallas kernels: 74.6 us -> 73.7 us  [per_device(): pl.pallas_call(functools.partial(whole_kernel, nd, ns, ny, nz, tpd), out_...]
where the time goes in v10:
time: 76.4 us; the launch traced here: 76.1 us
  Pallas kernels  75.4 us (99%)
    pallas_call x1, Pallas kernels, per_device(): pl.pallas_call(functools.partial(whole_kernel, nd, ns, ny, nz, tpd), out_...  73.7 us
    pallas_call x1, Pallas kernels, per_device(): pl.pallas_call(settle_kernel, out_shape=out_shape, in_specs=[any_spec] *...  1.79 us

profile of v10, /device:TPU:2, one launch (start us, length us, event | category | flops | bytes accessed | tf_op | source)
XLA Modules:
  0.0 76.1 jit_solution(10416785297254829069)
XLA Ops:
  0.6 73.7 %whole.1 = (bf16[128,1024]{1,0:T(8,128)(2,1)}, bf16[128,1024]{1,0:T(8,128)(2,1)}, f32[32,384]{1,0:T(8,128)}) custom-call(bf16[1,128,1024]{2,1,0:T(8,128)(2,1)} %x_in.1, bf16[1024,3072]{1,0:T(8,128)(2,1)} %w_in.1, bf16[1,128,1024]{2,1,0:T(8,128)(2,1)} %cot_in.1, s32[1,4,32]{2,1,0:T(4,128)} %bitcast.4, s32[1,32]{1,0:T(1,128)} %counts_in.1), custom_call_target="tpu_custom_call" | custom-call | tf_op jit(solution)/shard_map/whole/pallas_call | solution.py:616
  74.3 1.8 %settle.1 = (bf16[128,1024]{1,0:T(8,128)(2,1)}, bf16[128,1024]{1,0:T(8,128)(2,1)}, f32[32,384]{1,0:T(8,128)}) custom-call(bf16[128,1024]{1,0:T(8,128)(2,1)} %get-tuple-element.9.mix_in, bf16[128,1024]{1,0:T(8,128)(2,1)} %get-tuple-element.10.gn_in, f32[32,384]{1,0:T(8,128)} %get-tuple-element.11.wg_in), custom_call_target="tpu_custom_call" | custom-call | tf_op jit(solution)/shard_map/settle/pallas_call | solution.py:696

commit v11 on v10

--- a/solution.py
+++ b/solution.py
@@ -25,8 +25,9 @@
     barrier = pltpu.get_barrier_semaphore()
 
     def seq_hello(k, c):
+        far = 1 + lax.rem(k + ns // 2, ns - 1)
         pl.semaphore_signal(
-            barrier, inc=1, device_id=(me_d, lax.rem(me_s + k, ns)), device_id_type=MESH
+            barrier, inc=1, device_id=(me_d, lax.rem(me_s + far, ns)), device_id_type=MESH
         )
         return c
 
@@ -88,7 +89,6 @@
     def landed(ref, sem):
         pltpu.make_async_copy(ref, ref, sem).wait()
 
-    barrier = greet(me_d, me_s, nd, ns)
     load_x = pltpu.make_async_copy(x_in.at[0], x_vm, load_sem.at[0])
     load_cot = pltpu.make_async_copy(cot_in.at[0], cot_vm, load_sem.at[1])
     load_x.start()
@@ -102,25 +102,17 @@
                 w_sem.at[part, i],
             ).start()
 
-    def kv_weights(i, c):
+    ahead = 2
+    for i in range(ahead):
         w_start(0, i)
-        return c
-
-    def q_weights(i, c):
-        w_start(1, i)
-        return c
-
+    barrier = greet(me_d, me_s, nd, ns)
+    load_cot.start()
     small_loads = [
         pltpu.make_async_copy(src, dst, load_sem.at[2 + n])
         for n, (src, dst) in enumerate(
             ((cols_in, cols_ref), (cols_in.at[0], cols_vec), (counts_in, counts_ref))
         )
     ]
-    lax.fori_loop(0, ng, kv_weights, 0)
-    load_cot.start()
-    lax.fori_loop(0, ng, q_weights, 0)
-    for load in small_loads:
-        load.start()
     load_x.wait()
 
     def pieces_copy(out, into, send_sem, recv_sem):
@@ -161,6 +153,12 @@
             pl.semaphore_wait(barrier, ns + nd - 2)
 
         start_group(i, own_kv, kv_copy)
+
+        @pl.when(i + ahead < ng)
+        def _():
+            w_start(0, i + ahead)
+
+        w_start(1, i)
         return c
 
     def project_q(i, c):
@@ -177,6 +175,8 @@
         return c
 
     lax.fori_loop(0, ng, project_kv, 0)
+    for load in small_loads:
+        load.start()
     load_cot.wait()
     lax.fori_loop(0, ng, project_q, 0)
 
@@ -305,7 +305,7 @@
 
     def piece_copy(lo, send_sem, recv_sem):
         def copy(i, j):
-            peer = row_at(4 * i + j)
+            peer = peer_at(me_s, i, j, ng, -1)
             piece = pl.ds(lo, FEAT)
             return remote(
                 row_out.at[peer, piece], row_in.at[me_s, piece],

time: 76.4 us -> 77.2 us (1.010)
  no operation moved by 1% of the time
where the time goes in v11:
time: 77.2 us; the launch traced here: 76.8 us
  Pallas kernels  76.1 us (99%)
    pallas_call x1, Pallas kernels, per_device(): pl.pallas_call(functools.partial(whole_kernel, nd, ns, ny, nz, tpd), out_...  74.3 us
    pallas_call x1, Pallas kernels, per_device(): pl.pallas_call(settle_kernel, out_shape=out_shape, in_specs=[any_spec] *...  1.79 us

profile of v11, /device:TPU:2, one launch (start us, length us, event | category | flops | bytes accessed | tf_op | source)
XLA Modules:
  0.0 76.8 jit_solution(5122430848165214263)
XLA Ops:
  0.6 74.3 %whole.1 = (bf16[128,1024]{1,0:T(8,128)(2,1)}, bf16[128,1024]{1,0:T(8,128)(2,1)}, f32[32,384]{1,0:T(8,128)}) custom-call(bf16[1,128,1024]{2,1,0:T(8,128)(2,1)} %x_in.1, bf16[1024,3072]{1,0:T(8,128)(2,1)} %w_in.1, bf16[1,128,1024]{2,1,0:T(8,128)(2,1)} %cot_in.1, s32[1,4,32]{2,1,0:T(4,128)} %bitcast.4, s32[1,32]{1,0:T(1,128)} %counts_in.1), custom_call_target="tpu_custom_call" | custom-call | tf_op jit(solution)/shard_map/whole/pallas_call | solution.py:616
  75.0 1.8 %settle.1 = (bf16[128,1024]{1,0:T(8,128)(2,1)}, bf16[128,1024]{1,0:T(8,128)(2,1)}, f32[32,384]{1,0:T(8,128)}) custom-call(bf16[128,1024]{1,0:T(8,128)(2,1)} %get-tuple-element.9.mix_in, bf16[128,1024]{1,0:T(8,128)(2,1)} %get-tuple-element.10.gn_in, f32[32,384]{1,0:T(8,128)} %get-tuple-element.11.wg_in), custom_call_target="tpu_custom_call" | custom-call | tf_op jit(solution)/shard_map/settle/pallas_call | solution.py:696

commit v12 on v11

--- a/solution.py
+++ b/solution.py
@@ -343,9 +343,9 @@
     one_step(2, 0)
 
     def four_rows(i, c):
-        @pl.when(i > 0)
+        @pl.when(i > 1)
         def _():
-            start_group(i - 1, own_row, row_copy)
+            start_group(i - 2, own_row, row_copy)
 
         landed(qd_in.at[pl.ds(0, 4)], qd_r.at[i + 1])
         for u in range(4):
@@ -353,7 +353,8 @@
         return c
 
     lax.fori_loop(0, ng - 1, four_rows, 0)
-    start_group(ng - 2, own_row, row_copy)
+    for i in range(max(ng - 3, 0), ng - 1):
+        start_group(i, own_row, row_copy)
     soft_stage(1)
     grad_stage(nb - 2, 0)
     grad_stage(nb - 1, 1)
@@ -539,9 +540,7 @@
             mid[which * half : (which + 1) * half, t * BLK : (t + 1) * BLK] = total.astype(BF16)
     for k in far_first:
         last_copy(k).start()
-    lax.fori_loop(steps_gn // 2, steps_gn, node_cols, 0)
-    gn_done = pltpu.make_async_copy(gn_ref, gn_out, out_sem.at[1])
-    gn_done.start()
+    lax.fori_loop(steps_gn // 2, 3 * steps_gn // 4, node_cols, 0)
     landed(z_in, z_r)
     total = zpart[:, me_z].astype(F32)
     for k in range(1, nz):
@@ -549,6 +548,9 @@
     z_mid[...] = total.astype(BF16)
     for k in range(1, ny):
         y_copy(k).start()
+    lax.fori_loop(3 * steps_gn // 4, steps_gn, node_cols, 0)
+    gn_done = pltpu.make_async_copy(gn_ref, gn_out, out_sem.at[1])
+    gn_done.start()
 
     landed(row_in.at[:, pl.ds(0, FEAT)], late_r)
     lax.fori_loop(0, ng, take_late, 0)

time: 77.2 us -> 78.4 us (1.016)
  Pallas kernels: 76.1 us -> 76.9 us
    pallas_call x1, Pallas kernels: 74.3 us -> 75.1 us  [per_device(): pl.pallas_call(functools.partial(whole_kernel, nd, ns, ny, nz, tpd), out_...]
where the time goes in v12:
time: 78.4 us; the launch traced here: 77.6 us
  Pallas kernels  76.9 us (98%)
    pallas_call x1, Pallas kernels, per_device(): pl.pallas_call(functools.partial(whole_kernel, nd, ns, ny, nz, tpd), out_...  75.1 us
    pallas_call x1, Pallas kernels, per_device(): pl.pallas_call(settle_kernel, out_shape=out_shape, in_specs=[any_spec] *...  1.79 us

profile of v12, /device:TPU:2, one launch (start us, length us, event | category | flops | bytes accessed | tf_op | source)
XLA Modules:
  0.0 77.6 jit_solution(16143304166514693205)
XLA Ops:
  0.6 75.1 %whole.1 = (bf16[128,1024]{1,0:T(8,128)(2,1)}, bf16[128,1024]{1,0:T(8,128)(2,1)}, f32[32,384]{1,0:T(8,128)}) custom-call(bf16[1,128,1024]{2,1,0:T(8,128)(2,1)} %x_in.1, bf16[1024,3072]{1,0:T(8,128)(2,1)} %w_in.1, bf16[1,128,1024]{2,1,0:T(8,128)(2,1)} %cot_in.1, s32[1,4,32]{2,1,0:T(4,128)} %bitcast.4, s32[1,32]{1,0:T(1,128)} %counts_in.1), custom_call_target="tpu_custom_call" | custom-call | tf_op jit(solution)/shard_map/whole/pallas_call | solution.py:618
  75.8 1.8 %settle.1 = (bf16[128,1024]{1,0:T(8,128)(2,1)}, bf16[128,1024]{1,0:T(8,128)(2,1)}, f32[32,384]{1,0:T(8,128)}) custom-call(bf16[128,1024]{1,0:T(8,128)(2,1)} %get-tuple-element.9.mix_in, bf16[128,1024]{1,0:T(8,128)(2,1)} %get-tuple-element.10.gn_in, f32[32,384]{1,0:T(8,128)} %get-tuple-element.11.wg_in), custom_call_target="tpu_custom_call" | custom-call | tf_op jit(solution)/shard_map/settle/pallas_call | solution.py:698

commit v13 on v10

--- a/solution.py
+++ b/solution.py
@@ -358,7 +358,6 @@
     grad_stage(nb - 2, 0)
     grad_stage(nb - 1, 1)
     start_group(ng - 1, own_row, row_copy)
-    own_late.start()
 
     def col_send(i, c):
         for j in range(4):
@@ -370,6 +369,7 @@
         return c
 
     lax.fori_loop(0, ng, col_send, 0)
+    own_late.start()
     others = nd // 2 - 1
     if others:
         landed(xt_all.at[:, pl.ds(0, others * BLK)], xt_r)
@@ -539,9 +539,7 @@
             mid[which * half : (which + 1) * half, t * BLK : (t + 1) * BLK] = total.astype(BF16)
     for k in far_first:
         last_copy(k).start()
-    lax.fori_loop(steps_gn // 2, steps_gn, node_cols, 0)
-    gn_done = pltpu.make_async_copy(gn_ref, gn_out, out_sem.at[1])
-    gn_done.start()
+    lax.fori_loop(steps_gn // 2, 3 * steps_gn // 4, node_cols, 0)
     landed(z_in, z_r)
     total = zpart[:, me_z].astype(F32)
     for k in range(1, nz):
@@ -549,6 +547,9 @@
     z_mid[...] = total.astype(BF16)
     for k in range(1, ny):
         y_copy(k).start()
+    lax.fori_loop(3 * steps_gn // 4, steps_gn, node_cols, 0)
+    gn_done = pltpu.make_async_copy(gn_ref, gn_out, out_sem.at[1])
+    gn_done.start()
 
     landed(row_in.at[:, pl.ds(0, FEAT)], late_r)
     lax.fori_loop(0, ng, take_late, 0)

time: 76.4 us -> 76.2 us (level)
  no operation moved by 1% of the time
where the time goes in v13:
time: 76.2 us; the launch traced here: 76.1 us
  Pallas kernels  75.4 us (99%)
    pallas_call x1, Pallas kernels, per_device(): pl.pallas_call(functools.partial(whole_kernel, nd, ns, ny, nz, tpd), out_...  73.6 us
    pallas_call x1, Pallas kernels, per_device(): pl.pallas_call(settle_kernel, out_shape=out_shape, in_specs=[any_spec] *...  1.79 us

profile of v13, /device:TPU:2, one launch (start us, length us, event | category | flops | bytes accessed | tf_op | source)
XLA Modules:
  0.0 76.1 jit_solution(16061438790503033782)
XLA Ops:
  0.6 73.6 %whole.1 = (bf16[128,1024]{1,0:T(8,128)(2,1)}, bf16[128,1024]{1,0:T(8,128)(2,1)}, f32[32,384]{1,0:T(8,128)}) custom-call(bf16[1,128,1024]{2,1,0:T(8,128)(2,1)} %x_in.1, bf16[1024,3072]{1,0:T(8,128)(2,1)} %w_in.1, bf16[1,128,1024]{2,1,0:T(8,128)(2,1)} %cot_in.1, s32[1,4,32]{2,1,0:T(4,128)} %bitcast.4, s32[1,32]{1,0:T(1,128)} %counts_in.1), custom_call_target="tpu_custom_call" | custom-call | tf_op jit(solution)/shard_map/whole/pallas_call | solution.py:617
  74.3 1.8 %settle.1 = (bf16[128,1024]{1,0:T(8,128)(2,1)}, bf16[128,1024]{1,0:T(8,128)(2,1)}, f32[32,384]{1,0:T(8,128)}) custom-call(bf16[128,1024]{1,0:T(8,128)(2,1)} %get-tuple-element.9.mix_in, bf16[128,1024]{1,0:T(8,128)(2,1)} %get-tuple-element.10.gn_in, f32[32,384]{1,0:T(8,128)} %get-tuple-element.11.wg_in), custom_call_target="tpu_custom_call" | custom-call | tf_op jit(solution)/shard_map/settle/pallas_call | solution.py:697

commit v14 on v13

--- a/solution.py
+++ b/solution.py
@@ -353,11 +353,9 @@
         return c
 
     lax.fori_loop(0, ng - 1, four_rows, 0)
-    start_group(ng - 2, own_row, row_copy)
     soft_stage(1)
     grad_stage(nb - 2, 0)
     grad_stage(nb - 1, 1)
-    start_group(ng - 1, own_row, row_copy)
 
     def col_send(i, c):
         for j in range(4):
@@ -368,7 +366,10 @@
         start_group(i, own_col, col_copy)
         return c
 
-    lax.fori_loop(0, ng, col_send, 0)
+    lax.fori_loop(0, ng // 2, col_send, 0)
+    start_group(ng - 2, own_row, row_copy)
+    start_group(ng - 1, own_row, row_copy)
+    lax.fori_loop(ng // 2, ng, col_send, 0)
     own_late.start()
     others = nd // 2 - 1
     if others:

time: 76.2 us -> 77.6 us (1.018)
  Pallas kernels: 75.4 us -> 76.9 us
    pallas_call x1, Pallas kernels: 73.6 us -> 75.1 us  [per_device(): pl.pallas_call(functools.partial(whole_kernel, nd, ns, ny, nz, tpd), out_...]
where the time goes in v14:
time: 77.6 us; the launch traced here: 77.5 us
  Pallas kernels  76.9 us (99%)
    pallas_call x1, Pallas kernels, per_device(): pl.pallas_call(functools.partial(whole_kernel, nd, ns, ny, nz, tpd), out_...  75.1 us
    pallas_call x1, Pallas kernels, per_device(): pl.pallas_call(settle_kernel, out_shape=out_shape, in_specs=[any_spec] *...  1.79 us

profile of v14, /device:TPU:2, one launch (start us, length us, event | category | flops | bytes accessed | tf_op | source)
XLA Modules:
  0.0 77.5 jit_solution(11570660503441039407)
XLA Ops:
  0.6 75.1 %whole.1 = (bf16[128,1024]{1,0:T(8,128)(2,1)}, bf16[128,1024]{1,0:T(8,128)(2,1)}, f32[32,384]{1,0:T(8,128)}) custom-call(bf16[1,128,1024]{2,1,0:T(8,128)(2,1)} %x_in.1, bf16[1024,3072]{1,0:T(8,128)(2,1)} %w_in.1, bf16[1,128,1024]{2,1,0:T(8,128)(2,1)} %cot_in.1, s32[1,4,32]{2,1,0:T(4,128)} %bitcast.4, s32[1,32]{1,0:T(1,128)} %counts_in.1), custom_call_target="tpu_custom_call" | custom-call | tf_op jit(solution)/shard_map/whole/pallas_call | solution.py:618
  75.7 1.8 %settle.1 = (bf16[128,1024]{1,0:T(8,128)(2,1)}, bf16[128,1024]{1,0:T(8,128)(2,1)}, f32[32,384]{1,0:T(8,128)}) custom-call(bf16[128,1024]{1,0:T(8,128)(2,1)} %get-tuple-element.9.mix_in, bf16[128,1024]{1,0:T(8,128)(2,1)} %get-tuple-element.10.gn_in, f32[32,384]{1,0:T(8,128)} %get-tuple-element.11.wg_in), custom_call_target="tpu_custom_call" | custom-call | tf_op jit(solution)/shard_map/settle/pallas_call | solution.py:698
